TPU v7x, 512 devices: a whole 4x8x8 slice. The times are simulated.
512 devices in a mesh: tg: 8 (over x, core), pw: 64 (over y, z).
Axes of the slice: x: 4, y: 8, z: 8, core: 2. Of those that a mesh axis runs over, the one named last changes fastest.
Arguments:
- orbital_coefficients: float32 [8, 2, 4096, 192], P(None, None, ('tg', 'pw')), may hold values from -6 to 6
- potential: float32 [192, 36864], P('pw'), may hold values from -2 to 2
- line_lateral_place: int32 [36864], replicated, may hold values from 0 to 36863, as said below
- stick_count: int32 [512], replicated, may hold values from 1 to 8, 2560 in all
- proj_atom: int32 [2048], replicated, may hold values from 0 to 511
- atom_pos: float32 [3, 512], replicated, may hold values from 0 to 1
- proj_radius: float32 [2048], replicated, may hold values from 2 to 40
- proj_diag: float32 [2048], replicated, may hold values from 1 to 10
- ionic_pseudo_dij: float32 [2048], replicated, may hold values from -1 to 1
Outputs:
- hpsi: float32 [8, 2, 4096, 192], P(None, None, ('tg', 'pw'))
Inputs may be any that keep to these rules, and one draw needn't show every extreme that they name: line_lateral_place holds 36864 distinct column positions; the first 4096 belong to the stick slots in order and are columns with gx^2 + gy^2 <= 48^2 in random order, or, where that disc holds fewer than 4096 columns, all of them followed by the nearest columns outside it. stick_count[k] counts the live slots among the 8 slots k * 8 and on; the live ones come first; some block is full.
All inputs are finite; a program needn't handle non-finite values.
Results may differ from a plain program's by a relative error of at most 0.0003.
Values sent between devices are 32-bit elements; how exact they have to be, the bound alone decides.
No kernel may reach another device: no remote copies, remote signals or barrier semaphores. Data moves between devices by JAX's collectives and lax.ppermute only.
A program may use at most 128 MiB of HBM per device.

v0:
```python
import math

import jax
import jax.numpy as jnp
import numpy as np
from jax import lax
from jax.experimental import pallas as pl
from jax.experimental.pallas import tpu as pltpu
from jax.sharding import PartitionSpec as P

EDGE = 192
TEAMS = 8
SHEETS = 64
DEPTH = 3
ROWS = DEPTH + 1
LINES = 8
STICKS = TEAMS * LINES
NPROJ = 2048
NATOM = 512
CUT = 48
HALF_ROWS = 64
CHUNK = 512
CHUNKS = SHEETS * STICKS // CHUNK
PCHUNK = 256
BLOCKS = NPROJ // 128

F32 = jnp.float32
BF16 = jnp.bfloat16

NN = (((1,), (0,)), ((), ()))
NT = (((1,), (1,)), ((), ()))


def split_table(table):
    high = table.astype(np.float32).astype(jnp.bfloat16)
    low = (table - high.astype(np.float64)).astype(np.float32).astype(jnp.bfloat16)
    return high, low


def depth_table():
    steps = np.arange(EDGE)
    planes = steps.reshape(SHEETS, DEPTH).T.reshape(-1)
    turns = (planes[:, None] * steps[None, :] % EDGE) * (2.0 * math.pi / EDGE)
    return np.concatenate([np.cos(turns), np.sin(turns)], axis=0)


def column_phase(freqs, valid):
    turns = (freqs[:, None] * np.arange(EDGE)[None, :] % EDGE) * (2.0 * math.pi / EDGE)
    keep = valid[:, None].astype(np.float64)
    return np.cos(turns) * keep, np.sin(turns) * keep


def lateral_tables():
    spot = np.arange(2 * HALF_ROWS)
    y_cos, y_sin = column_phase(spot - CUT, spot <= 2 * CUT)
    pad = ((0, 0), (0, 256 - EDGE))
    y_cos, y_sin = np.pad(y_cos, pad), np.pad(y_sin, pad)
    y_inverse = np.block([[y_cos, y_sin], [-y_sin, y_cos]])
    x_spot = 2 * (spot % HALF_ROWS) + spot // HALF_ROWS
    x_cos, x_sin = column_phase(x_spot - CUT, x_spot <= 2 * CUT)
    x_forward = np.block([[x_cos, x_sin], [-x_sin, x_cos]])
    return y_inverse, x_forward.T, x_forward, y_inverse.T


def split(value):
    high = value.astype(BF16)
    return high, (value - high.astype(F32)).astype(BF16)


def mul(left, right, form):
    return lax.dot_general(left, right, form, preferred_element_type=F32)


def dot3(left, right, form):
    return mul(left[0], right[0], form) + mul(left[0], right[1], form) + mul(left[1], right[0], form)


def lateral_split(cols):
    x = (cols * 43691) >> 23
    y = cols - x * EDGE
    x = jnp.where(x < EDGE // 2, x, x - EDGE)
    y = jnp.where(y < EDGE // 2, y, y - EDGE)
    return x, y


def sincos_turns(turns):
    quarter = turns * 4.0
    near = jnp.floor(quarter + 0.5)
    x = (quarter - near) * (0.5 * math.pi)
    which = near.astype(jnp.int32) & 3
    xx = x * x
    sine = x * (1.0 + xx * (-1.0 / 6 + xx * (1.0 / 120 + xx * (-1.0 / 5040 + xx * (1.0 / 362880)))))
    cosine = 1.0 + xx * (-0.5 + xx * (1.0 / 24 + xx * (-1.0 / 720 + xx * (1.0 / 40320))))
    odd = (which & 1) == 1
    c = jnp.where(odd, sine, cosine)
    s = jnp.where(odd, cosine, sine)
    return jnp.where(((which + 1) & 2) == 2, -c, c), jnp.where((which & 2) == 2, -s, s)


def own_lateral(cols_ref, sheet):
    row = cols_ref[pl.ds(sheet, 1), :]
    x, y = lateral_split(row)
    eye = lax.broadcasted_iota(jnp.int32, (STICKS, STICKS), 0) == lax.broadcasted_iota(
        jnp.int32, (STICKS, STICKS), 1
    )

    def upright(value):
        wide = jnp.broadcast_to(value.astype(F32), (STICKS, STICKS))
        return jnp.sum(jnp.where(eye, wide, 0.0), axis=1, keepdims=True)

    return upright(x), upright(y)


def live_column(counts_ref, sheet, team):
    line = lax.broadcasted_iota(jnp.int32, (LINES, EDGE), 0)
    return line < counts_ref[team * SHEETS + sheet]


def live_sticks(sticks_ref, counts_ref, sheet):
    rows = []
    for part in range(2):
        for team in range(TEAMS):
            live = live_column(counts_ref, sheet, team)
            rows.append(jnp.where(live, sticks_ref[team, part], 0.0))
    return jnp.concatenate(rows, axis=0)


def table_kernel(sheet_ref, cols_ref, atom_ref, pos_ref, radius_ref, a_ref, bh_ref, bl_ref, mask_ref):
    sheet = sheet_ref[0]
    gx, gy = own_lateral(cols_ref, sheet)
    gxy = gx * gx + gy * gy
    pos = pos_ref[...]
    first = pos.astype(BF16).astype(F32)
    second = (pos - first).astype(BF16).astype(F32)
    third = (pos - first - second).astype(BF16).astype(F32)
    line = lax.broadcasted_iota(jnp.int32, (16, NATOM), 0)
    rows = jnp.zeros((16, NATOM), F32)
    for step, piece in enumerate((first, second, third)):
        for axis in range(3):
            rows = jnp.where(line == 3 * step + axis, piece[axis : axis + 1, :], rows)
    rows = rows.astype(BF16)
    low_g = lax.broadcasted_iota(jnp.int32, (8, PCHUNK), 0).astype(F32)
    for at in range(0, NPROJ, PCHUNK):
        here = slice(at, at + PCHUNK)
        atoms = lax.broadcasted_iota(jnp.int32, (NATOM, PCHUNK), 0)
        member = jnp.where(atoms == atom_ref[:, here], 1.0, 0.0).astype(BF16)
        mask_ref[:, here] = member
        placed = mul(rows, member, NN)
        tx, ty, tz = (
            placed[axis : axis + 1] + placed[3 + axis : 4 + axis] + placed[6 + axis : 7 + axis]
            for axis in range(3)
        )
        spread = radius_ref[:, here] / (EDGE * EDGE)
        cosine, sine = sincos_turns(gx * tx + gy * ty)
        amp = jnp.exp(-spread * gxy)
        a_ref[:STICKS, here] = amp * cosine
        a_ref[STICKS:, here] = -amp * sine
        low_c, low_s = sincos_turns(low_g * tz)
        for bank in range(3):
            high_g = (
                lax.broadcasted_iota(jnp.int32, (8, PCHUNK), 0) + bank * 8
            ) * 8
            high_g = jnp.where(high_g < EDGE // 2, high_g, high_g - EDGE).astype(F32)
            high_c, high_s = sincos_turns(high_g * tz)
            for pair in range(4):
                re_rows, im_rows = [], []
                for inner in range(2):
                    row = pair * 2 + inner
                    hc, hs = high_c[row : row + 1], high_s[row : row + 1]
                    first_g = (bank * 8 + row) * 8
                    first_g = first_g if first_g < EDGE // 2 else first_g - EDGE
                    g = low_g + float(first_g)
                    amp_z = jnp.exp(-spread * (g * g))
                    re_rows.append(amp_z * (hc * low_c - hs * low_s))
                    im_rows.append(-amp_z * (hs * low_c + hc * low_s))
                z = (bank * 8 + pair * 2) * 8
                high, low = split(jnp.concatenate(re_rows, axis=0))
                bh_ref[z : z + 16, here] = high
                bl_ref[z : z + 16, here] = low
                high, low = split(jnp.concatenate(im_rows, axis=0))
                bh_ref[EDGE + z : EDGE + z + 16, here] = high
                bl_ref[EDGE + z : EDGE + z + 16, here] = low


def rows_of(re, im):
    re_high = re.astype(BF16).astype(F32)
    im_high = im.astype(BF16).astype(F32)
    line = lax.broadcasted_iota(jnp.int32, (16, re.shape[1]), 0)
    rows = jnp.where(line == 0, re_high, 0.0)
    rows = jnp.where(line == 1, im_high, rows)
    rows = jnp.where(line == 2, re - re_high, rows)
    return jnp.where(line == 3, im - im_high, rows).astype(BF16)


def every(start):
    return pl.ds(start, SHEETS, stride=ROWS)


def project_kernel(
    sheet_ref, counts_ref, sticks_ref, th_ref, tl_ref, a_ref, bh_ref, bl_ref, mask_ref, diag_ref, dij_ref,
    out_ref, becp_ref,
):
    coeff = split(live_sticks(sticks_ref, counts_ref, sheet_ref[0]))
    both = dot3((th_ref[...], tl_ref[...]), coeff, NT)
    with_cos, with_sin = both[:EDGE], both[EDGE:]
    by_depth = with_cos + jnp.concatenate([-with_sin[:, STICKS:], with_sin[:, :STICKS]], axis=1)
    for plane in range(DEPTH):
        out_ref[every(plane), :] = by_depth[plane * SHEETS : (plane + 1) * SHEETS]
    out_ref[every(DEPTH), :] = jnp.zeros((SHEETS, 128), F32)
    for at in range(0, NPROJ, PCHUNK):
        here = slice(at, at + PCHUNK)
        with_re = dot3(coeff, (bh_ref[:EDGE, here], bl_ref[:EDGE, here]), NN)
        with_im = dot3(coeff, (bh_ref[EDGE:, here], bl_ref[EDGE:, here]), NN)
        y_re = with_re[:STICKS] + with_im[STICKS:]
        y_im = with_re[STICKS:] - with_im[:STICKS]
        a_re, a_im = a_ref[:STICKS, here], a_ref[STICKS:, here]
        becp_ref[0:1, here] = jnp.sum(a_re * y_re + a_im * y_im, axis=0, keepdims=True)
        becp_ref[1:2, here] = jnp.sum(a_re * y_im - a_im * y_re, axis=0, keepdims=True)
    scale = 1.0 / (math.sqrt(TEAMS * SHEETS * LINES * EDGE) * math.sqrt(NPROJ))
    re, im = becp_ref[0:1, :] * scale, becp_ref[1:2, :] * scale
    dij, diag = dij_ref[...], diag_ref[...]
    per_atom = mul(rows_of(re * dij, im * dij), mask_ref[...], NT)
    common = mul(
        rows_of(per_atom[0:1] + per_atom[2:3], per_atom[1:2] + per_atom[3:4]), mask_ref[...], NN
    )
    w = (
        re * diag + dij * (common[0:1] + common[2:3]),
        im * diag + dij * (common[1:2] + common[3:4]),
    )
    for part in range(2):
        for block in range(BLOCKS):
            row = ROWS * (part * BLOCKS + block) + DEPTH
            out_ref[row : row + 1, :] = w[part][:, block * 128 : (block + 1) * 128]


def spread_kernel(cols_ref, x_ref, hot_ref):
    half = SHEETS // 2
    x, y = lateral_split(jnp.concatenate([cols_ref[:half, :], cols_ref[half:, :]], axis=1))
    x, y = x + CUT, y + CUT
    x_ref[0] = x >> 1
    x_ref[1] = (x & 1) * 128 + y
    rows256 = lax.broadcasted_iota(jnp.int32, (256, 128), 0)
    per = CHUNK // 128
    for chunk in range(CHUNKS):
        for inner in range(per):
            r = chunk * per + inner
            lanes = slice(inner * 128, (inner + 1) * 128)
            hot_ref[chunk, :, lanes] = jnp.where(rows256 == x_ref[1, r : r + 1, :], 1.0, 0.0).astype(BF16)


def plane_kernel(
    x_ref, hot_ref, sticks_ref, potential_ref,
    yih_ref, yil_ref, xih_ref, xil_ref, xfh_ref, xfl_ref, yfh_ref, yfl_ref,
    out_ref, v_ref, left_ref, pick_ref,
):
    half = SHEETS // 2
    for plane in range(DEPTH):
        rows = sticks_ref[every(plane), :]
        top, bottom = rows[:half], rows[half:]
        for part in range(2):
            lanes = slice(part * STICKS, (part + 1) * STICKS)
            value = jnp.concatenate([top[:, lanes], bottom[:, lanes]], axis=1)
            high = value.astype(BF16).astype(F32)
            at = 2 * (2 * plane + part)
            v_ref[at] = high
            v_ref[at + 1] = value - high
    summed = jnp.sum(sticks_ref[every(DEPTH), :], axis=0, keepdims=True)
    out_ref[every(DEPTH), :] = jnp.broadcast_to(summed, (SHEETS, 128))
    rows64 = lax.broadcasted_iota(jnp.int32, (HALF_ROWS, 128), 0)
    per = CHUNK // 128
    total = jnp.zeros((12 * HALF_ROWS, 256), F32)
    for chunk in range(CHUNKS):
        slot = chunk % 2
        for inner in range(per):
            r = chunk * per + inner
            lanes = slice(inner * 128, (inner + 1) * 128)
            member = rows64 == x_ref[0, r : r + 1, :]
            for k in range(12):
                left_ref[slot, k * HALF_ROWS : (k + 1) * HALF_ROWS, lanes] = jnp.where(
                    member, v_ref[k, r : r + 1, :], 0.0
                ).astype(BF16)
        total = total + mul(left_ref[slot], hot_ref[chunk], NT)
    grids = []
    for plane in range(DEPTH):
        parts = []
        for part in range(2):
            at = 2 * (2 * plane + part) * HALF_ROWS
            grid = total[at : at + HALF_ROWS] + total[at + HALF_ROWS : at + 2 * HALF_ROWS]
            parts.append(jnp.concatenate([grid[:, :128], grid[:, 128:]], axis=0))
        grids.append(jnp.concatenate(parts, axis=1))
    work = jnp.concatenate(grids, axis=0)
    work = dot3(split(work), (yih_ref[...], yil_ref[...]), NN)
    work = jnp.concatenate(
        [
            jnp.concatenate(
                [work[p * 128 : (p + 1) * 128, :256], work[p * 128 : (p + 1) * 128, 256:]], axis=0
            )
            for p in range(DEPTH)
        ],
        axis=1,
    )
    work = dot3((xih_ref[...], xil_ref[...]), split(work), NN)
    local = jnp.concatenate([potential_ref[p] for p in range(DEPTH)], axis=1)
    work = jnp.concatenate([work[:EDGE] * local, work[EDGE:] * local], axis=0)
    work = dot3((xfh_ref[...], xfl_ref[...]), split(work), NN)
    work = jnp.concatenate(
        [
            jnp.concatenate(
                [work[:128, p * 256 : (p + 1) * 256], work[128:, p * 256 : (p + 1) * 256]], axis=1
            )
            for p in range(DEPTH)
        ],
        axis=0,
    )
    work = dot3(split(work), (yfh_ref[...], yfl_ref[...]), NN)
    pieces = []
    for p in range(DEPTH):
        for c in range(2):
            block = work[p * 128 : (p + 1) * 128, c * 128 : (c + 1) * 128]
            pieces.append(jnp.concatenate([block[:HALF_ROWS], block[HALF_ROWS:]], axis=1))
    high, low = split(jnp.concatenate(pieces, axis=0))
    for chunk in range(CHUNKS):
        hot = hot_ref[chunk]
        found = mul(high, hot, NN) + mul(low, hot, NN)
        for inner in range(per):
            r = chunk * per + inner
            lanes = slice(inner * 128, (inner + 1) * 128)
            member = rows64 == x_ref[0, r : r + 1, :]
            for k in range(6):
                pick_ref[k, r : r + 1, :] = jnp.sum(
                    jnp.where(member, found[k * HALF_ROWS : (k + 1) * HALF_ROWS, lanes], 0.0),
                    axis=0,
                    keepdims=True,
                )
    for plane in range(DEPTH):
        re, im = pick_ref[2 * plane], pick_ref[2 * plane + 1]
        out_ref[every(plane), :] = jnp.concatenate(
            [
                jnp.concatenate([re[:, :STICKS], im[:, :STICKS]], axis=1),
                jnp.concatenate([re[:, STICKS:], im[:, STICKS:]], axis=1),
            ],
            axis=0,
        )


def finish_kernel(
    sheet_ref, counts_ref, cols_ref, sticks_ref, back_ref, a_ref, bh_ref, bl_ref, th_ref, tl_ref, out_ref
):
    sheet = sheet_ref[0]
    vnl_re = jnp.zeros((2 * STICKS, EDGE), F32)
    vnl_im = jnp.zeros((2 * STICKS, EDGE), F32)
    step = 2 * PCHUNK
    for at in range(0, NPROJ, step):
        here = slice(at, at + step)
        a_re, a_im = a_ref[:STICKS, here], a_ref[STICKS:, here]
        w_re, w_im = (
            jnp.concatenate(
                [
                    back_ref[row : row + 1, :]
                    for row in range(
                        ROWS * (part * BLOCKS + at // 128) + DEPTH,
                        ROWS * (part * BLOCKS + (at + step) // 128) + DEPTH,
                        ROWS,
                    )
                ],
                axis=1,
            )
            for part in range(2)
        )
        weighted = split(
            jnp.concatenate([a_re * w_re - a_im * w_im, a_re * w_im + a_im * w_re], axis=0)
        )
        vnl_re = vnl_re + dot3(weighted, (bh_ref[:EDGE, here], bl_ref[:EDGE, here]), NT)
        vnl_im = vnl_im + dot3(weighted, (bh_ref[EDGE:, here], bl_ref[EDGE:, here]), NT)
    back = jnp.concatenate([back_ref[every(plane), :] for plane in range(DEPTH)], axis=0)
    back = split(back.T)
    with_cos = dot3(back, (th_ref[:EDGE], tl_ref[:EDGE]), NN)
    with_sin = dot3(back, (th_ref[EDGE:], tl_ref[EDGE:]), NN)
    box_scale = 1.0 / float(EDGE) ** 3
    sums = (
        (with_cos[:STICKS] + with_sin[STICKS:]) * box_scale + (vnl_re[:STICKS] - vnl_im[STICKS:]),
        (with_cos[STICKS:] - with_sin[:STICKS]) * box_scale + (vnl_re[STICKS:] + vnl_im[:STICKS]),
    )
    gx, gy = own_lateral(cols_ref, sheet)
    gz = lax.broadcasted_iota(jnp.int32, (1, EDGE), 1)
    gz = jnp.where(gz < EDGE // 2, gz, gz - EDGE).astype(F32)
    kinetic = 2.0 * (((gx * gx + gy * gy) + gz * gz) / (EDGE * EDGE))
    for team in range(TEAMS):
        live = live_column(counts_ref, sheet, team)
        rows = slice(team * LINES, (team + 1) * LINES)
        for part in range(2):
            value = kinetic[rows] * sticks_ref[team, part] + sums[part][rows]
            out_ref[team, part] = jnp.where(live, value, 0.0)


def call(kernel, n_scalars, n_inputs, outs, scratch=(), flops=0, limit=20 << 20):
    smem = pl.BlockSpec(memory_space=pltpu.SMEM)
    vmem = pl.BlockSpec(memory_space=pltpu.VMEM)
    return pl.pallas_call(
        kernel,
        out_shape=outs,
        in_specs=[smem] * n_scalars + [vmem] * n_inputs,
        out_specs=jax.tree.map(lambda _: vmem, outs),
        scratch_shapes=list(scratch),
        compiler_params=pltpu.CompilerParams(vmem_limit_bytes=limit),
        cost_estimate=pl.CostEstimate(flops=flops, bytes_accessed=4 << 20, transcendentals=0),
    )


def shape(dims, dtype=F32):
    return jax.ShapeDtypeStruct(dims, dtype)


def make_tables(sheet, cols, proj_atom, atom_pos, proj_radius):
    return call(
        table_kernel, 1, 4,
        (
            shape((2 * STICKS, NPROJ)),
            shape((2 * EDGE, NPROJ), BF16),
            shape((2 * EDGE, NPROJ), BF16),
            shape((NATOM, NPROJ), BF16),
        ),
        flops=2 << 30,
    )(sheet, cols, proj_atom.reshape(1, NPROJ), atom_pos, proj_radius.reshape(1, NPROJ))


def project(sheet, counts, sticks, tables, proj_diag, dij):
    a, bh, bl, mask = tables
    return call(
        project_kernel, 2, 9, shape((SHEETS * ROWS, 2 * STICKS)), [pltpu.VMEM((2, NPROJ), F32)], flops=3 << 30
    )(
        sheet, counts, sticks, *split_table(depth_table()), a, bh, bl, mask,
        proj_diag.reshape(1, NPROJ), dij.reshape(1, NPROJ),
    )


def spread(cols):
    return call(
        spread_kernel, 0, 1,
        (shape((2, SHEETS // 2, 128), jnp.int32), shape((CHUNKS, 256, CHUNK), BF16)),
        flops=1 << 30,
    )(cols)


def plane_work(spots, sticks, potential):
    tables = [piece for table in lateral_tables() for piece in split_table(table)]
    padded = jnp.pad(potential.reshape(DEPTH, EDGE, EDGE), ((0, 0), (0, 0), (0, 256 - EDGE)))
    return call(
        plane_kernel, 0, 12, shape((SHEETS * ROWS, 2 * STICKS)),
        [
            pltpu.VMEM((12, SHEETS // 2, 128), F32),
            pltpu.VMEM((2, 12 * HALF_ROWS, CHUNK), BF16),
            pltpu.VMEM((6, SHEETS // 2, 128), F32),
        ],
        flops=8 << 30,
        limit=28 << 20,
    )(*spots, sticks, padded, *tables)


def finish(sheet, counts, cols, sticks, back, tables):
    a, bh, bl, _ = tables
    return call(finish_kernel, 2, 8, shape((TEAMS, 2, LINES, EDGE)), flops=3 << 30)(
        sheet, counts, cols, sticks, back, a, bh, bl, *split_table(depth_table())
    )


def over_sheets(rows):
    sent = rows.reshape(SHEETS, ROWS, 2 * STICKS)
    return lax.all_to_all(sent, "pw", split_axis=0, concat_axis=0, tiled=True).reshape(rows.shape)


def body(
    orbital_coefficients,
    potential,
    line_lateral_place,
    stick_count,
    proj_atom,
    atom_pos,
    proj_radius,
    proj_diag,
    ionic_pseudo_dij,
):
    sheet = lax.axis_index("pw").astype(jnp.int32).reshape(1)
    layout = line_lateral_place[: TEAMS * SHEETS * LINES].reshape(TEAMS, SHEETS, LINES)
    cols = jnp.transpose(layout, (1, 0, 2)).reshape(SHEETS, STICKS)
    sticks = lax.all_to_all(orbital_coefficients, "tg", split_axis=0, concat_axis=0, tiled=True)
    tables = make_tables(sheet, cols, proj_atom, atom_pos, proj_radius)
    by_depth = project(sheet, stick_count, sticks, tables, proj_diag, ionic_pseudo_dij)
    by_plane = over_sheets(by_depth)
    picked = plane_work(spread(cols), by_plane, potential)
    back = over_sheets(picked)
    done = finish(sheet, stick_count, cols, sticks, back, tables)
    return lax.all_to_all(done, "tg", split_axis=0, concat_axis=0, tiled=True)


def solution(mesh):
    return jax.shard_map(
        body,
        mesh=mesh,
        in_specs=(
            P(None, None, ("tg", "pw"), None),
            P("pw", None),
            P(),
            P(),
            P(),
            P(),
            P(),
            P(),
            P(),
        ),
        out_specs=P(None, None, ("tg", "pw"), None),
        check_vma=False,
    )
```

profile of v0, /device:TPU:1, one launch (start us, length us, event | category | flops | bytes accessed | tf_op | source)
XLA Modules:
  0.0 93.9 jit_solution(16455315890815191925)
XLA Ops:
  0.0 10.1 %all-to-all-start = ((f32[8,2,8,192]{3,2,1,0:T(8,128)}), f32[8,2,8,192]{3,2,1,0:T(8,128)S(1)}, u32[]{:S(2)}, u32[]{:S(2)}) async-start(f32[8,2,8,192]{3,2,1,0:T(8,128)} %param.21), calls=%async_computation | async-start | bytes 262144 | tf_op jit(solution)/shard_map/all_to_all | solution.py:486
  10.2 0.7 slice.11
  10.9 0.2 reshape.45
  11.0 0.1 copy.22
  11.1 0.1 copy.25.cols_ref
  11.2 0.0 copy-start
  11.2 0.7 copy-done
  11.9 0.0 copy-start.1
  11.9 0.7 copy-done.1
  12.6 0.0 copy-start.2
  12.6 0.7 copy-done.2
  13.3 0.0 copy-start.3
  13.3 0.0 copy-start.4
  13.3 0.0 copy-start.11
  13.4 2.8 %shard_map.200 = (f32[128,2048]{1,0:T(8,128)S(1)}, bf16[384,2048]{1,0:T(8,128)(2,1)S(1)}, bf16[384,2048]{1,0:T(8,128)(2,1)S(1)}, bf16[512,2048]{1,0:T(8,128)(2,1)S(1)}) custom-call(s32[1]{0:T(128)} %bitcast.sheet_ref, s32[64,64]{1,0:T(8,128)S(1)} %copy.25.cols_ref, s32[1,2048]{1,0:T(1,128)S(1)} %bitcast.14, f32[3,512]{1,0:T(4,128)S(1)} %copy-done.1, ...), custom_call_target="tpu_custom_call" | custom-call | flops 2147483648 | bytes 4194304 | tf_op jit(solution)/shard_map/pallas_call | solution.py:415
  16.2 0.0 copy-start.18
  16.2 1.3 %copy-done.18 = bf16[512,2048]{1,0:T(8,128)(2,1)} copy-done((bf16[512,2048]{1,0:T(8,128)(2,1)}, bf16[512,2048]{1,0:T(8,128)(2,1)S(1)}, u32[]{:S(2)}) %copy-start.18) | copy-done | bytes 2097176
  17.6 1.1 %copy-done.20 = bf16[384,2048]{1,0:T(8,128)(2,1)} copy-done((bf16[384,2048]{1,0:T(8,128)(2,1)}, bf16[384,2048]{1,0:T(8,128)(2,1)S(1)}, u32[]{:S(2)}) %copy-start.20) | copy-done | bytes 1572888
  18.7 1.2 %copy-done.23 = bf16[384,2048]{1,0:T(8,128)(2,1)} copy-done((bf16[384,2048]{1,0:T(8,128)(2,1)}, bf16[384,2048]{1,0:T(8,128)(2,1)S(1)}, u32[]{:S(2)}) %copy-start.23) | copy-done | bytes 1572888
  19.9 0.0 all-to-all-done.sticks_ref
  19.9 0.0 copy-done.3
  19.9 0.0 copy-done.4
  19.9 0.0 copy-done.5
  19.9 0.0 copy-done.10
  19.9 0.0 copy-done.11
  20.0 0.0 copy-start.19
  20.0 1.9 %copy-done.19 = bf16[512,2048]{1,0:T(8,128)(2,1)S(1)} copy-done((bf16[512,2048]{1,0:T(8,128)(2,1)S(1)}, bf16[512,2048]{1,0:T(8,128)(2,1)}, u32[]{:S(2)}) %copy-start.19) | copy-done | bytes 2097176
  21.9 1.4 %copy-done.21 = bf16[384,2048]{1,0:T(8,128)(2,1)S(1)} copy-done((bf16[384,2048]{1,0:T(8,128)(2,1)S(1)}, bf16[384,2048]{1,0:T(8,128)(2,1)}, u32[]{:S(2)}) %copy-start.21) | copy-done | bytes 1572888
  23.3 1.4 %copy-done.24 = bf16[384,2048]{1,0:T(8,128)(2,1)S(1)} copy-done((bf16[384,2048]{1,0:T(8,128)(2,1)S(1)}, bf16[384,2048]{1,0:T(8,128)(2,1)}, u32[]{:S(2)}) %copy-start.24) | copy-done | bytes 1572888
  24.7 3.4 %shard_map.201 = f32[256,128]{1,0:T(8,128)} custom-call(s32[1]{0:T(128)} %bitcast.sheet_ref, s32[512]{0:T(512)S(1)} %copy-done.5, f32[8,2,8,192]{3,2,1,0:T(8,128)S(1)} %all-to-all-done.sticks_ref, bf16[384,192]{1,0:T(8,128)(2,1)S(1)} %copy-done.10, bf16[384,192]{1,0:T(8,128)(2,1)S(1)} %copy-done.11, f32[128,2048]{1,0:T(8,128)S(1)} %get-tuple-element.13.a_ref, ...), custom_call_target="tpu_custom_call" | custom-call | flops 3221225472 | bytes 4194304 | tf_op jit(solution)/shard_map/pallas_call | solution.py:429
  28.1 0.0 copy-done.26
  28.1 12.1 %all-to-all-start.1 = ((f32[64,4,128]{2,1,0:T(4,128)}), f32[64,4,128]{2,1,0:T(4,128)S(1)}, u32[]{:S(2)}, u32[]{:S(2)}) async-start(f32[64,4,128]{2,1,0:T(4,128)} %bitcast.7), calls=%async_computation.1 | async-start | bytes 262144 | tf_op jit(solution)/shard_map/all_to_all | solution.py:469
  40.2 0.0 copy-done.28
  40.3 0.4 reshape.53
  40.7 0.0 copy-start.6
  40.7 0.0 copy-start.7
  40.7 0.0 copy-start.8
  40.7 0.0 copy-start.9
  40.7 0.0 copy-start.12
  40.7 0.0 copy-start.13
  40.8 0.0 copy-start.14
  40.8 0.0 copy-start.15
  40.8 0.8 shard_map.199
  41.5 0.0 copy-start.16
  41.6 1.3 %copy-done.16 = bf16[8,256,512]{2,1,0:T(8,128)(2,1)} copy-done((bf16[8,256,512]{2,1,0:T(8,128)(2,1)}, bf16[8,256,512]{2,1,0:T(8,128)(2,1)S(1)}, u32[]{:S(2)}) %copy-start.16) | copy-done | bytes 2097176
  42.9 8.7 %all-to-all-done.1 = f32[64,4,128]{2,1,0:T(4,128)S(1)} async-done(((f32[64,4,128]{2,1,0:T(4,128)}), f32[64,4,128]{2,1,0:T(4,128)S(1)}, u32[]{:S(2)}, u32[]{:S(2)}) %all-to-all-start.1) | async-done | bytes 131104 | tf_op jit(solution)/shard_map/all_to_all | solution.py:469
  51.6 0.0 copy-done.6
  51.6 0.0 copy-done.7
  51.6 0.0 copy-done.8
  51.6 0.0 copy-done.9
  51.6 0.0 copy-done.12
  51.7 0.0 copy-done.13
  51.7 0.0 copy-done.14
  51.7 0.0 copy-done.15
  51.7 0.0 copy-start.17
  51.7 1.6 %copy-done.17 = bf16[8,256,512]{2,1,0:T(8,128)(2,1)S(1)} copy-done((bf16[8,256,512]{2,1,0:T(8,128)(2,1)S(1)}, bf16[8,256,512]{2,1,0:T(8,128)(2,1)}, u32[]{:S(2)}) %copy-start.17) | copy-done | bytes 2097176
  53.3 9.6 %shard_map.202 = f32[256,128]{1,0:T(8,128)S(1)} custom-call(s32[2,32,128]{2,1,0:T(8,128)S(1)} %get-tuple-element.11.x_ref, bf16[8,256,512]{2,1,0:T(8,128)(2,1)S(1)} %copy-done.17, f32[256,128]{1,0:T(8,128)S(1)} %bitcast.11, f32[3,192,256]{2,1,0:T(8,128)S(1)} %pad.4.potential_ref, bf16[256,512]{1,0:T(8,128)(2,1)S(1)} %copy-done.6, ...), custom_call_target="tpu_custom_call" | custom-call | flops 8589934592 | bytes 4194304 | tf_op jit(solution)/shard_map/pallas_call | solution.py:448
  62.8 15.7 %all_to_all.20 = f32[64,4,128]{2,1,0:T(4,128)S(1)} all-to-all(f32[64,4,128]{2,1,0:T(4,128)S(1)} %bitcast.12), channel_id=1, replica_groups=mesh['tg'=8,'pw'=64] {'pw'}, dimensions={0} | all-to-all | bytes 262144 | tf_op jit(solution)/shard_map/all_to_all | solution.py:469
  78.5 0.0 copy-done.22
  78.5 0.0 copy-done.25
  78.5 0.0 copy-done.27
  78.5 2.4 %shard_map.203 = f32[8,2,8,192]{3,2,1,0:T(8,128)S(1)} custom-call(s32[1]{0:T(128)} %bitcast.sheet_ref, s32[512]{0:T(512)S(1)} %copy-done.5, s32[64,64]{1,0:T(8,128)S(1)} %copy.25.cols_ref, f32[8,2,8,192]{3,2,1,0:T(8,128)S(1)} %all-to-all-done.sticks_ref, f32[256,128]{1,0:T(8,128)S(1)} %bitcast.13, f32[128,2048]{1,0:T(8,128)S(1)} %copy-done.27, ...), custom_call_target="tpu_custom_call" | custom-call | flops 3221225472 | bytes 4194304 | tf_op jit(solution)/shard_map/pallas_call | solution.py:462
  80.9 12.4 %all_to_all.21 = f32[8,2,8,192]{3,2,1,0:T(8,128)S(1)} all-to-all(f32[8,2,8,192]{3,2,1,0:T(8,128)S(1)} %shard_map.203), channel_id=1, replica_groups=mesh['tg'=8,'pw'=64] {'tg'}, dimensions={0} | all-to-all | bytes 196608 | tf_op jit(solution)/shard_map/all_to_all | solution.py:493
  93.3 0.7 copy.27
  (12 shorter events, 0.1 us)
Async XLA Ops:
  0.0 19.9 %all-to-all-start = ((f32[8,2,8,192]{3,2,1,0:T(8,128)}), f32[8,2,8,192]{3,2,1,0:T(8,128)S(1)}, u32[]{:S(2)}, u32[]{:S(2)}) async-start(f32[8,2,8,192]{3,2,1,0:T(8,128)} %param.21), calls=%async_computation | async-start | bytes 262144 | tf_op jit(solution)/shard_map/all_to_all | solution.py:486
  11.2 0.7 copy-start
  11.9 0.7 copy-start.1
  12.6 0.7 copy-start.2
  13.3 6.6 %copy-start.3 = (f32[2048]{0:T(1024)S(1)}, f32[2048]{0:T(1024)}, u32[]{:S(2)}) copy-start(f32[2048]{0:T(1024)} %param.28) | copy-start | bytes 24580
  13.3 6.6 %copy-start.4 = (f32[2048]{0:T(1024)S(1)}, f32[2048]{0:T(1024)}, u32[]{:S(2)}) copy-start(f32[2048]{0:T(1024)} %param.29) | copy-start | bytes 24580
  13.3 6.6 %copy-start.5 = (s32[512]{0:T(512)S(1)}, s32[512]{0:T(512)}, u32[]{:S(2)}) copy-start(s32[512]{0:T(512)} %counts_ref.3) | copy-start | bytes 6148
  13.3 6.6 %copy-start.10 = (bf16[384,192]{1,0:T(8,128)(2,1)S(1)}, bf16[384,192]{1,0:T(8,128)(2,1)}, u32[]{:S(2)}) copy-start(bf16[384,192]{1,0:T(8,128)(2,1)} %constant.27.clone.th_ref) | copy-start | bytes 442372
  13.3 6.6 %copy-start.11 = (bf16[384,192]{1,0:T(8,128)(2,1)S(1)}, bf16[384,192]{1,0:T(8,128)(2,1)}, u32[]{:S(2)}) copy-start(bf16[384,192]{1,0:T(8,128)(2,1)} %constant.28.clone.tl_ref) | copy-start | bytes 442372
  16.2 1.4 %copy-start.18 = (bf16[512,2048]{1,0:T(8,128)(2,1)}, bf16[512,2048]{1,0:T(8,128)(2,1)S(1)}, u32[]{:S(2)}) copy-start(bf16[512,2048]{1,0:T(8,128)(2,1)S(1)} %get-tuple-element.16.mask_ref) | copy-start | bytes 6291460
  17.6 1.2 %copy-start.20 = (bf16[384,2048]{1,0:T(8,128)(2,1)}, bf16[384,2048]{1,0:T(8,128)(2,1)S(1)}, u32[]{:S(2)}) copy-start(bf16[384,2048]{1,0:T(8,128)(2,1)S(1)} %get-tuple-element.14.bh_ref) | copy-start | bytes 4718596
  18.7 1.2 %copy-start.23 = (bf16[384,2048]{1,0:T(8,128)(2,1)}, bf16[384,2048]{1,0:T(8,128)(2,1)S(1)}, u32[]{:S(2)}) copy-start(bf16[384,2048]{1,0:T(8,128)(2,1)S(1)} %get-tuple-element.15.bl_ref) | copy-start | bytes 4718596
  19.9 8.2 %copy-start.26 = (f32[128,2048]{1,0:T(8,128)}, f32[128,2048]{1,0:T(8,128)S(1)}, u32[]{:S(2)}) copy-start(f32[128,2048]{1,0:T(8,128)S(1)} %get-tuple-element.13.a_ref) | copy-start | bytes 3145732
  20.0 1.9 %copy-start.19 = (bf16[512,2048]{1,0:T(8,128)(2,1)S(1)}, bf16[512,2048]{1,0:T(8,128)(2,1)}, u32[]{:S(2)}) copy-start(bf16[512,2048]{1,0:T(8,128)(2,1)} %copy-done.18) | copy-start | bytes 6291460
  21.9 1.4 %copy-start.21 = (bf16[384,2048]{1,0:T(8,128)(2,1)S(1)}, bf16[384,2048]{1,0:T(8,128)(2,1)}, u32[]{:S(2)}) copy-start(bf16[384,2048]{1,0:T(8,128)(2,1)} %copy-done.20) | copy-start | bytes 4718596
  23.3 1.4 %copy-start.24 = (bf16[384,2048]{1,0:T(8,128)(2,1)S(1)}, bf16[384,2048]{1,0:T(8,128)(2,1)}, u32[]{:S(2)}) copy-start(bf16[384,2048]{1,0:T(8,128)(2,1)} %copy-done.23) | copy-start | bytes 4718596
  24.7 15.5 %copy-start.28 = (f32[3,36864]{1,0:T(4,128)S(1)}, f32[3,36864]{1,0:T(4,128)}, u32[]{:S(2)}) copy-start(f32[3,36864]{1,0:T(4,128)} %param.22) | copy-start | bytes 1327108
  28.1 23.5 %all-to-all-start.1 = ((f32[64,4,128]{2,1,0:T(4,128)}), f32[64,4,128]{2,1,0:T(4,128)S(1)}, u32[]{:S(2)}, u32[]{:S(2)}) async-start(f32[64,4,128]{2,1,0:T(4,128)} %bitcast.7), calls=%async_computation.1 | async-start | bytes 262144 | tf_op jit(solution)/shard_map/all_to_all | solution.py:469
  40.7 11.0 %copy-start.6 = (bf16[256,512]{1,0:T(8,128)(2,1)S(1)}, bf16[256,512]{1,0:T(8,128)(2,1)}, u32[]{:S(2)}) copy-start(bf16[256,512]{1,0:T(8,128)(2,1)} %constant.29.clone.yih_ref) | copy-start | bytes 786436
  40.7 10.9 %copy-start.7 = (bf16[256,512]{1,0:T(8,128)(2,1)S(1)}, bf16[256,512]{1,0:T(8,128)(2,1)}, u32[]{:S(2)}) copy-start(bf16[256,512]{1,0:T(8,128)(2,1)} %constant.30.clone.yil_ref) | copy-start | bytes 786436
  40.7 10.9 %copy-start.8 = (bf16[512,256]{1,0:T(8,128)(2,1)S(1)}, bf16[512,256]{1,0:T(8,128)(2,1)}, u32[]{:S(2)}) copy-start(bf16[512,256]{1,0:T(8,128)(2,1)} %constant.35.clone.yfh_ref) | copy-start | bytes 786436
  40.7 10.9 %copy-start.9 = (bf16[512,256]{1,0:T(8,128)(2,1)S(1)}, bf16[512,256]{1,0:T(8,128)(2,1)}, u32[]{:S(2)}) copy-start(bf16[512,256]{1,0:T(8,128)(2,1)} %constant.36.clone.yfl_ref) | copy-start | bytes 786436
  40.7 10.9 %copy-start.12 = (bf16[384,256]{1,0:T(8,128)(2,1)S(1)}, bf16[384,256]{1,0:T(8,128)(2,1)}, u32[]{:S(2)}) copy-start(bf16[384,256]{1,0:T(8,128)(2,1)} %constant.31.clone.xih_ref) | copy-start | bytes 589828
  40.7 10.9 %copy-start.13 = (bf16[384,256]{1,0:T(8,128)(2,1)S(1)}, bf16[384,256]{1,0:T(8,128)(2,1)}, u32[]{:S(2)}) copy-start(bf16[384,256]{1,0:T(8,128)(2,1)} %constant.32.clone.xil_ref) | copy-start | bytes 589828
  40.8 10.9 %copy-start.14 = (bf16[256,384]{1,0:T(8,128)(2,1)S(1)}, bf16[256,384]{1,0:T(8,128)(2,1)}, u32[]{:S(2)}) copy-start(bf16[256,384]{1,0:T(8,128)(2,1)} %constant.33.clone.xfh_ref) | copy-start | bytes 589828
  40.8 10.9 %copy-start.15 = (bf16[256,384]{1,0:T(8,128)(2,1)S(1)}, bf16[256,384]{1,0:T(8,128)(2,1)}, u32[]{:S(2)}) copy-start(bf16[256,384]{1,0:T(8,128)(2,1)} %constant.34.clone.xfl_ref) | copy-start | bytes 589828
  41.5 1.4 %copy-start.16 = (bf16[8,256,512]{2,1,0:T(8,128)(2,1)}, bf16[8,256,512]{2,1,0:T(8,128)(2,1)S(1)}, u32[]{:S(2)}) copy-start(bf16[8,256,512]{2,1,0:T(8,128)(2,1)S(1)} %get-tuple-element.12.hot_ref) | copy-start | bytes 6291460
  51.7 1.6 %copy-start.17 = (bf16[8,256,512]{2,1,0:T(8,128)(2,1)S(1)}, bf16[8,256,512]{2,1,0:T(8,128)(2,1)}, u32[]{:S(2)}) copy-start(bf16[8,256,512]{2,1,0:T(8,128)(2,1)} %copy-done.16) | copy-start | bytes 6291460
  53.3 25.2 %copy-start.22 = (bf16[384,2048]{1,0:T(8,128)(2,1)S(1)}, bf16[384,2048]{1,0:T(8,128)(2,1)}, u32[]{:S(2)}) copy-start(bf16[384,2048]{1,0:T(8,128)(2,1)} %copy-done.20) | copy-start | bytes 4718596
  53.3 25.2 %copy-start.25 = (bf16[384,2048]{1,0:T(8,128)(2,1)S(1)}, bf16[384,2048]{1,0:T(8,128)(2,1)}, u32[]{:S(2)}) copy-start(bf16[384,2048]{1,0:T(8,128)(2,1)} %copy-done.23) | copy-start | bytes 4718596
  53.3 25.2 %copy-start.27 = (f32[128,2048]{1,0:T(8,128)S(1)}, f32[128,2048]{1,0:T(8,128)}, u32[]{:S(2)}) copy-start(f32[128,2048]{1,0:T(8,128)} %copy-done.26) | copy-start | bytes 3145732
where the time goes:
time: 94.6 us; the launch traced here: 93.9 us
  blocking collectives  28.1 us (30%)
  starting transfers between devices  22.3 us (24%)
  Pallas kernels  18.9 us (20%)
  local copies, waits for them, and re-layouts  15.7 us (17%)
  waiting for transfers between devices  8.73 us (9%)
    all_to_all x1, blocking collectives, over_sheets(): lax.all_to_all(sent, 'pw', split_axis=0, concat_axis=0, tiled=True)  15.7 us
    unnamed x59, local copies, waits for them, and re-layouts  14.2 us
    all_to_all x1, blocking collectives, body(): return lax.all_to_all(done, 'tg', split_axis=0, concat_axis=0, tiled=True)  12.4 us
    all_to_all x1, starting transfers between devices, over_sheets(): lax.all_to_all(sent, 'pw', split_axis=0, concat_axis=0, tiled=True)  12.1 us
    all_to_all x1, starting transfers between devices, body(): lax.all_to_all(orbital_coefficients, 'tg', split_axis=0, concat_axis=0, t...  10.1 us
    pallas_call x1, Pallas kernels, plane_work(): call(plane_kernel, 0, 12, shape((SHEETS * ROWS, 2 * STICKS)), [pltpu.VMEM...  9.55 us
    all_to_all x1, waiting for transfers between devices, over_sheets(): lax.all_to_all(sent, 'pw', split_axis=0, concat_axis=0, tiled=True)  8.73 us
    pallas_call x1, Pallas kernels, project(): call(project_kernel, 2, 9, shape((SHEETS * ROWS, 2 * STICKS)), [pltpu.VME...  3.38 us
  transfers between devices with their start and end apart: 2, of which 1 were waited for; matrix products, arithmetic and copies ran while one was open for 2% of the time, Pallas kernels for 4%

commit v1 on v0

--- a/solution.py
+++ b/solution.py
@@ -44,6 +44,15 @@
     return np.concatenate([np.cos(turns), np.sin(turns)], axis=0)
 
 
+def fold_matrix():
+    fold = np.zeros((EDGE, 256))
+    for z in range(EDGE):
+        g = z if z < EDGE // 2 else z - EDGE
+        fold[z, abs(g)] = 1.0
+        fold[z, 128 + abs(g)] = np.sign(g)
+    return fold.astype(jnp.bfloat16)
+
+
 def column_phase(freqs, valid):
     turns = (freqs[:, None] * np.arange(EDGE)[None, :] % EDGE) * (2.0 * math.pi / EDGE)
     keep = valid[:, None].astype(np.float64)
@@ -125,10 +134,27 @@
     return jnp.concatenate(rows, axis=0)
 
 
-def table_kernel(sheet_ref, cols_ref, atom_ref, pos_ref, radius_ref, a_ref, bh_ref, bl_ref, mask_ref):
-    sheet = sheet_ref[0]
-    gx, gy = own_lateral(cols_ref, sheet)
+def member_of(atom_row):
+    atoms = lax.broadcasted_iota(jnp.int32, (NATOM, atom_row.shape[1]), 0)
+    return jnp.where(atoms == atom_row, 1.0, 0.0).astype(BF16)
+
+
+def table_kernel(
+    sheet_ref, cols_ref, atom_hbm, pos_hbm, radius_hbm, a_hbm, bh_hbm, bl_hbm,
+    atom_ref, pos_ref, radius_ref, a_ref, bh_ref, bl_ref, in_sem, out_sem,
+):
+    loads = [
+        pltpu.make_async_copy(source, target, in_sem.at[k])
+        for k, (source, target) in enumerate(
+            ((atom_hbm, atom_ref), (pos_hbm, pos_ref), (radius_hbm, radius_ref))
+        )
+    ]
+    for load in loads:
+        load.start()
+    gx, gy = own_lateral(cols_ref, sheet_ref[0])
     gxy = gx * gx + gy * gy
+    for load in loads:
+        load.wait()
     pos = pos_ref[...]
     first = pos.astype(BF16).astype(F32)
     second = (pos - first).astype(BF16).astype(F32)
@@ -142,10 +168,7 @@
     low_g = lax.broadcasted_iota(jnp.int32, (8, PCHUNK), 0).astype(F32)
     for at in range(0, NPROJ, PCHUNK):
         here = slice(at, at + PCHUNK)
-        atoms = lax.broadcasted_iota(jnp.int32, (NATOM, PCHUNK), 0)
-        member = jnp.where(atoms == atom_ref[:, here], 1.0, 0.0).astype(BF16)
-        mask_ref[:, here] = member
-        placed = mul(rows, member, NN)
+        placed = mul(rows, member_of(atom_ref[:, here]), NN)
         tx, ty, tz = (
             placed[axis : axis + 1] + placed[3 + axis : 4 + axis] + placed[6 + axis : 7 + axis]
             for axis in range(3)
@@ -156,30 +179,31 @@
         a_ref[:STICKS, here] = amp * cosine
         a_ref[STICKS:, here] = -amp * sine
         low_c, low_s = sincos_turns(low_g * tz)
-        for bank in range(3):
-            high_g = (
-                lax.broadcasted_iota(jnp.int32, (8, PCHUNK), 0) + bank * 8
-            ) * 8
-            high_g = jnp.where(high_g < EDGE // 2, high_g, high_g - EDGE).astype(F32)
-            high_c, high_s = sincos_turns(high_g * tz)
+        for bank in range(2):
+            high_g = lax.broadcasted_iota(jnp.int32, (8, PCHUNK), 0) * 8 + bank * 64
+            high_c, high_s = sincos_turns(high_g.astype(F32) * tz)
             for pair in range(4):
                 re_rows, im_rows = [], []
                 for inner in range(2):
                     row = pair * 2 + inner
                     hc, hs = high_c[row : row + 1], high_s[row : row + 1]
-                    first_g = (bank * 8 + row) * 8
-                    first_g = first_g if first_g < EDGE // 2 else first_g - EDGE
-                    g = low_g + float(first_g)
+                    g = low_g + float((bank * 8 + row) * 8)
                     amp_z = jnp.exp(-spread * (g * g))
                     re_rows.append(amp_z * (hc * low_c - hs * low_s))
                     im_rows.append(-amp_z * (hs * low_c + hc * low_s))
                 z = (bank * 8 + pair * 2) * 8
-                high, low = split(jnp.concatenate(re_rows, axis=0))
-                bh_ref[z : z + 16, here] = high
-                bl_ref[z : z + 16, here] = low
-                high, low = split(jnp.concatenate(im_rows, axis=0))
-                bh_ref[EDGE + z : EDGE + z + 16, here] = high
-                bl_ref[EDGE + z : EDGE + z + 16, here] = low
+                for base, found in ((z, re_rows), (128 + z, im_rows)):
+                    high, low = split(jnp.concatenate(found, axis=0))
+                    bh_ref[base : base + 16, here] = high
+                    bl_ref[base : base + 16, here] = low
+    stores = [
+        pltpu.make_async_copy(source, target, out_sem.at[k])
+        for k, (source, target) in enumerate(((a_ref, a_hbm), (bh_ref, bh_hbm), (bl_ref, bl_hbm)))
+    ]
+    for store in stores:
+        store.start()
+    for store in stores:
+        store.wait()
 
 
 def rows_of(re, im):
@@ -197,22 +221,40 @@
 
 
 def project_kernel(
-    sheet_ref, counts_ref, sticks_ref, th_ref, tl_ref, a_ref, bh_ref, bl_ref, mask_ref, diag_ref, dij_ref,
-    out_ref, becp_ref,
+    sheet_ref, counts_ref, sticks_ref, th_ref, tl_ref, fold_ref, atom_ref, diag_ref, dij_ref, a_hbm, bh_hbm, bl_hbm,
+    out_ref, becp_ref, mask_ref, a_ref, bh_ref, bl_ref, sem,
 ):
+    loads = [
+        pltpu.make_async_copy(source, target, sem.at[k])
+        for k, (source, target) in enumerate(((bh_hbm, bh_ref), (bl_hbm, bl_ref), (a_hbm, a_ref)))
+    ]
+    for load in loads:
+        load.start()
+    for at in range(0, NPROJ, PCHUNK):
+        mask_ref[:, at : at + PCHUNK] = member_of(atom_ref[:, at : at + PCHUNK])
     coeff = split(live_sticks(sticks_ref, counts_ref, sheet_ref[0]))
     both = dot3((th_ref[...], tl_ref[...]), coeff, NT)
     with_cos, with_sin = both[:EDGE], both[EDGE:]
     by_depth = with_cos + jnp.concatenate([-with_sin[:, STICKS:], with_sin[:, :STICKS]], axis=1)
+    folded = mul(coeff[0], fold_ref[...], NN) + mul(coeff[1], fold_ref[...], NN)
+    paired = split(
+        jnp.concatenate(
+            [
+                jnp.concatenate([folded[:STICKS, :128], folded[STICKS:, 128:]], axis=1),
+                jnp.concatenate([folded[STICKS:, :128], -folded[:STICKS, 128:]], axis=1),
+            ],
+            axis=0,
+        )
+    )
     for plane in range(DEPTH):
         out_ref[every(plane), :] = by_depth[plane * SHEETS : (plane + 1) * SHEETS]
     out_ref[every(DEPTH), :] = jnp.zeros((SHEETS, 128), F32)
+    for load in loads:
+        load.wait()
     for at in range(0, NPROJ, PCHUNK):
         here = slice(at, at + PCHUNK)
-        with_re = dot3(coeff, (bh_ref[:EDGE, here], bl_ref[:EDGE, here]), NN)
-        with_im = dot3(coeff, (bh_ref[EDGE:, here], bl_ref[EDGE:, here]), NN)
-        y_re = with_re[:STICKS] + with_im[STICKS:]
-        y_im = with_re[STICKS:] - with_im[:STICKS]
+        y = dot3(paired, (bh_ref[:, here], bl_ref[:, here]), NN)
+        y_re, y_im = y[:STICKS], y[STICKS:]
         a_re, a_im = a_ref[:STICKS, here], a_ref[STICKS:, here]
         becp_ref[0:1, here] = jnp.sum(a_re * y_re + a_im * y_im, axis=0, keepdims=True)
         becp_ref[1:2, here] = jnp.sum(a_re * y_im - a_im * y_re, axis=0, keepdims=True)
@@ -233,27 +275,16 @@
             out_ref[row : row + 1, :] = w[part][:, block * 128 : (block + 1) * 128]
 
 
-def spread_kernel(cols_ref, x_ref, hot_ref):
+def plane_kernel(
+    cols_ref, sticks_ref, potential_ref,
+    yih_ref, yil_ref, xih_ref, xil_ref, xfh_ref, xfl_ref, yfh_ref, yfl_ref,
+    out_ref, x_ref, v_ref, hot_ref, left_ref, pick_ref,
+):
     half = SHEETS // 2
     x, y = lateral_split(jnp.concatenate([cols_ref[:half, :], cols_ref[half:, :]], axis=1))
     x, y = x + CUT, y + CUT
     x_ref[0] = x >> 1
     x_ref[1] = (x & 1) * 128 + y
-    rows256 = lax.broadcasted_iota(jnp.int32, (256, 128), 0)
-    per = CHUNK // 128
-    for chunk in range(CHUNKS):
-        for inner in range(per):
-            r = chunk * per + inner
-            lanes = slice(inner * 128, (inner + 1) * 128)
-            hot_ref[chunk, :, lanes] = jnp.where(rows256 == x_ref[1, r : r + 1, :], 1.0, 0.0).astype(BF16)
-
-
-def plane_kernel(
-    x_ref, hot_ref, sticks_ref, potential_ref,
-    yih_ref, yil_ref, xih_ref, xil_ref, xfh_ref, xfl_ref, yfh_ref, yfl_ref,
-    out_ref, v_ref, left_ref, pick_ref,
-):
-    half = SHEETS // 2
     for plane in range(DEPTH):
         rows = sticks_ref[every(plane), :]
         top, bottom = rows[:half], rows[half:]
@@ -267,6 +298,7 @@
     summed = jnp.sum(sticks_ref[every(DEPTH), :], axis=0, keepdims=True)
     out_ref[every(DEPTH), :] = jnp.broadcast_to(summed, (SHEETS, 128))
     rows64 = lax.broadcasted_iota(jnp.int32, (HALF_ROWS, 128), 0)
+    rows256 = lax.broadcasted_iota(jnp.int32, (256, 128), 0)
     per = CHUNK // 128
     total = jnp.zeros((12 * HALF_ROWS, 256), F32)
     for chunk in range(CHUNKS):
@@ -274,11 +306,12 @@
         for inner in range(per):
             r = chunk * per + inner
             lanes = slice(inner * 128, (inner + 1) * 128)
-            member = rows64 == x_ref[0, r : r + 1, :]
+            member = jnp.where(rows64 == x_ref[0, r : r + 1, :], 1.0, 0.0).astype(BF16)
+            hot_ref[chunk, :, lanes] = jnp.where(rows256 == x_ref[1, r : r + 1, :], 1.0, 0.0).astype(BF16)
             for k in range(12):
-                left_ref[slot, k * HALF_ROWS : (k + 1) * HALF_ROWS, lanes] = jnp.where(
-                    member, v_ref[k, r : r + 1, :], 0.0
-                ).astype(BF16)
+                value = jnp.broadcast_to(v_ref[k, r : r + 1, :], (16, 128)).astype(BF16)
+                value = jnp.concatenate([value] * (HALF_ROWS // 16), axis=0)
+                left_ref[slot, k * HALF_ROWS : (k + 1) * HALF_ROWS, lanes] = member * value
         total = total + mul(left_ref[slot], hot_ref[chunk], NT)
     grids = []
     for plane in range(DEPTH):
@@ -344,11 +377,11 @@
 
 
 def finish_kernel(
-    sheet_ref, counts_ref, cols_ref, sticks_ref, back_ref, a_ref, bh_ref, bl_ref, th_ref, tl_ref, out_ref
+    sheet_ref, counts_ref, cols_ref, sticks_ref, back_ref, a_ref, bh_ref, bl_ref, th_ref, tl_ref, fold_ref,
+    out_ref,
 ):
     sheet = sheet_ref[0]
-    vnl_re = jnp.zeros((2 * STICKS, EDGE), F32)
-    vnl_im = jnp.zeros((2 * STICKS, EDGE), F32)
+    vnl = jnp.zeros((2 * STICKS, 256), F32)
     step = 2 * PCHUNK
     for at in range(0, NPROJ, step):
         here = slice(at, at + step)
@@ -370,16 +403,25 @@
         weighted = split(
             jnp.concatenate([a_re * w_re - a_im * w_im, a_re * w_im + a_im * w_re], axis=0)
         )
-        vnl_re = vnl_re + dot3(weighted, (bh_ref[:EDGE, here], bl_ref[:EDGE, here]), NT)
-        vnl_im = vnl_im + dot3(weighted, (bh_ref[EDGE:, here], bl_ref[EDGE:, here]), NT)
+        vnl = vnl + dot3(weighted, (bh_ref[:, here], bl_ref[:, here]), NT)
+    vnl = split(
+        jnp.concatenate(
+            [
+                jnp.concatenate([vnl[:STICKS, :128], -vnl[STICKS:, 128:]], axis=1),
+                jnp.concatenate([vnl[STICKS:, :128], vnl[:STICKS, 128:]], axis=1),
+            ],
+            axis=0,
+        )
+    )
+    vnl = mul(vnl[0], fold_ref[...], NT) + mul(vnl[1], fold_ref[...], NT)
     back = jnp.concatenate([back_ref[every(plane), :] for plane in range(DEPTH)], axis=0)
     back = split(back.T)
     with_cos = dot3(back, (th_ref[:EDGE], tl_ref[:EDGE]), NN)
     with_sin = dot3(back, (th_ref[EDGE:], tl_ref[EDGE:]), NN)
     box_scale = 1.0 / float(EDGE) ** 3
     sums = (
-        (with_cos[:STICKS] + with_sin[STICKS:]) * box_scale + (vnl_re[:STICKS] - vnl_im[STICKS:]),
-        (with_cos[STICKS:] - with_sin[:STICKS]) * box_scale + (vnl_re[STICKS:] + vnl_im[:STICKS]),
+        (with_cos[:STICKS] + with_sin[STICKS:]) * box_scale + vnl[:STICKS],
+        (with_cos[STICKS:] - with_sin[:STICKS]) * box_scale + vnl[STICKS:],
     )
     gx, gy = own_lateral(cols_ref, sheet)
     gz = lax.broadcasted_iota(jnp.int32, (1, EDGE), 1)
@@ -393,14 +435,13 @@
             out_ref[team, part] = jnp.where(live, value, 0.0)
 
 
-def call(kernel, n_scalars, n_inputs, outs, scratch=(), flops=0, limit=20 << 20):
-    smem = pl.BlockSpec(memory_space=pltpu.SMEM)
-    vmem = pl.BlockSpec(memory_space=pltpu.VMEM)
+def call(kernel, places, outs, scratch=(), flops=0, limit=20 << 20, out_place=pltpu.VMEM):
+    kinds = {"s": pltpu.SMEM, "v": pltpu.VMEM, "h": pltpu.HBM}
     return pl.pallas_call(
         kernel,
         out_shape=outs,
-        in_specs=[smem] * n_scalars + [vmem] * n_inputs,
-        out_specs=jax.tree.map(lambda _: vmem, outs),
+        in_specs=[pl.BlockSpec(memory_space=kinds[place]) for place in places],
+        out_specs=jax.tree.map(lambda _: pl.BlockSpec(memory_space=out_place), outs),
         scratch_shapes=list(scratch),
         compiler_params=pltpu.CompilerParams(vmem_limit_bytes=limit),
         cost_estimate=pl.CostEstimate(flops=flops, bytes_accessed=4 << 20, transcendentals=0),
@@ -411,56 +452,61 @@
     return jax.ShapeDtypeStruct(dims, dtype)
 
 
+TABLES = (((2 * STICKS, NPROJ), F32), ((256, NPROJ), BF16), ((256, NPROJ), BF16))
+
+
 def make_tables(sheet, cols, proj_atom, atom_pos, proj_radius):
     return call(
-        table_kernel, 1, 4,
-        (
-            shape((2 * STICKS, NPROJ)),
-            shape((2 * EDGE, NPROJ), BF16),
-            shape((2 * EDGE, NPROJ), BF16),
-            shape((NATOM, NPROJ), BF16),
-        ),
+        table_kernel, "svhhh", tuple(shape(*table) for table in TABLES),
+        [
+            pltpu.VMEM((1, NPROJ), jnp.int32),
+            pltpu.VMEM((3, NATOM), F32),
+            pltpu.VMEM((1, NPROJ), F32),
+            *(pltpu.VMEM(*table) for table in TABLES),
+            pltpu.SemaphoreType.DMA((3,)),
+            pltpu.SemaphoreType.DMA((3,)),
+        ],
         flops=2 << 30,
+        out_place=pltpu.HBM,
     )(sheet, cols, proj_atom.reshape(1, NPROJ), atom_pos, proj_radius.reshape(1, NPROJ))
 
 
-def project(sheet, counts, sticks, tables, proj_diag, dij):
-    a, bh, bl, mask = tables
+def project(sheet, counts, sticks, tables, proj_atom, proj_diag, dij):
     return call(
-        project_kernel, 2, 9, shape((SHEETS * ROWS, 2 * STICKS)), [pltpu.VMEM((2, NPROJ), F32)], flops=3 << 30
+        project_kernel, "ssvvvvvvvhhh", shape((SHEETS * ROWS, 2 * STICKS)),
+        [
+            pltpu.VMEM((2, NPROJ), F32),
+            pltpu.VMEM((NATOM, NPROJ), BF16),
+            *(pltpu.VMEM(*table) for table in TABLES),
+            pltpu.SemaphoreType.DMA((3,)),
+        ],
+        flops=3 << 30,
     )(
-        sheet, counts, sticks, *split_table(depth_table()), a, bh, bl, mask,
-        proj_diag.reshape(1, NPROJ), dij.reshape(1, NPROJ),
-    )
-
-
-def spread(cols):
-    return call(
-        spread_kernel, 0, 1,
-        (shape((2, SHEETS // 2, 128), jnp.int32), shape((CHUNKS, 256, CHUNK), BF16)),
-        flops=1 << 30,
-    )(cols)
-
-
-def plane_work(spots, sticks, potential):
+        sheet, counts, sticks, *split_table(depth_table()), fold_matrix(),
+        proj_atom.reshape(1, NPROJ), proj_diag.reshape(1, NPROJ), dij.reshape(1, NPROJ), *tables,
+    )
+
+
+def plane_work(cols, sticks, potential):
     tables = [piece for table in lateral_tables() for piece in split_table(table)]
     padded = jnp.pad(potential.reshape(DEPTH, EDGE, EDGE), ((0, 0), (0, 0), (0, 256 - EDGE)))
     return call(
-        plane_kernel, 0, 12, shape((SHEETS * ROWS, 2 * STICKS)),
+        plane_kernel, "v" * 11, shape((SHEETS * ROWS, 2 * STICKS)),
         [
+            pltpu.VMEM((2, SHEETS // 2, 128), jnp.int32),
             pltpu.VMEM((12, SHEETS // 2, 128), F32),
+            pltpu.VMEM((CHUNKS, 256, CHUNK), BF16),
             pltpu.VMEM((2, 12 * HALF_ROWS, CHUNK), BF16),
             pltpu.VMEM((6, SHEETS // 2, 128), F32),
         ],
         flops=8 << 30,
         limit=28 << 20,
-    )(*spots, sticks, padded, *tables)
+    )(cols, sticks, padded, *tables)
 
 
 def finish(sheet, counts, cols, sticks, back, tables):
-    a, bh, bl, _ = tables
-    return call(finish_kernel, 2, 8, shape((TEAMS, 2, LINES, EDGE)), flops=3 << 30)(
-        sheet, counts, cols, sticks, back, a, bh, bl, *split_table(depth_table())
+    return call(finish_kernel, "ssvvvvvvvvv", shape((TEAMS, 2, LINES, EDGE)), flops=3 << 30)(
+        sheet, counts, cols, sticks, back, *tables, *split_table(depth_table()), fold_matrix()
     )
 
 
@@ -485,9 +531,9 @@
     cols = jnp.transpose(layout, (1, 0, 2)).reshape(SHEETS, STICKS)
     sticks = lax.all_to_all(orbital_coefficients, "tg", split_axis=0, concat_axis=0, tiled=True)
     tables = make_tables(sheet, cols, proj_atom, atom_pos, proj_radius)
-    by_depth = project(sheet, stick_count, sticks, tables, proj_diag, ionic_pseudo_dij)
+    by_depth = project(sheet, stick_count, sticks, tables, proj_atom, proj_diag, ionic_pseudo_dij)
     by_plane = over_sheets(by_depth)
-    picked = plane_work(spread(cols), by_plane, potential)
+    picked = plane_work(cols, by_plane, potential)
     back = over_sheets(picked)
     done = finish(sheet, stick_count, cols, sticks, back, tables)
     return lax.all_to_all(done, "tg", split_axis=0, concat_axis=0, tiled=True)

time: 94.6 us -> 88.4 us (0.934)
  local copies, waits for them, and re-layouts: 15.7 us -> 9.88 us
    unnamed x59 -> x53, local copies, waits for them, and re-layouts: 14.2 us -> 6.44 us
    pad x1, local copies, waits for them, and re-layouts: 0.04 us -> 1.19 us  [plane_work(): jnp.pad(potential.reshape(DEPTH, EDGE, EDGE), ((0, 0), (0, 0), (0, 256 -...]
    pallas_call x5 -> x4, Pallas kernels: 18.9 us -> 18.4 us  [the longest x1 9.36 us: plane_work(): call(plane_kernel, 'v' * 11, shape((SHEETS * ROWS, 2 * STICKS)), [pltpu.V...]
  transfers between devices with their start and end apart: 2 -> 2, of which waited for: 1 -> 1; matrix products, arithmetic and copies ran while one was open for 2% -> 3% of each run, Pallas kernels for 4% -> 3%
where the time goes in v1:
time: 88.4 us; the launch traced here: 87.8 us
  blocking collectives  28.1 us (32%)
  starting transfers between devices  22.3 us (25%)
  Pallas kernels  18.4 us (21%)
  local copies, waits for them, and re-layouts  9.88 us (11%)
  waiting for transfers between devices  8.93 us (10%)
    all_to_all x1, blocking collectives, over_sheets(): lax.all_to_all(sent, 'pw', split_axis=0, concat_axis=0, tiled=True)  15.7 us
    all_to_all x1, blocking collectives, body(): return lax.all_to_all(done, 'tg', split_axis=0, concat_axis=0, tiled=True)  12.4 us
    all_to_all x1, starting transfers between devices, over_sheets(): lax.all_to_all(sent, 'pw', split_axis=0, concat_axis=0, tiled=True)  12.2 us
    all_to_all x1, starting transfers between devices, body(): lax.all_to_all(orbital_coefficients, 'tg', split_axis=0, concat_axis=0, t...  10.1 us
    pallas_call x1, Pallas kernels, plane_work(): call(plane_kernel, 'v' * 11, shape((SHEETS * ROWS, 2 * STICKS)), [pltpu.V...  9.36 us
    all_to_all x1, waiting for transfers between devices, over_sheets(): lax.all_to_all(sent, 'pw', split_axis=0, concat_axis=0, tiled=True)  8.93 us
    unnamed x53, local copies, waits for them, and re-layouts  6.44 us
    pallas_call x1, Pallas kernels, project(): call(project_kernel, 'ssvvvvvvvhhh', shape((SHEETS * ROWS, 2 * STICKS)),...  4.15 us
  transfers between devices with their start and end apart: 2, of which 1 were waited for; matrix products, arithmetic and copies ran while one was open for 3% of the time, Pallas kernels for 3%

profile of v1, /device:TPU:1, one launch (start us, length us, event | category | flops | bytes accessed | tf_op | source)
XLA Modules:
  0.0 87.8 jit_solution(6895371210496992597)
XLA Ops:
  0.0 10.1 %all-to-all-start = ((f32[8,2,8,192]{3,2,1,0:T(8,128)}), f32[8,2,8,192]{3,2,1,0:T(8,128)S(1)}, u32[]{:S(2)}, u32[]{:S(2)}) async-start(f32[8,2,8,192]{3,2,1,0:T(8,128)} %param.23), calls=%async_computation | async-start | bytes 262144 | tf_op jit(solution)/shard_map/all_to_all | solution.py:532
  10.2 0.0 slice-start
  10.2 0.7 slice-done
  10.9 0.2 reshape.46
  11.0 0.1 copy.24
  11.1 0.0 copy-start
  11.1 0.0 copy-start.1
  11.1 0.0 copy-start.2
  11.1 0.1 copy.27.cols_ref
  11.2 0.6 copy-done
  11.9 0.0 copy-done.1
  11.9 0.0 copy-done.2
  11.9 0.0 copy-start.4
  11.9 0.0 copy-start.5
  11.9 0.0 copy-start.10
  11.9 0.0 copy-start.11
  11.9 0.0 copy-start.16
  11.9 2.6 %shard_map.217 = (f32[128,2048]{1,0:T(8,128)S(1)}, bf16[256,2048]{1,0:T(8,128)(2,1)S(1)}, bf16[256,2048]{1,0:T(8,128)(2,1)S(1)}) custom-call(s32[1]{0:T(128)} %bitcast.sheet_ref, s32[64,64]{1,0:T(8,128)S(1)} %copy.27.cols_ref, s32[1,2048]{1,0:T(1,128)S(1)} %bitcast.15, f32[3,512]{1,0:T(4,128)S(1)} %copy-done, f32[1,2048]{1,0:T(1,128)S(1)} %bitcast.14), custom_call_target="tpu_custom_call" | custom-call | flops 2147483648 | bytes 4194304 | tf_op jit(solution)/shard_map/pallas_call | solution.py:459
  14.5 0.0 copy-start.19
  14.6 1.0 %copy-done.19 = bf16[256,2048]{1,0:T(8,128)(2,1)} copy-done((bf16[256,2048]{1,0:T(8,128)(2,1)}, bf16[256,2048]{1,0:T(8,128)(2,1)S(1)}, u32[]{:S(2)}) %copy-start.19) | copy-done | bytes 1048600
  15.5 0.0 copy-start.22
  15.5 1.0 %copy-done.22 = bf16[256,2048]{1,0:T(8,128)(2,1)} copy-done((bf16[256,2048]{1,0:T(8,128)(2,1)}, bf16[256,2048]{1,0:T(8,128)(2,1)S(1)}, u32[]{:S(2)}) %copy-start.22) | copy-done | bytes 1048600
  16.5 0.0 copy-start.17
  16.5 0.0 copy-start.3
  16.5 0.0 all-to-all-done.sticks_ref
  16.5 0.0 copy-done.4
  16.5 0.0 copy-done.5
  16.5 0.0 copy-done.10
  16.5 0.0 copy-done.11
  16.5 0.0 copy-done.16
  16.5 0.6 copy-done.3
  17.2 0.0 copy-start.20
  17.2 1.2 %copy-done.20 = bf16[256,2048]{1,0:T(8,128)(2,1)S(1)} copy-done((bf16[256,2048]{1,0:T(8,128)(2,1)S(1)}, bf16[256,2048]{1,0:T(8,128)(2,1)}, u32[]{:S(2)}) %copy-start.20) | copy-done | bytes 1048600
  18.4 1.2 %copy-done.23 = bf16[256,2048]{1,0:T(8,128)(2,1)S(1)} copy-done((bf16[256,2048]{1,0:T(8,128)(2,1)S(1)}, bf16[256,2048]{1,0:T(8,128)(2,1)}, u32[]{:S(2)}) %copy-start.23) | copy-done | bytes 1048600
  19.6 4.2 %shard_map.218 = f32[256,128]{1,0:T(8,128)} custom-call(s32[1]{0:T(128)} %bitcast.sheet_ref, s32[512]{0:T(512)S(1)} %copy-done.5, f32[8,2,8,192]{3,2,1,0:T(8,128)S(1)} %all-to-all-done.sticks_ref, bf16[384,192]{1,0:T(8,128)(2,1)S(1)} %copy-done.11, bf16[384,192]{1,0:T(8,128)(2,1)S(1)} %copy-done.10, bf16[192,256]{1,0:T(8,128)(2,1)S(1)} %copy-done.16, ...), custom_call_target="tpu_custom_call" | custom-call | flops 3221225472 | bytes 4194304 | tf_op jit(solution)/shard_map/pallas_call | solution.py:475
  23.8 0.0 copy-done.17
  23.8 12.2 %all-to-all-start.1 = ((f32[64,4,128]{2,1,0:T(4,128)}), f32[64,4,128]{2,1,0:T(4,128)S(1)}, u32[]{:S(2)}, u32[]{:S(2)}) async-start(f32[64,4,128]{2,1,0:T(4,128)} %bitcast.7), calls=%async_computation.1 | async-start | bytes 262144 | tf_op jit(solution)/shard_map/all_to_all | solution.py:515
  36.0 0.0 copy-done.25
  36.0 0.0 copy-start.12
  36.0 0.0 copy-start.13
  36.0 0.0 copy-start.14
  36.0 0.0 copy-start.15
  36.0 1.2 %reshape.54 = f32[3,192,192]{2,1,0:T(8,128)} reshape(f32[3,36864]{1,0:T(4,128)S(1)} %copy-done.25) | data formatting | bytes 884736 | tf_op jit(solution)/shard_map/reshape | solution.py:492
  37.2 1.2 %pad.4.potential_ref = f32[3,192,256]{2,1,0:T(8,128)S(1)} pad(f32[3,192,192]{2,1,0:T(8,128)} %reshape.54, f32[]{:T(128)} %constant.28.clone.1), padding=0_0x0_0x0_64 | pad | bytes 1032196 | tf_op jit(solution)/shard_map/jit(_pad)/pad | solution.py:492
  38.4 8.9 %all-to-all-done.1 = f32[64,4,128]{2,1,0:T(4,128)S(1)} async-done(((f32[64,4,128]{2,1,0:T(4,128)}), f32[64,4,128]{2,1,0:T(4,128)S(1)}, u32[]{:S(2)}, u32[]{:S(2)}) %all-to-all-start.1) | async-done | bytes 131104 | tf_op jit(solution)/shard_map/all_to_all | solution.py:515
  47.4 0.0 copy-done.12
  47.4 0.0 copy-done.13
  47.4 0.0 copy-done.14
  47.4 0.0 copy-done.15
  47.4 0.0 copy-done.6
  47.4 0.0 copy-done.7
  47.4 0.0 copy-done.8
  47.4 0.0 copy-done.9
  47.4 0.0 copy-start.18
  47.4 0.0 copy-start.21
  47.4 0.0 copy-start.24
  47.4 9.4 %shard_map.219 = f32[256,128]{1,0:T(8,128)S(1)} custom-call(s32[64,64]{1,0:T(8,128)S(1)} %copy.27.cols_ref, f32[256,128]{1,0:T(8,128)S(1)} %bitcast.11, f32[3,192,256]{2,1,0:T(8,128)S(1)} %pad.4.potential_ref, bf16[256,512]{1,0:T(8,128)(2,1)S(1)} %copy-done.9, bf16[256,512]{1,0:T(8,128)(2,1)S(1)} %copy-done.8, bf16[384,256]{1,0:T(8,128)(2,1)S(1)} %copy-done.15, ...), custom_call_target="tpu_custom_call" | custom-call | flops 8589934592 | bytes 4194304 | tf_op jit(solution)/shard_map/pallas_call | solution.py:493
  56.8 15.7 %all_to_all.20 = f32[64,4,128]{2,1,0:T(4,128)S(1)} all-to-all(f32[64,4,128]{2,1,0:T(4,128)S(1)} %bitcast.12), channel_id=1, replica_groups=mesh['tg'=8,'pw'=64] {'pw'}, dimensions={0} | all-to-all | bytes 262144 | tf_op jit(solution)/shard_map/all_to_all | solution.py:515
  72.5 0.0 copy-done.18
  72.5 0.0 copy-done.21
  72.5 0.0 copy-done.24
  72.5 2.2 %shard_map.220 = f32[8,2,8,192]{3,2,1,0:T(8,128)S(1)} custom-call(s32[1]{0:T(128)} %bitcast.sheet_ref, s32[512]{0:T(512)S(1)} %copy-done.5, s32[64,64]{1,0:T(8,128)S(1)} %copy.27.cols_ref, f32[8,2,8,192]{3,2,1,0:T(8,128)S(1)} %all-to-all-done.sticks_ref, f32[256,128]{1,0:T(8,128)S(1)} %bitcast.13, f32[128,2048]{1,0:T(8,128)S(1)} %copy-done.18, ...), custom_call_target="tpu_custom_call" | custom-call | flops 3221225472 | bytes 4194304 | tf_op jit(solution)/shard_map/pallas_call | solution.py:508
  74.7 12.4 %all_to_all.21 = f32[8,2,8,192]{3,2,1,0:T(8,128)S(1)} all-to-all(f32[8,2,8,192]{3,2,1,0:T(8,128)S(1)} %shard_map.220), channel_id=1, replica_groups=mesh['tg'=8,'pw'=64] {'tg'}, dimensions={0} | all-to-all | bytes 196608 | tf_op jit(solution)/shard_map/all_to_all | solution.py:539
  87.1 0.7 copy.29
  (6 shorter events, 0.0 us)
Async XLA Ops:
  0.0 16.5 %all-to-all-start = ((f32[8,2,8,192]{3,2,1,0:T(8,128)}), f32[8,2,8,192]{3,2,1,0:T(8,128)S(1)}, u32[]{:S(2)}, u32[]{:S(2)}) async-start(f32[8,2,8,192]{3,2,1,0:T(8,128)} %param.23), calls=%async_computation | async-start | bytes 262144 | tf_op jit(solution)/shard_map/all_to_all | solution.py:532
  10.2 0.7 slice-start
  11.1 0.7 copy-start
  11.1 0.7 copy-start.1
  11.1 0.7 copy-start.2
  11.9 4.6 %copy-start.4 = (f32[2048]{0:T(1024)S(1)}, f32[2048]{0:T(1024)}, u32[]{:S(2)}) copy-start(f32[2048]{0:T(1024)} %param.31) | copy-start | bytes 24580
  11.9 4.6 %copy-start.5 = (s32[512]{0:T(512)S(1)}, s32[512]{0:T(512)}, u32[]{:S(2)}) copy-start(s32[512]{0:T(512)} %counts_ref.3) | copy-start | bytes 6148
  11.9 4.6 %copy-start.10 = (bf16[384,192]{1,0:T(8,128)(2,1)S(1)}, bf16[384,192]{1,0:T(8,128)(2,1)}, u32[]{:S(2)}) copy-start(bf16[384,192]{1,0:T(8,128)(2,1)} %constant.30.clone.tl_ref) | copy-start | bytes 442372
  11.9 4.6 %copy-start.11 = (bf16[384,192]{1,0:T(8,128)(2,1)S(1)}, bf16[384,192]{1,0:T(8,128)(2,1)}, u32[]{:S(2)}) copy-start(bf16[384,192]{1,0:T(8,128)(2,1)} %constant.29.clone.th_ref) | copy-start | bytes 442372
  11.9 4.6 %copy-start.16 = (bf16[192,256]{1,0:T(8,128)(2,1)S(1)}, bf16[192,256]{1,0:T(8,128)(2,1)}, u32[]{:S(2)}) copy-start(bf16[192,256]{1,0:T(8,128)(2,1)} %constant.31.clone.fold_ref) | copy-start | bytes 294916
  14.5 1.0 %copy-start.19 = (bf16[256,2048]{1,0:T(8,128)(2,1)}, bf16[256,2048]{1,0:T(8,128)(2,1)S(1)}, u32[]{:S(2)}) copy-start(bf16[256,2048]{1,0:T(8,128)(2,1)S(1)} %get-tuple-element.9.bh_hbm.bh_ref) | copy-start | bytes 3145732
  15.5 1.0 %copy-start.22 = (bf16[256,2048]{1,0:T(8,128)(2,1)}, bf16[256,2048]{1,0:T(8,128)(2,1)S(1)}, u32[]{:S(2)}) copy-start(bf16[256,2048]{1,0:T(8,128)(2,1)S(1)} %get-tuple-element.10.bl_hbm.bl_ref) | copy-start | bytes 3145732
  16.5 7.3 %copy-start.17 = (f32[128,2048]{1,0:T(8,128)}, f32[128,2048]{1,0:T(8,128)S(1)}, u32[]{:S(2)}) copy-start(f32[128,2048]{1,0:T(8,128)S(1)} %get-tuple-element.8.a_hbm.a_ref) | copy-start | bytes 3145732
  16.5 0.7 copy-start.3
  17.2 1.2 %copy-start.20 = (bf16[256,2048]{1,0:T(8,128)(2,1)S(1)}, bf16[256,2048]{1,0:T(8,128)(2,1)}, u32[]{:S(2)}) copy-start(bf16[256,2048]{1,0:T(8,128)(2,1)} %copy-done.19) | copy-start | bytes 3145732
  18.4 1.2 %copy-start.23 = (bf16[256,2048]{1,0:T(8,128)(2,1)S(1)}, bf16[256,2048]{1,0:T(8,128)(2,1)}, u32[]{:S(2)}) copy-start(bf16[256,2048]{1,0:T(8,128)(2,1)} %copy-done.22) | copy-start | bytes 3145732
  19.6 16.3 %copy-start.25 = (f32[3,36864]{1,0:T(4,128)S(1)}, f32[3,36864]{1,0:T(4,128)}, u32[]{:S(2)}) copy-start(f32[3,36864]{1,0:T(4,128)} %param.24) | copy-start | bytes 1327108
  23.8 23.5 %all-to-all-start.1 = ((f32[64,4,128]{2,1,0:T(4,128)}), f32[64,4,128]{2,1,0:T(4,128)S(1)}, u32[]{:S(2)}, u32[]{:S(2)}) async-start(f32[64,4,128]{2,1,0:T(4,128)} %bitcast.7), calls=%async_computation.1 | async-start | bytes 262144 | tf_op jit(solution)/shard_map/all_to_all | solution.py:515
  36.0 11.4 %copy-start.12 = (bf16[256,384]{1,0:T(8,128)(2,1)S(1)}, bf16[256,384]{1,0:T(8,128)(2,1)}, u32[]{:S(2)}) copy-start(bf16[256,384]{1,0:T(8,128)(2,1)} %constant.37.clone.xfl_ref) | copy-start | bytes 589828
  36.0 11.4 %copy-start.13 = (bf16[256,384]{1,0:T(8,128)(2,1)S(1)}, bf16[256,384]{1,0:T(8,128)(2,1)}, u32[]{:S(2)}) copy-start(bf16[256,384]{1,0:T(8,128)(2,1)} %constant.36.clone.xfh_ref) | copy-start | bytes 589828
  36.0 11.3 %copy-start.14 = (bf16[384,256]{1,0:T(8,128)(2,1)S(1)}, bf16[384,256]{1,0:T(8,128)(2,1)}, u32[]{:S(2)}) copy-start(bf16[384,256]{1,0:T(8,128)(2,1)} %constant.35.clone.xil_ref) | copy-start | bytes 589828
  36.0 11.3 %copy-start.15 = (bf16[384,256]{1,0:T(8,128)(2,1)S(1)}, bf16[384,256]{1,0:T(8,128)(2,1)}, u32[]{:S(2)}) copy-start(bf16[384,256]{1,0:T(8,128)(2,1)} %constant.34.clone.xih_ref) | copy-start | bytes 589828
  37.2 10.2 %copy-start.6 = (bf16[512,256]{1,0:T(8,128)(2,1)S(1)}, bf16[512,256]{1,0:T(8,128)(2,1)}, u32[]{:S(2)}) copy-start(bf16[512,256]{1,0:T(8,128)(2,1)} %constant.39.clone.yfl_ref) | copy-start | bytes 786436
  37.2 10.2 %copy-start.7 = (bf16[512,256]{1,0:T(8,128)(2,1)S(1)}, bf16[512,256]{1,0:T(8,128)(2,1)}, u32[]{:S(2)}) copy-start(bf16[512,256]{1,0:T(8,128)(2,1)} %constant.38.clone.yfh_ref) | copy-start | bytes 786436
  37.2 10.2 %copy-start.8 = (bf16[256,512]{1,0:T(8,128)(2,1)S(1)}, bf16[256,512]{1,0:T(8,128)(2,1)}, u32[]{:S(2)}) copy-start(bf16[256,512]{1,0:T(8,128)(2,1)} %constant.33.clone.yil_ref) | copy-start | bytes 786436
  37.2 10.2 %copy-start.9 = (bf16[256,512]{1,0:T(8,128)(2,1)S(1)}, bf16[256,512]{1,0:T(8,128)(2,1)}, u32[]{:S(2)}) copy-start(bf16[256,512]{1,0:T(8,128)(2,1)} %constant.32.clone.yih_ref) | copy-start | bytes 786436
  47.4 25.1 %copy-start.18 = (f32[128,2048]{1,0:T(8,128)S(1)}, f32[128,2048]{1,0:T(8,128)}, u32[]{:S(2)}) copy-start(f32[128,2048]{1,0:T(8,128)} %copy-done.17) | copy-start | bytes 3145732
  47.4 25.1 %copy-start.21 = (bf16[256,2048]{1,0:T(8,128)(2,1)S(1)}, bf16[256,2048]{1,0:T(8,128)(2,1)}, u32[]{:S(2)}) copy-start(bf16[256,2048]{1,0:T(8,128)(2,1)} %copy-done.19) | copy-start | bytes 3145732
  47.4 25.1 %copy-start.24 = (bf16[256,2048]{1,0:T(8,128)(2,1)S(1)}, bf16[256,2048]{1,0:T(8,128)(2,1)}, u32[]{:S(2)}) copy-start(bf16[256,2048]{1,0:T(8,128)(2,1)} %copy-done.22) | copy-start | bytes 3145732

commit v2 on v1

--- a/solution.py
+++ b/solution.py
@@ -139,12 +139,9 @@
     return jnp.where(atoms == atom_row, 1.0, 0.0).astype(BF16)
 
 
-def table_kernel(
-    sheet_ref, cols_ref, atom_hbm, pos_hbm, radius_hbm, a_hbm, bh_hbm, bl_hbm,
-    atom_ref, pos_ref, radius_ref, a_ref, bh_ref, bl_ref, in_sem, out_sem,
-):
+def place_kernel(sheet_ref, cols_ref, atom_hbm, pos_hbm, radius_hbm, a_ref, place_ref, atom_ref, pos_ref, radius_ref, sem):
     loads = [
-        pltpu.make_async_copy(source, target, in_sem.at[k])
+        pltpu.make_async_copy(source, target, sem.at[k])
         for k, (source, target) in enumerate(
             ((atom_hbm, atom_ref), (pos_hbm, pos_ref), (radius_hbm, radius_ref))
         )
@@ -165,7 +162,6 @@
         for axis in range(3):
             rows = jnp.where(line == 3 * step + axis, piece[axis : axis + 1, :], rows)
     rows = rows.astype(BF16)
-    low_g = lax.broadcasted_iota(jnp.int32, (8, PCHUNK), 0).astype(F32)
     for at in range(0, NPROJ, PCHUNK):
         here = slice(at, at + PCHUNK)
         placed = mul(rows, member_of(atom_ref[:, here]), NN)
@@ -174,10 +170,19 @@
             for axis in range(3)
         )
         spread = radius_ref[:, here] / (EDGE * EDGE)
+        place_ref[0:1, here] = tz
+        place_ref[1:2, here] = spread
         cosine, sine = sincos_turns(gx * tx + gy * ty)
         amp = jnp.exp(-spread * gxy)
         a_ref[:STICKS, here] = amp * cosine
         a_ref[STICKS:, here] = -amp * sine
+
+
+def depth_factors(place_ref, bh_ref, bl_ref):
+    low_g = lax.broadcasted_iota(jnp.int32, (8, PCHUNK), 0).astype(F32)
+    for at in range(0, NPROJ, PCHUNK):
+        here = slice(at, at + PCHUNK)
+        tz, spread = place_ref[0:1, here], place_ref[1:2, here]
         low_c, low_s = sincos_turns(low_g * tz)
         for bank in range(2):
             high_g = lax.broadcasted_iota(jnp.int32, (8, PCHUNK), 0) * 8 + bank * 64
@@ -196,14 +201,6 @@
                     high, low = split(jnp.concatenate(found, axis=0))
                     bh_ref[base : base + 16, here] = high
                     bl_ref[base : base + 16, here] = low
-    stores = [
-        pltpu.make_async_copy(source, target, out_sem.at[k])
-        for k, (source, target) in enumerate(((a_ref, a_hbm), (bh_ref, bh_hbm), (bl_ref, bl_hbm)))
-    ]
-    for store in stores:
-        store.start()
-    for store in stores:
-        store.wait()
 
 
 def rows_of(re, im):
@@ -221,15 +218,10 @@
 
 
 def project_kernel(
-    sheet_ref, counts_ref, sticks_ref, th_ref, tl_ref, fold_ref, atom_ref, diag_ref, dij_ref, a_hbm, bh_hbm, bl_hbm,
-    out_ref, becp_ref, mask_ref, a_ref, bh_ref, bl_ref, sem,
+    sheet_ref, counts_ref, sticks_ref, th_ref, tl_ref, fold_ref, atom_ref, diag_ref, dij_ref, a_ref, place_ref,
+    out_ref, bh_ref, bl_ref, becp_ref, mask_ref,
 ):
-    loads = [
-        pltpu.make_async_copy(source, target, sem.at[k])
-        for k, (source, target) in enumerate(((bh_hbm, bh_ref), (bl_hbm, bl_ref), (a_hbm, a_ref)))
-    ]
-    for load in loads:
-        load.start()
+    depth_factors(place_ref, bh_ref, bl_ref)
     for at in range(0, NPROJ, PCHUNK):
         mask_ref[:, at : at + PCHUNK] = member_of(atom_ref[:, at : at + PCHUNK])
     coeff = split(live_sticks(sticks_ref, counts_ref, sheet_ref[0]))
@@ -249,8 +241,6 @@
     for plane in range(DEPTH):
         out_ref[every(plane), :] = by_depth[plane * SHEETS : (plane + 1) * SHEETS]
     out_ref[every(DEPTH), :] = jnp.zeros((SHEETS, 128), F32)
-    for load in loads:
-        load.wait()
     for at in range(0, NPROJ, PCHUNK):
         here = slice(at, at + PCHUNK)
         y = dot3(paired, (bh_ref[:, here], bl_ref[:, here]), NN)
@@ -435,13 +425,13 @@
             out_ref[team, part] = jnp.where(live, value, 0.0)
 
 
-def call(kernel, places, outs, scratch=(), flops=0, limit=20 << 20, out_place=pltpu.VMEM):
+def call(kernel, places, outs, scratch=(), flops=0, limit=20 << 20):
     kinds = {"s": pltpu.SMEM, "v": pltpu.VMEM, "h": pltpu.HBM}
     return pl.pallas_call(
         kernel,
         out_shape=outs,
         in_specs=[pl.BlockSpec(memory_space=kinds[place]) for place in places],
-        out_specs=jax.tree.map(lambda _: pl.BlockSpec(memory_space=out_place), outs),
+        out_specs=jax.tree.map(lambda _: pl.BlockSpec(memory_space=pltpu.VMEM), outs),
         scratch_shapes=list(scratch),
         compiler_params=pltpu.CompilerParams(vmem_limit_bytes=limit),
         cost_estimate=pl.CostEstimate(flops=flops, bytes_accessed=4 << 20, transcendentals=0),
@@ -452,38 +442,28 @@
     return jax.ShapeDtypeStruct(dims, dtype)
 
 
-TABLES = (((2 * STICKS, NPROJ), F32), ((256, NPROJ), BF16), ((256, NPROJ), BF16))
-
-
-def make_tables(sheet, cols, proj_atom, atom_pos, proj_radius):
+def make_places(sheet, cols, proj_atom, atom_pos, proj_radius):
     return call(
-        table_kernel, "svhhh", tuple(shape(*table) for table in TABLES),
+        place_kernel, "svhhh", (shape((2 * STICKS, NPROJ)), shape((2, NPROJ))),
         [
             pltpu.VMEM((1, NPROJ), jnp.int32),
             pltpu.VMEM((3, NATOM), F32),
             pltpu.VMEM((1, NPROJ), F32),
-            *(pltpu.VMEM(*table) for table in TABLES),
-            pltpu.SemaphoreType.DMA((3,)),
             pltpu.SemaphoreType.DMA((3,)),
         ],
         flops=2 << 30,
-        out_place=pltpu.HBM,
     )(sheet, cols, proj_atom.reshape(1, NPROJ), atom_pos, proj_radius.reshape(1, NPROJ))
 
 
-def project(sheet, counts, sticks, tables, proj_atom, proj_diag, dij):
+def project(sheet, counts, sticks, places, proj_atom, proj_diag, dij):
     return call(
-        project_kernel, "ssvvvvvvvhhh", shape((SHEETS * ROWS, 2 * STICKS)),
-        [
-            pltpu.VMEM((2, NPROJ), F32),
-            pltpu.VMEM((NATOM, NPROJ), BF16),
-            *(pltpu.VMEM(*table) for table in TABLES),
-            pltpu.SemaphoreType.DMA((3,)),
-        ],
+        project_kernel, "ssvvvvvvvvv",
+        (shape((SHEETS * ROWS, 2 * STICKS)), shape((256, NPROJ), BF16), shape((256, NPROJ), BF16)),
+        [pltpu.VMEM((2, NPROJ), F32), pltpu.VMEM((NATOM, NPROJ), BF16)],
         flops=3 << 30,
     )(
         sheet, counts, sticks, *split_table(depth_table()), fold_matrix(),
-        proj_atom.reshape(1, NPROJ), proj_diag.reshape(1, NPROJ), dij.reshape(1, NPROJ), *tables,
+        proj_atom.reshape(1, NPROJ), proj_diag.reshape(1, NPROJ), dij.reshape(1, NPROJ), *places,
     )
 
 
@@ -530,12 +510,12 @@
     layout = line_lateral_place[: TEAMS * SHEETS * LINES].reshape(TEAMS, SHEETS, LINES)
     cols = jnp.transpose(layout, (1, 0, 2)).reshape(SHEETS, STICKS)
     sticks = lax.all_to_all(orbital_coefficients, "tg", split_axis=0, concat_axis=0, tiled=True)
-    tables = make_tables(sheet, cols, proj_atom, atom_pos, proj_radius)
-    by_depth = project(sheet, stick_count, sticks, tables, proj_atom, proj_diag, ionic_pseudo_dij)
+    places = make_places(sheet, cols, proj_atom, atom_pos, proj_radius)
+    by_depth, *factors = project(sheet, stick_count, sticks, places, proj_atom, proj_diag, ionic_pseudo_dij)
     by_plane = over_sheets(by_depth)
     picked = plane_work(cols, by_plane, potential)
     back = over_sheets(picked)
-    done = finish(sheet, stick_count, cols, sticks, back, tables)
+    done = finish(sheet, stick_count, cols, sticks, back, (places[0], *factors))
     return lax.all_to_all(done, "tg", split_axis=0, concat_axis=0, tiled=True)
 
 

time: 88.4 us -> 84.8 us (0.959)
  local copies, waits for them, and re-layouts: 9.88 us -> 7.45 us
  waiting for transfers between devices: 8.93 us -> 11.1 us
  blocking collectives: 28.1 us -> 26.4 us
  Pallas kernels: 18.4 us -> 16.9 us
    unnamed x53 -> x49, local copies, waits for them, and re-layouts: 6.44 us -> 4 us
    all_to_all x1, waiting for transfers between devices: 0.01 us -> 2.15 us  [body(): lax.all_to_all(orbital_coefficients, 'tg', split_axis=0, concat_axis=0, t...]
    pallas_call x2, Pallas kernels: 6.78 us -> 5.3 us  [the longest x1 3.93 us: project(): call(project_kernel, 'ssvvvvvvvvv', (shape((SHEETS * ROWS, 2 * STICKS)),...]
    all_to_all x1, blocking collectives: 12.4 us -> 11 us  [body(): return lax.all_to_all(done, 'tg', split_axis=0, concat_axis=0, tiled=True)]
  transfers between devices with their start and end apart: 2 -> 2, of which waited for: 1 -> 2; matrix products, arithmetic and copies ran while one was open for 3% -> 3% of each run, Pallas kernels for 3% -> 2%
where the time goes in v2:
time: 84.8 us; the launch traced here: 84.3 us
  blocking collectives  26.4 us (31%)
  starting transfers between devices  22.3 us (26%)
  Pallas kernels  16.9 us (20%)
  waiting for transfers between devices  11.1 us (13%)
  local copies, waits for them, and re-layouts  7.45 us (9%)
    all_to_all x1, blocking collectives, over_sheets(): lax.all_to_all(sent, 'pw', split_axis=0, concat_axis=0, tiled=True)  15.4 us
    all_to_all x1, starting transfers between devices, over_sheets(): lax.all_to_all(sent, 'pw', split_axis=0, concat_axis=0, tiled=True)  12.1 us
    all_to_all x1, blocking collectives, body(): return lax.all_to_all(done, 'tg', split_axis=0, concat_axis=0, tiled=True)  11 us
    all_to_all x1, starting transfers between devices, body(): lax.all_to_all(orbital_coefficients, 'tg', split_axis=0, concat_axis=0, t...  10.1 us
    pallas_call x1, Pallas kernels, plane_work(): call(plane_kernel, 'v' * 11, shape((SHEETS * ROWS, 2 * STICKS)), [pltpu.V...  9.36 us
    all_to_all x1, waiting for transfers between devices, over_sheets(): lax.all_to_all(sent, 'pw', split_axis=0, concat_axis=0, tiled=True)  8.93 us
    unnamed x49, local copies, waits for them, and re-layouts  4 us
    pallas_call x1, Pallas kernels, project(): call(project_kernel, 'ssvvvvvvvvv', (shape((SHEETS * ROWS, 2 * STICKS)),...  3.93 us
  transfers between devices with their start and end apart: 2, of which 2 were waited for; matrix products, arithmetic and copies ran while one was open for 3% of the time, Pallas kernels for 2%

profile of v2, /device:TPU:1, one launch (start us, length us, event | category | flops | bytes accessed | tf_op | source)
XLA Modules:
  0.0 84.3 jit_solution(17822852127915627300)
XLA Ops:
  0.0 10.1 %all-to-all-start = ((f32[8,2,8,192]{3,2,1,0:T(8,128)}), f32[8,2,8,192]{3,2,1,0:T(8,128)S(1)}, u32[]{:S(2)}, u32[]{:S(2)}) async-start(f32[8,2,8,192]{3,2,1,0:T(8,128)} %param.23), calls=%async_computation | async-start | bytes 262144 | tf_op jit(solution)/shard_map/all_to_all | solution.py:512
  10.2 0.0 slice-start
  10.2 0.7 slice-done
  10.9 0.2 reshape.46
  11.0 0.1 copy.24
  11.1 0.0 copy-start
  11.1 0.0 copy-start.1
  11.1 0.0 copy-start.2
  11.1 0.1 copy.27.cols_ref
  11.2 0.6 copy-done
  11.9 0.0 copy-done.1
  11.9 0.0 copy-done.2
  11.9 0.0 copy-start.3
  11.9 0.0 copy-start.4
  11.9 0.0 copy-start.10
  11.9 0.0 copy-start.11
  11.9 0.0 copy-start.16
  11.9 1.4 %shard_map.217 = (f32[128,2048]{1,0:T(8,128)S(1)}, f32[2,2048]{1,0:T(2,128)S(1)}) custom-call(s32[1]{0:T(128)} %bitcast.sheet_ref, s32[64,64]{1,0:T(8,128)S(1)} %copy.27.cols_ref, s32[1,2048]{1,0:T(1,128)S(1)} %bitcast.15, f32[3,512]{1,0:T(4,128)S(1)} %copy-done, f32[1,2048]{1,0:T(1,128)S(1)} %bitcast.14), custom_call_target="tpu_custom_call" | custom-call | flops 2147483648 | bytes 4194304 | tf_op jit(solution)/shard_map/pallas_call | solution.py:446
  13.3 0.0 copy-start.17
  13.3 2.1 %all-to-all-done.sticks_ref = f32[8,2,8,192]{3,2,1,0:T(8,128)S(1)} async-done(((f32[8,2,8,192]{3,2,1,0:T(8,128)}), f32[8,2,8,192]{3,2,1,0:T(8,128)S(1)}, u32[]{:S(2)}, u32[]{:S(2)}) %all-to-all-start) | async-done | bytes 98336 | tf_op jit(solution)/shard_map/all_to_all | solution.py:512
  15.4 0.0 copy-start.5
  15.4 0.0 copy-done.3
  15.4 0.0 copy-done.4
  15.5 0.0 copy-done.10
  15.5 0.0 copy-done.11
  15.5 0.0 copy-done.16
  15.5 0.6 copy-done.5
  16.1 0.0 copy-start.23
  16.1 3.9 %shard_map.218 = (f32[256,128]{1,0:T(8,128)}, bf16[256,2048]{1,0:T(8,128)(2,1)S(1)}, bf16[256,2048]{1,0:T(8,128)(2,1)S(1)}) custom-call(s32[1]{0:T(128)} %bitcast.sheet_ref, s32[512]{0:T(512)S(1)} %copy-done.5, f32[8,2,8,192]{3,2,1,0:T(8,128)S(1)} %all-to-all-done.sticks_ref, bf16[384,192]{1,0:T(8,128)(2,1)S(1)} %copy-done.11, ...), custom_call_target="tpu_custom_call" | custom-call | flops 3221225472 | bytes 4194304 | tf_op jit(solution)/shard_map/pallas_call | solution.py:459
  20.1 0.0 copy-done.17
  20.1 0.0 copy-start.19
  20.1 1.0 %copy-done.19 = bf16[256,2048]{1,0:T(8,128)(2,1)} copy-done((bf16[256,2048]{1,0:T(8,128)(2,1)}, bf16[256,2048]{1,0:T(8,128)(2,1)S(1)}, u32[]{:S(2)}) %copy-start.19) | copy-done | bytes 1048600
  21.0 0.0 copy-start.21
  21.0 1.0 %copy-done.21 = bf16[256,2048]{1,0:T(8,128)(2,1)} copy-done((bf16[256,2048]{1,0:T(8,128)(2,1)}, bf16[256,2048]{1,0:T(8,128)(2,1)S(1)}, u32[]{:S(2)}) %copy-start.21) | copy-done | bytes 1048600
  22.0 12.1 %all-to-all-start.1 = ((f32[64,4,128]{2,1,0:T(4,128)}), f32[64,4,128]{2,1,0:T(4,128)S(1)}, u32[]{:S(2)}, u32[]{:S(2)}) async-start(f32[64,4,128]{2,1,0:T(4,128)} %bitcast.7), calls=%async_computation.1 | async-start | bytes 262144 | tf_op jit(solution)/shard_map/all_to_all | solution.py:495
  34.2 0.0 copy-done.23
  34.2 0.0 copy-start.12
  34.2 0.0 copy-start.13
  34.2 0.0 copy-start.14
  34.2 0.0 copy-start.15
  34.2 1.2 %reshape.54 = f32[3,192,192]{2,1,0:T(8,128)} reshape(f32[3,36864]{1,0:T(4,128)S(1)} %copy-done.23) | data formatting | bytes 884736 | tf_op jit(solution)/shard_map/reshape | solution.py:472
  35.4 0.0 copy-start.6
  35.4 0.0 copy-start.7
  35.4 1.2 %pad.4.potential_ref = f32[3,192,256]{2,1,0:T(8,128)S(1)} pad(f32[3,192,192]{2,1,0:T(8,128)} %reshape.54, f32[]{:T(128)} %constant.28.clone.1), padding=0_0x0_0x0_64 | pad | bytes 1032196 | tf_op jit(solution)/shard_map/jit(_pad)/pad | solution.py:472
  36.6 8.9 %all-to-all-done.1 = f32[64,4,128]{2,1,0:T(4,128)S(1)} async-done(((f32[64,4,128]{2,1,0:T(4,128)}), f32[64,4,128]{2,1,0:T(4,128)S(1)}, u32[]{:S(2)}, u32[]{:S(2)}) %all-to-all-start.1) | async-done | bytes 131104 | tf_op jit(solution)/shard_map/all_to_all | solution.py:495
  45.5 0.0 copy-done.12
  45.5 0.0 copy-done.13
  45.5 0.0 copy-done.14
  45.6 0.0 copy-done.15
  45.6 0.0 copy-done.6
  45.6 0.0 copy-done.7
  45.6 0.0 copy-done.8
  45.6 0.0 copy-done.9
  45.6 0.0 copy-start.18
  45.6 0.0 copy-start.20
  45.6 0.0 copy-start.22
  45.6 9.4 %shard_map.219 = f32[256,128]{1,0:T(8,128)S(1)} custom-call(s32[64,64]{1,0:T(8,128)S(1)} %copy.27.cols_ref, f32[256,128]{1,0:T(8,128)S(1)} %bitcast.11, f32[3,192,256]{2,1,0:T(8,128)S(1)} %pad.4.potential_ref, bf16[256,512]{1,0:T(8,128)(2,1)S(1)} %copy-done.9, bf16[256,512]{1,0:T(8,128)(2,1)S(1)} %copy-done.8, bf16[384,256]{1,0:T(8,128)(2,1)S(1)} %copy-done.15, ...), custom_call_target="tpu_custom_call" | custom-call | flops 8589934592 | bytes 4194304 | tf_op jit(solution)/shard_map/pallas_call | solution.py:473
  55.0 15.4 %all_to_all.20 = f32[64,4,128]{2,1,0:T(4,128)S(1)} all-to-all(f32[64,4,128]{2,1,0:T(4,128)S(1)} %bitcast.13), channel_id=1, replica_groups=mesh['tg'=8,'pw'=64] {'pw'}, dimensions={0} | all-to-all | bytes 262144 | tf_op jit(solution)/shard_map/all_to_all | solution.py:495
  70.4 0.0 copy-done.18
  70.4 0.0 copy-done.20
  70.4 0.0 copy-done.22
  70.4 2.2 %shard_map.220 = f32[8,2,8,192]{3,2,1,0:T(8,128)S(1)} custom-call(s32[1]{0:T(128)} %bitcast.sheet_ref, s32[512]{0:T(512)S(1)} %copy-done.5, s32[64,64]{1,0:T(8,128)S(1)} %copy.27.cols_ref, f32[8,2,8,192]{3,2,1,0:T(8,128)S(1)} %all-to-all-done.sticks_ref, f32[256,128]{1,0:T(8,128)S(1)} %bitcast.12, f32[128,2048]{1,0:T(8,128)S(1)} %copy-done.18, ...), custom_call_target="tpu_custom_call" | custom-call | flops 3221225472 | bytes 4194304 | tf_op jit(solution)/shard_map/pallas_call | solution.py:488
  72.7 11.0 %all_to_all.21 = f32[8,2,8,192]{3,2,1,0:T(8,128)S(1)} all-to-all(f32[8,2,8,192]{3,2,1,0:T(8,128)S(1)} %shard_map.220), channel_id=1, replica_groups=mesh['tg'=8,'pw'=64] {'tg'}, dimensions={0} | all-to-all | bytes 196608 | tf_op jit(solution)/shard_map/all_to_all | solution.py:519
  83.6 0.7 copy.29
  (2 shorter events, 0.0 us)
Async XLA Ops:
  0.0 15.4 %all-to-all-start = ((f32[8,2,8,192]{3,2,1,0:T(8,128)}), f32[8,2,8,192]{3,2,1,0:T(8,128)S(1)}, u32[]{:S(2)}, u32[]{:S(2)}) async-start(f32[8,2,8,192]{3,2,1,0:T(8,128)} %param.23), calls=%async_computation | async-start | bytes 262144 | tf_op jit(solution)/shard_map/all_to_all | solution.py:512
  10.2 0.7 slice-start
  11.1 0.7 copy-start
  11.1 0.7 copy-start.1
  11.1 0.7 copy-start.2
  11.9 3.6 %copy-start.3 = (f32[2048]{0:T(1024)S(1)}, f32[2048]{0:T(1024)}, u32[]{:S(2)}) copy-start(f32[2048]{0:T(1024)} %param.30) | copy-start | bytes 24580
  11.9 3.6 %copy-start.4 = (f32[2048]{0:T(1024)S(1)}, f32[2048]{0:T(1024)}, u32[]{:S(2)}) copy-start(f32[2048]{0:T(1024)} %param.31) | copy-start | bytes 24580
  11.9 3.6 %copy-start.10 = (bf16[384,192]{1,0:T(8,128)(2,1)S(1)}, bf16[384,192]{1,0:T(8,128)(2,1)}, u32[]{:S(2)}) copy-start(bf16[384,192]{1,0:T(8,128)(2,1)} %constant.30.clone.tl_ref) | copy-start | bytes 442372
  11.9 3.6 %copy-start.11 = (bf16[384,192]{1,0:T(8,128)(2,1)S(1)}, bf16[384,192]{1,0:T(8,128)(2,1)}, u32[]{:S(2)}) copy-start(bf16[384,192]{1,0:T(8,128)(2,1)} %constant.29.clone.th_ref) | copy-start | bytes 442372
  11.9 3.6 %copy-start.16 = (bf16[192,256]{1,0:T(8,128)(2,1)S(1)}, bf16[192,256]{1,0:T(8,128)(2,1)}, u32[]{:S(2)}) copy-start(bf16[192,256]{1,0:T(8,128)(2,1)} %constant.31.clone.fold_ref) | copy-start | bytes 294916
  13.3 6.8 %copy-start.17 = (f32[128,2048]{1,0:T(8,128)}, f32[128,2048]{1,0:T(8,128)S(1)}, u32[]{:S(2)}) copy-start(f32[128,2048]{1,0:T(8,128)S(1)} %get-tuple-element.10.a_ref) | copy-start | bytes 3145732
  15.4 0.7 copy-start.5
  16.1 18.0 %copy-start.23 = (f32[3,36864]{1,0:T(4,128)S(1)}, f32[3,36864]{1,0:T(4,128)}, u32[]{:S(2)}) copy-start(f32[3,36864]{1,0:T(4,128)} %param.24) | copy-start | bytes 1327108
  20.1 1.0 %copy-start.19 = (bf16[256,2048]{1,0:T(8,128)(2,1)}, bf16[256,2048]{1,0:T(8,128)(2,1)S(1)}, u32[]{:S(2)}) copy-start(bf16[256,2048]{1,0:T(8,128)(2,1)S(1)} %get-tuple-element.13.bh_ref) | copy-start | bytes 3145732
  21.0 1.0 %copy-start.21 = (bf16[256,2048]{1,0:T(8,128)(2,1)}, bf16[256,2048]{1,0:T(8,128)(2,1)S(1)}, u32[]{:S(2)}) copy-start(bf16[256,2048]{1,0:T(8,128)(2,1)S(1)} %get-tuple-element.14.bl_ref) | copy-start | bytes 3145732
  22.0 23.5 %all-to-all-start.1 = ((f32[64,4,128]{2,1,0:T(4,128)}), f32[64,4,128]{2,1,0:T(4,128)S(1)}, u32[]{:S(2)}, u32[]{:S(2)}) async-start(f32[64,4,128]{2,1,0:T(4,128)} %bitcast.7), calls=%async_computation.1 | async-start | bytes 262144 | tf_op jit(solution)/shard_map/all_to_all | solution.py:495
  34.2 11.4 %copy-start.12 = (bf16[256,384]{1,0:T(8,128)(2,1)S(1)}, bf16[256,384]{1,0:T(8,128)(2,1)}, u32[]{:S(2)}) copy-start(bf16[256,384]{1,0:T(8,128)(2,1)} %constant.37.clone.xfl_ref) | copy-start | bytes 589828
  34.2 11.4 %copy-start.13 = (bf16[256,384]{1,0:T(8,128)(2,1)S(1)}, bf16[256,384]{1,0:T(8,128)(2,1)}, u32[]{:S(2)}) copy-start(bf16[256,384]{1,0:T(8,128)(2,1)} %constant.36.clone.xfh_ref) | copy-start | bytes 589828
  34.2 11.4 %copy-start.14 = (bf16[384,256]{1,0:T(8,128)(2,1)S(1)}, bf16[384,256]{1,0:T(8,128)(2,1)}, u32[]{:S(2)}) copy-start(bf16[384,256]{1,0:T(8,128)(2,1)} %constant.35.clone.xil_ref) | copy-start | bytes 589828
  34.2 11.4 %copy-start.15 = (bf16[384,256]{1,0:T(8,128)(2,1)S(1)}, bf16[384,256]{1,0:T(8,128)(2,1)}, u32[]{:S(2)}) copy-start(bf16[384,256]{1,0:T(8,128)(2,1)} %constant.34.clone.xih_ref) | copy-start | bytes 589828
  35.4 10.2 %copy-start.6 = (bf16[512,256]{1,0:T(8,128)(2,1)S(1)}, bf16[512,256]{1,0:T(8,128)(2,1)}, u32[]{:S(2)}) copy-start(bf16[512,256]{1,0:T(8,128)(2,1)} %constant.39.clone.yfl_ref) | copy-start | bytes 786436
  35.4 10.2 %copy-start.7 = (bf16[512,256]{1,0:T(8,128)(2,1)S(1)}, bf16[512,256]{1,0:T(8,128)(2,1)}, u32[]{:S(2)}) copy-start(bf16[512,256]{1,0:T(8,128)(2,1)} %constant.38.clone.yfh_ref) | copy-start | bytes 786436
  35.4 10.2 %copy-start.8 = (bf16[256,512]{1,0:T(8,128)(2,1)S(1)}, bf16[256,512]{1,0:T(8,128)(2,1)}, u32[]{:S(2)}) copy-start(bf16[256,512]{1,0:T(8,128)(2,1)} %constant.33.clone.yil_ref) | copy-start | bytes 786436
  35.4 10.2 %copy-start.9 = (bf16[256,512]{1,0:T(8,128)(2,1)S(1)}, bf16[256,512]{1,0:T(8,128)(2,1)}, u32[]{:S(2)}) copy-start(bf16[256,512]{1,0:T(8,128)(2,1)} %constant.32.clone.yih_ref) | copy-start | bytes 786436
  45.6 24.8 %copy-start.18 = (f32[128,2048]{1,0:T(8,128)S(1)}, f32[128,2048]{1,0:T(8,128)}, u32[]{:S(2)}) copy-start(f32[128,2048]{1,0:T(8,128)} %copy-done.17) | copy-start | bytes 3145732
  45.6 24.8 %copy-start.20 = (bf16[256,2048]{1,0:T(8,128)(2,1)S(1)}, bf16[256,2048]{1,0:T(8,128)(2,1)}, u32[]{:S(2)}) copy-start(bf16[256,2048]{1,0:T(8,128)(2,1)} %copy-done.19) | copy-start | bytes 3145732
  45.6 24.8 %copy-start.22 = (bf16[256,2048]{1,0:T(8,128)(2,1)S(1)}, bf16[256,2048]{1,0:T(8,128)(2,1)}, u32[]{:S(2)}) copy-start(bf16[256,2048]{1,0:T(8,128)(2,1)} %copy-done.21) | copy-start | bytes 3145732

commit v3 on v2

--- a/solution.py
+++ b/solution.py
@@ -19,7 +19,7 @@
 NATOM = 512
 CUT = 48
 HALF_ROWS = 64
-CHUNK = 512
+CHUNK = 1024
 CHUNKS = SHEETS * STICKS // CHUNK
 PCHUNK = 256
 BLOCKS = NPROJ // 128
@@ -288,7 +288,14 @@
     summed = jnp.sum(sticks_ref[every(DEPTH), :], axis=0, keepdims=True)
     out_ref[every(DEPTH), :] = jnp.broadcast_to(summed, (SHEETS, 128))
     rows64 = lax.broadcasted_iota(jnp.int32, (HALF_ROWS, 128), 0)
-    rows256 = lax.broadcasted_iota(jnp.int32, (256, 128), 0)
+    half_rows = rows64.astype(F32).astype(BF16)
+    full_rows = lax.broadcasted_iota(jnp.int32, (256, 128), 0).astype(F32).astype(BF16)
+    one, zero = jnp.ones((), BF16), jnp.zeros((), BF16)
+
+    def tall(row, height):
+        packed = jnp.broadcast_to(row, (16, 128)).astype(BF16)
+        return jnp.concatenate([packed] * (height // 16), axis=0)
+
     per = CHUNK // 128
     total = jnp.zeros((12 * HALF_ROWS, 256), F32)
     for chunk in range(CHUNKS):
@@ -296,11 +303,11 @@
         for inner in range(per):
             r = chunk * per + inner
             lanes = slice(inner * 128, (inner + 1) * 128)
-            member = jnp.where(rows64 == x_ref[0, r : r + 1, :], 1.0, 0.0).astype(BF16)
-            hot_ref[chunk, :, lanes] = jnp.where(rows256 == x_ref[1, r : r + 1, :], 1.0, 0.0).astype(BF16)
+            spot = x_ref[:, r : r + 1, :].astype(F32)
+            member = jnp.where(half_rows == tall(spot[0], HALF_ROWS), one, zero)
+            hot_ref[chunk, :, lanes] = jnp.where(full_rows == tall(spot[1], 256), one, zero)
             for k in range(12):
-                value = jnp.broadcast_to(v_ref[k, r : r + 1, :], (16, 128)).astype(BF16)
-                value = jnp.concatenate([value] * (HALF_ROWS // 16), axis=0)
+                value = tall(v_ref[k, r : r + 1, :], HALF_ROWS)
                 left_ref[slot, k * HALF_ROWS : (k + 1) * HALF_ROWS, lanes] = member * value
         total = total + mul(left_ref[slot], hot_ref[chunk], NT)
     grids = []
@@ -367,10 +374,11 @@
 
 
 def finish_kernel(
-    sheet_ref, counts_ref, cols_ref, sticks_ref, back_ref, a_ref, bh_ref, bl_ref, th_ref, tl_ref, fold_ref,
-    out_ref,
+    sheet_ref, counts_ref, cols_ref, sticks_ref, back_ref, a_ref, place_ref, th_ref, tl_ref, fold_ref,
+    out_ref, bh_ref, bl_ref,
 ):
     sheet = sheet_ref[0]
+    depth_factors(place_ref, bh_ref, bl_ref)
     vnl = jnp.zeros((2 * STICKS, 256), F32)
     step = 2 * PCHUNK
     for at in range(0, NPROJ, step):
@@ -455,11 +463,13 @@
     )(sheet, cols, proj_atom.reshape(1, NPROJ), atom_pos, proj_radius.reshape(1, NPROJ))
 
 
+FACTORS = [pltpu.VMEM((256, NPROJ), BF16)] * 2
+
+
 def project(sheet, counts, sticks, places, proj_atom, proj_diag, dij):
     return call(
-        project_kernel, "ssvvvvvvvvv",
-        (shape((SHEETS * ROWS, 2 * STICKS)), shape((256, NPROJ), BF16), shape((256, NPROJ), BF16)),
-        [pltpu.VMEM((2, NPROJ), F32), pltpu.VMEM((NATOM, NPROJ), BF16)],
+        project_kernel, "ssvvvvvvvvv", shape((SHEETS * ROWS, 2 * STICKS)),
+        [*FACTORS, pltpu.VMEM((2, NPROJ), F32), pltpu.VMEM((NATOM, NPROJ), BF16)],
         flops=3 << 30,
     )(
         sheet, counts, sticks, *split_table(depth_table()), fold_matrix(),
@@ -484,9 +494,9 @@
     )(cols, sticks, padded, *tables)
 
 
-def finish(sheet, counts, cols, sticks, back, tables):
-    return call(finish_kernel, "ssvvvvvvvvv", shape((TEAMS, 2, LINES, EDGE)), flops=3 << 30)(
-        sheet, counts, cols, sticks, back, *tables, *split_table(depth_table()), fold_matrix()
+def finish(sheet, counts, cols, sticks, back, places):
+    return call(finish_kernel, "ssvvvvvvvv", shape((TEAMS, 2, LINES, EDGE)), FACTORS, flops=3 << 30)(
+        sheet, counts, cols, sticks, back, *places, *split_table(depth_table()), fold_matrix()
     )
 
 
@@ -511,11 +521,11 @@
     cols = jnp.transpose(layout, (1, 0, 2)).reshape(SHEETS, STICKS)
     sticks = lax.all_to_all(orbital_coefficients, "tg", split_axis=0, concat_axis=0, tiled=True)
     places = make_places(sheet, cols, proj_atom, atom_pos, proj_radius)
-    by_depth, *factors = project(sheet, stick_count, sticks, places, proj_atom, proj_diag, ionic_pseudo_dij)
+    by_depth = project(sheet, stick_count, sticks, places, proj_atom, proj_diag, ionic_pseudo_dij)
     by_plane = over_sheets(by_depth)
     picked = plane_work(cols, by_plane, potential)
     back = over_sheets(picked)
-    done = finish(sheet, stick_count, cols, sticks, back, (places[0], *factors))
+    done = finish(sheet, stick_count, cols, sticks, back, places)
     return lax.all_to_all(done, "tg", split_axis=0, concat_axis=0, tiled=True)
 
 

time: 84.8 us -> 83 us (0.979)
  local copies, waits for them, and re-layouts: 7.45 us -> 5.52 us
    unnamed x49 -> x41, local copies, waits for them, and re-layouts: 4 us -> 2.04 us
where the time goes in v3:
time: 83 us; the launch traced here: 82.4 us
  blocking collectives  26.5 us (32%)
  starting transfers between devices  22.1 us (27%)
  Pallas kernels  16.9 us (20%)
  waiting for transfers between devices  11.2 us (13%)
  local copies, waits for them, and re-layouts  5.52 us (7%)
    all_to_all x1, blocking collectives, over_sheets(): lax.all_to_all(sent, 'pw', split_axis=0, concat_axis=0, tiled=True)  15.7 us
    all_to_all x1, starting transfers between devices, over_sheets(): lax.all_to_all(sent, 'pw', split_axis=0, concat_axis=0, tiled=True)  11.9 us
    all_to_all x1, blocking collectives, body(): return lax.all_to_all(done, 'tg', split_axis=0, concat_axis=0, tiled=True)  10.8 us
    all_to_all x1, starting transfers between devices, body(): lax.all_to_all(orbital_coefficients, 'tg', split_axis=0, concat_axis=0, t...  10.1 us
    all_to_all x1, waiting for transfers between devices, over_sheets(): lax.all_to_all(sent, 'pw', split_axis=0, concat_axis=0, tiled=True)  9.08 us
    pallas_call x1, Pallas kernels, plane_work(): call(plane_kernel, 'v' * 11, shape((SHEETS * ROWS, 2 * STICKS)), [pltpu.V...  9.03 us
    pallas_call x1, Pallas kernels, project(): call(project_kernel, 'ssvvvvvvvvv', shape((SHEETS * ROWS, 2 * STICKS)), [...  3.76 us
    pallas_call x1, Pallas kernels, finish(): call(finish_kernel, 'ssvvvvvvvv', shape((TEAMS, 2, LINES, EDGE)), FACTORS...  2.73 us
  transfers between devices with their start and end apart: 2, of which 2 were waited for; matrix products, arithmetic and copies ran while one was open for 3% of the time, Pallas kernels for 2%

profile of v3, /device:TPU:1, one launch (start us, length us, event | category | flops | bytes accessed | tf_op | source)
XLA Modules:
  0.0 82.4 jit_solution(16854496145196253988)
XLA Ops:
  0.0 10.1 %all-to-all-start = ((f32[8,2,8,192]{3,2,1,0:T(8,128)}), f32[8,2,8,192]{3,2,1,0:T(8,128)S(1)}, u32[]{:S(2)}, u32[]{:S(2)}) async-start(f32[8,2,8,192]{3,2,1,0:T(8,128)} %param.23), calls=%async_computation | async-start | bytes 262144 | tf_op jit(solution)/shard_map/all_to_all | solution.py:522
  10.2 0.0 slice-start
  10.2 0.7 slice-done
  10.9 0.2 reshape.46
  11.0 0.1 copy.24
  11.1 0.0 copy-start
  11.1 0.0 copy-start.1
  11.1 0.0 copy-start.2
  11.1 0.1 copy.27.cols_ref
  11.2 0.6 copy-done
  11.9 0.0 copy-done.1
  11.9 0.0 copy-done.2
  11.9 0.0 copy-start.3
  11.9 0.0 copy-start.4
  11.9 0.0 copy-start.10
  11.9 0.0 copy-start.11
  11.9 0.0 copy-start.16
  11.9 1.4 %shard_map.217 = (f32[128,2048]{1,0:T(8,128)S(1)}, f32[2,2048]{1,0:T(2,128)S(1)}) custom-call(s32[1]{0:T(128)} %bitcast.sheet_ref, s32[64,64]{1,0:T(8,128)S(1)} %copy.27.cols_ref, s32[1,2048]{1,0:T(1,128)S(1)} %bitcast.15, f32[3,512]{1,0:T(4,128)S(1)} %copy-done, f32[1,2048]{1,0:T(1,128)S(1)} %bitcast.14), custom_call_target="tpu_custom_call" | custom-call | flops 2147483648 | bytes 4194304 | tf_op jit(solution)/shard_map/pallas_call | solution.py:454
  13.3 0.0 copy-start.17
  13.3 2.1 %all-to-all-done.sticks_ref = f32[8,2,8,192]{3,2,1,0:T(8,128)S(1)} async-done(((f32[8,2,8,192]{3,2,1,0:T(8,128)}), f32[8,2,8,192]{3,2,1,0:T(8,128)S(1)}, u32[]{:S(2)}, u32[]{:S(2)}) %all-to-all-start) | async-done | bytes 98336 | tf_op jit(solution)/shard_map/all_to_all | solution.py:522
  15.4 0.0 copy-start.5
  15.4 0.0 copy-done.3
  15.4 0.0 copy-done.4
  15.5 0.0 copy-done.10
  15.5 0.0 copy-done.11
  15.5 0.0 copy-done.16
  15.5 0.6 copy-done.5
  16.1 0.0 copy-start.19
  16.1 3.8 %shard_map.218 = f32[256,128]{1,0:T(8,128)} custom-call(s32[1]{0:T(128)} %bitcast.sheet_ref, s32[512]{0:T(512)S(1)} %copy-done.5, f32[8,2,8,192]{3,2,1,0:T(8,128)S(1)} %all-to-all-done.sticks_ref, bf16[384,192]{1,0:T(8,128)(2,1)S(1)} %copy-done.11, bf16[384,192]{1,0:T(8,128)(2,1)S(1)} %copy-done.10, bf16[192,256]{1,0:T(8,128)(2,1)S(1)} %copy-done.16, ...), custom_call_target="tpu_custom_call" | custom-call | flops 3221225472 | bytes 4194304 | tf_op jit(solution)/shard_map/pallas_call | solution.py:470
  19.9 0.0 copy-done.17
  19.9 11.9 %all-to-all-start.1 = ((f32[64,4,128]{2,1,0:T(4,128)}), f32[64,4,128]{2,1,0:T(4,128)S(1)}, u32[]{:S(2)}, u32[]{:S(2)}) async-start(f32[64,4,128]{2,1,0:T(4,128)} %bitcast.7), calls=%async_computation.1 | async-start | bytes 262144 | tf_op jit(solution)/shard_map/all_to_all | solution.py:505
  31.8 0.0 copy-done.19
  31.8 0.0 copy-start.12
  31.9 0.0 copy-start.13
  31.9 0.0 copy-start.14
  31.9 0.0 copy-start.15
  31.9 1.2 %reshape.54 = f32[3,192,192]{2,1,0:T(8,128)} reshape(f32[3,36864]{1,0:T(4,128)S(1)} %copy-done.19) | data formatting | bytes 884736 | tf_op jit(solution)/shard_map/reshape | solution.py:482
  33.1 0.0 copy-start.6
  33.1 0.0 copy-start.7
  33.1 0.0 copy-start.8
  33.1 0.0 copy-start.9
  33.1 1.2 %pad.4.potential_ref = f32[3,192,256]{2,1,0:T(8,128)S(1)} pad(f32[3,192,192]{2,1,0:T(8,128)} %reshape.54, f32[]{:T(128)} %constant.28.clone.1), padding=0_0x0_0x0_64 | pad | bytes 1032196 | tf_op jit(solution)/shard_map/jit(_pad)/pad | solution.py:482
  34.3 9.1 %all-to-all-done.1 = f32[64,4,128]{2,1,0:T(4,128)S(1)} async-done(((f32[64,4,128]{2,1,0:T(4,128)}), f32[64,4,128]{2,1,0:T(4,128)S(1)}, u32[]{:S(2)}, u32[]{:S(2)}) %all-to-all-start.1) | async-done | bytes 131104 | tf_op jit(solution)/shard_map/all_to_all | solution.py:505
  43.4 0.0 copy-done.12
  43.4 0.0 copy-done.13
  43.4 0.0 copy-done.14
  43.4 0.0 copy-done.15
  43.4 0.0 copy-done.6
  43.4 0.0 copy-done.7
  43.5 0.0 copy-done.8
  43.5 0.0 copy-done.9
  43.5 0.0 copy-start.18
  43.5 9.0 %shard_map.219 = f32[256,128]{1,0:T(8,128)S(1)} custom-call(s32[64,64]{1,0:T(8,128)S(1)} %copy.27.cols_ref, f32[256,128]{1,0:T(8,128)S(1)} %bitcast.11, f32[3,192,256]{2,1,0:T(8,128)S(1)} %pad.4.potential_ref, bf16[256,512]{1,0:T(8,128)(2,1)S(1)} %copy-done.9, bf16[256,512]{1,0:T(8,128)(2,1)S(1)} %copy-done.8, bf16[384,256]{1,0:T(8,128)(2,1)S(1)} %copy-done.15, ...), custom_call_target="tpu_custom_call" | custom-call | flops 8589934592 | bytes 4194304 | tf_op jit(solution)/shard_map/pallas_call | solution.py:483
  52.5 15.7 %all_to_all.20 = f32[64,4,128]{2,1,0:T(4,128)S(1)} all-to-all(f32[64,4,128]{2,1,0:T(4,128)S(1)} %bitcast.12), channel_id=1, replica_groups=mesh['tg'=8,'pw'=64] {'pw'}, dimensions={0} | all-to-all | bytes 262144 | tf_op jit(solution)/shard_map/all_to_all | solution.py:505
  68.2 0.0 copy-done.18
  68.2 2.7 %shard_map.220 = f32[8,2,8,192]{3,2,1,0:T(8,128)S(1)} custom-call(s32[1]{0:T(128)} %bitcast.sheet_ref, s32[512]{0:T(512)S(1)} %copy-done.5, s32[64,64]{1,0:T(8,128)S(1)} %copy.27.cols_ref, f32[8,2,8,192]{3,2,1,0:T(8,128)S(1)} %all-to-all-done.sticks_ref, f32[256,128]{1,0:T(8,128)S(1)} %bitcast.13, f32[128,2048]{1,0:T(8,128)S(1)} %copy-done.18, ...), custom_call_target="tpu_custom_call" | custom-call | flops 3221225472 | bytes 4194304 | tf_op jit(solution)/shard_map/pallas_call | solution.py:498
  70.9 10.8 %all_to_all.21 = f32[8,2,8,192]{3,2,1,0:T(8,128)S(1)} all-to-all(f32[8,2,8,192]{3,2,1,0:T(8,128)S(1)} %shard_map.220), channel_id=1, replica_groups=mesh['tg'=8,'pw'=64] {'tg'}, dimensions={0} | all-to-all | bytes 196608 | tf_op jit(solution)/shard_map/all_to_all | solution.py:529
  81.8 0.7 copy.29
Async XLA Ops:
  0.0 15.4 %all-to-all-start = ((f32[8,2,8,192]{3,2,1,0:T(8,128)}), f32[8,2,8,192]{3,2,1,0:T(8,128)S(1)}, u32[]{:S(2)}, u32[]{:S(2)}) async-start(f32[8,2,8,192]{3,2,1,0:T(8,128)} %param.23), calls=%async_computation | async-start | bytes 262144 | tf_op jit(solution)/shard_map/all_to_all | solution.py:522
  10.2 0.7 slice-start
  11.1 0.7 copy-start
  11.1 0.7 copy-start.1
  11.1 0.7 copy-start.2
  11.9 3.6 %copy-start.3 = (f32[2048]{0:T(1024)S(1)}, f32[2048]{0:T(1024)}, u32[]{:S(2)}) copy-start(f32[2048]{0:T(1024)} %param.30) | copy-start | bytes 24580
  11.9 3.6 %copy-start.4 = (f32[2048]{0:T(1024)S(1)}, f32[2048]{0:T(1024)}, u32[]{:S(2)}) copy-start(f32[2048]{0:T(1024)} %param.31) | copy-start | bytes 24580
  11.9 3.6 %copy-start.10 = (bf16[384,192]{1,0:T(8,128)(2,1)S(1)}, bf16[384,192]{1,0:T(8,128)(2,1)}, u32[]{:S(2)}) copy-start(bf16[384,192]{1,0:T(8,128)(2,1)} %constant.30.clone.tl_ref) | copy-start | bytes 442372
  11.9 3.6 %copy-start.11 = (bf16[384,192]{1,0:T(8,128)(2,1)S(1)}, bf16[384,192]{1,0:T(8,128)(2,1)}, u32[]{:S(2)}) copy-start(bf16[384,192]{1,0:T(8,128)(2,1)} %constant.29.clone.th_ref) | copy-start | bytes 442372
  11.9 3.6 %copy-start.16 = (bf16[192,256]{1,0:T(8,128)(2,1)S(1)}, bf16[192,256]{1,0:T(8,128)(2,1)}, u32[]{:S(2)}) copy-start(bf16[192,256]{1,0:T(8,128)(2,1)} %constant.31.clone.fold_ref) | copy-start | bytes 294916
  13.3 6.6 %copy-start.17 = (f32[128,2048]{1,0:T(8,128)}, f32[128,2048]{1,0:T(8,128)S(1)}, u32[]{:S(2)}) copy-start(f32[128,2048]{1,0:T(8,128)S(1)} %get-tuple-element.7.a_ref) | copy-start | bytes 3145732
  15.4 0.7 copy-start.5
  16.1 15.7 %copy-start.19 = (f32[3,36864]{1,0:T(4,128)S(1)}, f32[3,36864]{1,0:T(4,128)}, u32[]{:S(2)}) copy-start(f32[3,36864]{1,0:T(4,128)} %param.24) | copy-start | bytes 1327108
  19.9 23.5 %all-to-all-start.1 = ((f32[64,4,128]{2,1,0:T(4,128)}), f32[64,4,128]{2,1,0:T(4,128)S(1)}, u32[]{:S(2)}, u32[]{:S(2)}) async-start(f32[64,4,128]{2,1,0:T(4,128)} %bitcast.7), calls=%async_computation.1 | async-start | bytes 262144 | tf_op jit(solution)/shard_map/all_to_all | solution.py:505
  31.8 11.6 %copy-start.12 = (bf16[256,384]{1,0:T(8,128)(2,1)S(1)}, bf16[256,384]{1,0:T(8,128)(2,1)}, u32[]{:S(2)}) copy-start(bf16[256,384]{1,0:T(8,128)(2,1)} %constant.37.clone.xfl_ref) | copy-start | bytes 589828
  31.9 11.6 %copy-start.13 = (bf16[256,384]{1,0:T(8,128)(2,1)S(1)}, bf16[256,384]{1,0:T(8,128)(2,1)}, u32[]{:S(2)}) copy-start(bf16[256,384]{1,0:T(8,128)(2,1)} %constant.36.clone.xfh_ref) | copy-start | bytes 589828
  31.9 11.6 %copy-start.14 = (bf16[384,256]{1,0:T(8,128)(2,1)S(1)}, bf16[384,256]{1,0:T(8,128)(2,1)}, u32[]{:S(2)}) copy-start(bf16[384,256]{1,0:T(8,128)(2,1)} %constant.35.clone.xil_ref) | copy-start | bytes 589828
  31.9 11.5 %copy-start.15 = (bf16[384,256]{1,0:T(8,128)(2,1)S(1)}, bf16[384,256]{1,0:T(8,128)(2,1)}, u32[]{:S(2)}) copy-start(bf16[384,256]{1,0:T(8,128)(2,1)} %constant.34.clone.xih_ref) | copy-start | bytes 589828
  33.1 10.3 %copy-start.6 = (bf16[512,256]{1,0:T(8,128)(2,1)S(1)}, bf16[512,256]{1,0:T(8,128)(2,1)}, u32[]{:S(2)}) copy-start(bf16[512,256]{1,0:T(8,128)(2,1)} %constant.39.clone.yfl_ref) | copy-start | bytes 786436
  33.1 10.3 %copy-start.7 = (bf16[512,256]{1,0:T(8,128)(2,1)S(1)}, bf16[512,256]{1,0:T(8,128)(2,1)}, u32[]{:S(2)}) copy-start(bf16[512,256]{1,0:T(8,128)(2,1)} %constant.38.clone.yfh_ref) | copy-start | bytes 786436
  33.1 10.3 %copy-start.8 = (bf16[256,512]{1,0:T(8,128)(2,1)S(1)}, bf16[256,512]{1,0:T(8,128)(2,1)}, u32[]{:S(2)}) copy-start(bf16[256,512]{1,0:T(8,128)(2,1)} %constant.33.clone.yil_ref) | copy-start | bytes 786436
  33.1 10.3 %copy-start.9 = (bf16[256,512]{1,0:T(8,128)(2,1)S(1)}, bf16[256,512]{1,0:T(8,128)(2,1)}, u32[]{:S(2)}) copy-start(bf16[256,512]{1,0:T(8,128)(2,1)} %constant.32.clone.yih_ref) | copy-start | bytes 786436
  43.5 24.7 %copy-start.18 = (f32[128,2048]{1,0:T(8,128)S(1)}, f32[128,2048]{1,0:T(8,128)}, u32[]{:S(2)}) copy-start(f32[128,2048]{1,0:T(8,128)} %copy-done.17) | copy-start | bytes 3145732

commit v4 on v3

--- a/solution.py
+++ b/solution.py
@@ -18,7 +18,7 @@
 NPROJ = 2048
 NATOM = 512
 CUT = 48
-HALF_ROWS = 64
+HALF_ROWS = 48
 CHUNK = 1024
 CHUNKS = SHEETS * STICKS // CHUNK
 PCHUNK = 256
@@ -60,12 +60,12 @@
 
 
 def lateral_tables():
-    spot = np.arange(2 * HALF_ROWS)
+    spot = np.arange(128)
     y_cos, y_sin = column_phase(spot - CUT, spot <= 2 * CUT)
     pad = ((0, 0), (0, 256 - EDGE))
     y_cos, y_sin = np.pad(y_cos, pad), np.pad(y_sin, pad)
     y_inverse = np.block([[y_cos, y_sin], [-y_sin, y_cos]])
-    x_spot = 2 * (spot % HALF_ROWS) + spot // HALF_ROWS
+    x_spot = np.where(spot < 2 * HALF_ROWS, 2 * (spot % HALF_ROWS) + spot // HALF_ROWS, spot)
     x_cos, x_sin = column_phase(x_spot - CUT, x_spot <= 2 * CUT)
     x_forward = np.block([[x_cos, x_sin], [-x_sin, x_cos]])
     return y_inverse, x_forward.T, x_forward, y_inverse.T
@@ -120,16 +120,11 @@
     return upright(x), upright(y)
 
 
-def live_column(counts_ref, sheet, team):
-    line = lax.broadcasted_iota(jnp.int32, (LINES, EDGE), 0)
-    return line < counts_ref[team * SHEETS + sheet]
-
-
-def live_sticks(sticks_ref, counts_ref, sheet):
+def live_sticks(sticks_ref, live_ref):
     rows = []
     for part in range(2):
         for team in range(TEAMS):
-            live = live_column(counts_ref, sheet, team)
+            live = live_ref[team * LINES : (team + 1) * LINES, :1] > 0.5
             rows.append(jnp.where(live, sticks_ref[team, part], 0.0))
     return jnp.concatenate(rows, axis=0)
 
@@ -139,7 +134,10 @@
     return jnp.where(atoms == atom_row, 1.0, 0.0).astype(BF16)
 
 
-def place_kernel(sheet_ref, cols_ref, atom_hbm, pos_hbm, radius_hbm, a_ref, place_ref, atom_ref, pos_ref, radius_ref, sem):
+def place_kernel(
+    sheet_ref, counts_ref, cols_ref, atom_hbm, pos_hbm, radius_hbm,
+    a_ref, place_ref, live_ref, atom_ref, pos_ref, radius_ref, sem,
+):
     loads = [
         pltpu.make_async_copy(source, target, sem.at[k])
         for k, (source, target) in enumerate(
@@ -148,6 +146,10 @@
     ]
     for load in loads:
         load.start()
+    for team in range(TEAMS):
+        line = lax.broadcasted_iota(jnp.int32, (LINES, 128), 0)
+        live = line < counts_ref[team * SHEETS + sheet_ref[0]]
+        live_ref[team * LINES : (team + 1) * LINES, :] = jnp.where(live, 1.0, 0.0)
     gx, gy = own_lateral(cols_ref, sheet_ref[0])
     gxy = gx * gx + gy * gy
     for load in loads:
@@ -218,13 +220,13 @@
 
 
 def project_kernel(
-    sheet_ref, counts_ref, sticks_ref, th_ref, tl_ref, fold_ref, atom_ref, diag_ref, dij_ref, a_ref, place_ref,
+    sticks_ref, th_ref, tl_ref, fold_ref, atom_ref, diag_ref, dij_ref, a_ref, place_ref, live_ref,
     out_ref, bh_ref, bl_ref, becp_ref, mask_ref,
 ):
     depth_factors(place_ref, bh_ref, bl_ref)
     for at in range(0, NPROJ, PCHUNK):
         mask_ref[:, at : at + PCHUNK] = member_of(atom_ref[:, at : at + PCHUNK])
-    coeff = split(live_sticks(sticks_ref, counts_ref, sheet_ref[0]))
+    coeff = split(live_sticks(sticks_ref, live_ref))
     both = dot3((th_ref[...], tl_ref[...]), coeff, NT)
     with_cos, with_sin = both[:EDGE], both[EDGE:]
     by_depth = with_cos + jnp.concatenate([-with_sin[:, STICKS:], with_sin[:, :STICKS]], axis=1)
@@ -287,8 +289,8 @@
             v_ref[at + 1] = value - high
     summed = jnp.sum(sticks_ref[every(DEPTH), :], axis=0, keepdims=True)
     out_ref[every(DEPTH), :] = jnp.broadcast_to(summed, (SHEETS, 128))
-    rows64 = lax.broadcasted_iota(jnp.int32, (HALF_ROWS, 128), 0)
-    half_rows = rows64.astype(F32).astype(BF16)
+    row_of = lax.broadcasted_iota(jnp.int32, (HALF_ROWS, 128), 0)
+    half_rows = row_of.astype(F32).astype(BF16)
     full_rows = lax.broadcasted_iota(jnp.int32, (256, 128), 0).astype(F32).astype(BF16)
     one, zero = jnp.ones((), BF16), jnp.zeros((), BF16)
 
@@ -310,13 +312,24 @@
                 value = tall(v_ref[k, r : r + 1, :], HALF_ROWS)
                 left_ref[slot, k * HALF_ROWS : (k + 1) * HALF_ROWS, lanes] = member * value
         total = total + mul(left_ref[slot], hot_ref[chunk], NT)
+    lone = x_ref[0] == HALF_ROWS
+    lone_spot = (lax.broadcasted_iota(jnp.int32, (32, 128), 0) == 0) & (
+        lax.broadcasted_iota(jnp.int32, (32, 128), 1) == CUT
+    )
+
+    def whole(value):
+        return jnp.sum(jnp.sum(value, axis=0, keepdims=True), axis=1, keepdims=True)
+
     grids = []
     for plane in range(DEPTH):
         parts = []
         for part in range(2):
             at = 2 * (2 * plane + part) * HALF_ROWS
             grid = total[at : at + HALF_ROWS] + total[at + HALF_ROWS : at + 2 * HALF_ROWS]
-            parts.append(jnp.concatenate([grid[:, :128], grid[:, 128:]], axis=0))
+            at = 2 * (2 * plane + part)
+            extra = whole(jnp.where(lone, v_ref[at] + v_ref[at + 1], 0.0))
+            extra = jnp.where(lone_spot, extra, 0.0)
+            parts.append(jnp.concatenate([grid[:, :128], grid[:, 128:], extra], axis=0))
         grids.append(jnp.concatenate(parts, axis=1))
     work = jnp.concatenate(grids, axis=0)
     work = dot3(split(work), (yih_ref[...], yil_ref[...]), NN)
@@ -343,11 +356,14 @@
         axis=0,
     )
     work = dot3(split(work), (yfh_ref[...], yfl_ref[...]), NN)
-    pieces = []
+    pieces, extras = [], []
     for p in range(DEPTH):
         for c in range(2):
             block = work[p * 128 : (p + 1) * 128, c * 128 : (c + 1) * 128]
-            pieces.append(jnp.concatenate([block[:HALF_ROWS], block[HALF_ROWS:]], axis=1))
+            pieces.append(
+                jnp.concatenate([block[:HALF_ROWS], block[HALF_ROWS : 2 * HALF_ROWS]], axis=1)
+            )
+            extras.append(whole(jnp.where(lone_spot, block[2 * HALF_ROWS :], 0.0)))
     high, low = split(jnp.concatenate(pieces, axis=0))
     for chunk in range(CHUNKS):
         hot = hot_ref[chunk]
@@ -355,7 +371,7 @@
         for inner in range(per):
             r = chunk * per + inner
             lanes = slice(inner * 128, (inner + 1) * 128)
-            member = rows64 == x_ref[0, r : r + 1, :]
+            member = row_of == x_ref[0, r : r + 1, :]
             for k in range(6):
                 pick_ref[k, r : r + 1, :] = jnp.sum(
                     jnp.where(member, found[k * HALF_ROWS : (k + 1) * HALF_ROWS, lanes], 0.0),
@@ -363,7 +379,8 @@
                     keepdims=True,
                 )
     for plane in range(DEPTH):
-        re, im = pick_ref[2 * plane], pick_ref[2 * plane + 1]
+        re = pick_ref[2 * plane] + jnp.where(lone, extras[2 * plane], 0.0)
+        im = pick_ref[2 * plane + 1] + jnp.where(lone, extras[2 * plane + 1], 0.0)
         out_ref[every(plane), :] = jnp.concatenate(
             [
                 jnp.concatenate([re[:, :STICKS], im[:, :STICKS]], axis=1),
@@ -374,7 +391,7 @@
 
 
 def finish_kernel(
-    sheet_ref, counts_ref, cols_ref, sticks_ref, back_ref, a_ref, place_ref, th_ref, tl_ref, fold_ref,
+    sheet_ref, cols_ref, sticks_ref, back_ref, a_ref, place_ref, live_ref, th_ref, tl_ref, fold_ref,
     out_ref, bh_ref, bl_ref,
 ):
     sheet = sheet_ref[0]
@@ -426,8 +443,8 @@
     gz = jnp.where(gz < EDGE // 2, gz, gz - EDGE).astype(F32)
     kinetic = 2.0 * (((gx * gx + gy * gy) + gz * gz) / (EDGE * EDGE))
     for team in range(TEAMS):
-        live = live_column(counts_ref, sheet, team)
         rows = slice(team * LINES, (team + 1) * LINES)
+        live = live_ref[rows, :1] > 0.5
         for part in range(2):
             value = kinetic[rows] * sticks_ref[team, part] + sums[part][rows]
             out_ref[team, part] = jnp.where(live, value, 0.0)
@@ -450,9 +467,9 @@
     return jax.ShapeDtypeStruct(dims, dtype)
 
 
-def make_places(sheet, cols, proj_atom, atom_pos, proj_radius):
+def make_places(sheet, counts, cols, proj_atom, atom_pos, proj_radius):
     return call(
-        place_kernel, "svhhh", (shape((2 * STICKS, NPROJ)), shape((2, NPROJ))),
+        place_kernel, "ssvhhh", (shape((2 * STICKS, NPROJ)), shape((2, NPROJ)), shape((STICKS, 128))),
         [
             pltpu.VMEM((1, NPROJ), jnp.int32),
             pltpu.VMEM((3, NATOM), F32),
@@ -460,19 +477,19 @@
             pltpu.SemaphoreType.DMA((3,)),
         ],
         flops=2 << 30,
-    )(sheet, cols, proj_atom.reshape(1, NPROJ), atom_pos, proj_radius.reshape(1, NPROJ))
+    )(sheet, counts, cols, proj_atom.reshape(1, NPROJ), atom_pos, proj_radius.reshape(1, NPROJ))
 
 
 FACTORS = [pltpu.VMEM((256, NPROJ), BF16)] * 2
 
 
-def project(sheet, counts, sticks, places, proj_atom, proj_diag, dij):
+def project(sticks, places, proj_atom, proj_diag, dij):
     return call(
-        project_kernel, "ssvvvvvvvvv", shape((SHEETS * ROWS, 2 * STICKS)),
+        project_kernel, "v" * 10, shape((SHEETS * ROWS, 2 * STICKS)),
         [*FACTORS, pltpu.VMEM((2, NPROJ), F32), pltpu.VMEM((NATOM, NPROJ), BF16)],
         flops=3 << 30,
     )(
-        sheet, counts, sticks, *split_table(depth_table()), fold_matrix(),
+        sticks, *split_table(depth_table()), fold_matrix(),
         proj_atom.reshape(1, NPROJ), proj_diag.reshape(1, NPROJ), dij.reshape(1, NPROJ), *places,
     )
 
@@ -494,9 +511,9 @@
     )(cols, sticks, padded, *tables)
 
 
-def finish(sheet, counts, cols, sticks, back, places):
-    return call(finish_kernel, "ssvvvvvvvv", shape((TEAMS, 2, LINES, EDGE)), FACTORS, flops=3 << 30)(
-        sheet, counts, cols, sticks, back, *places, *split_table(depth_table()), fold_matrix()
+def finish(sheet, cols, sticks, back, places):
+    return call(finish_kernel, "s" + "v" * 9, shape((TEAMS, 2, LINES, EDGE)), FACTORS, flops=3 << 30)(
+        sheet, cols, sticks, back, *places, *split_table(depth_table()), fold_matrix()
     )
 
 
@@ -520,12 +537,12 @@
     layout = line_lateral_place[: TEAMS * SHEETS * LINES].reshape(TEAMS, SHEETS, LINES)
     cols = jnp.transpose(layout, (1, 0, 2)).reshape(SHEETS, STICKS)
     sticks = lax.all_to_all(orbital_coefficients, "tg", split_axis=0, concat_axis=0, tiled=True)
-    places = make_places(sheet, cols, proj_atom, atom_pos, proj_radius)
-    by_depth = project(sheet, stick_count, sticks, places, proj_atom, proj_diag, ionic_pseudo_dij)
+    places = make_places(sheet, stick_count, cols, proj_atom, atom_pos, proj_radius)
+    by_depth = project(sticks, places, proj_atom, proj_diag, ionic_pseudo_dij)
     by_plane = over_sheets(by_depth)
     picked = plane_work(cols, by_plane, potential)
     back = over_sheets(picked)
-    done = finish(sheet, stick_count, cols, sticks, back, places)
+    done = finish(sheet, cols, sticks, back, places)
     return lax.all_to_all(done, "tg", split_axis=0, concat_axis=0, tiled=True)
 
 

time: 83 us -> 80.7 us (0.972)
  Pallas kernels: 16.9 us -> 15.2 us
    pallas_call x1, Pallas kernels: 9.03 us -> 7.8 us  [plane_work(): call(plane_kernel, 'v' * 11, shape((SHEETS * ROWS, 2 * STICKS)), [pltpu.V...]
    all_to_all x1, blocking collectives: 10.8 us -> 11.7 us  [body(): return lax.all_to_all(done, 'tg', split_axis=0, concat_axis=0, tiled=True)]
where the time goes in v4:
time: 80.7 us; the launch traced here: 80.2 us
  blocking collectives  27.2 us (34%)
  starting transfers between devices  22.1 us (27%)
  Pallas kernels  15.2 us (19%)
  waiting for transfers between devices  10.6 us (13%)
  local copies, waits for them, and re-layouts  4.91 us (6%)
    all_to_all x1, blocking collectives, over_sheets(): lax.all_to_all(sent, 'pw', split_axis=0, concat_axis=0, tiled=True)  15.5 us
    all_to_all x1, starting transfers between devices, over_sheets(): lax.all_to_all(sent, 'pw', split_axis=0, concat_axis=0, tiled=True)  11.9 us
    all_to_all x1, blocking collectives, body(): return lax.all_to_all(done, 'tg', split_axis=0, concat_axis=0, tiled=True)  11.7 us
    all_to_all x1, starting transfers between devices, body(): lax.all_to_all(orbital_coefficients, 'tg', split_axis=0, concat_axis=0, t...  10.1 us
    all_to_all x1, waiting for transfers between devices, over_sheets(): lax.all_to_all(sent, 'pw', split_axis=0, concat_axis=0, tiled=True)  9.08 us
    pallas_call x1, Pallas kernels, plane_work(): call(plane_kernel, 'v' * 11, shape((SHEETS * ROWS, 2 * STICKS)), [pltpu.V...  7.8 us
    pallas_call x1, Pallas kernels, project(): call(project_kernel, 'v' * 10, shape((SHEETS * ROWS, 2 * STICKS)), [*FACT...  3.26 us
    pallas_call x1, Pallas kernels, finish(): call(finish_kernel, 's' + 'v' * 9, shape((TEAMS, 2, LINES, EDGE)), FACTOR...  2.2 us
  transfers between devices with their start and end apart: 2, of which 2 were waited for; matrix products, arithmetic and copies ran while one was open for 3% of the time, Pallas kernels for 2%

profile of v4, /device:TPU:1, one launch (start us, length us, event | category | flops | bytes accessed | tf_op | source)
XLA Modules:
  0.0 80.2 jit_solution(11779506423272277207)
XLA Ops:
  0.0 10.1 %all-to-all-start = ((f32[8,2,8,192]{3,2,1,0:T(8,128)}), f32[8,2,8,192]{3,2,1,0:T(8,128)S(1)}, u32[]{:S(2)}, u32[]{:S(2)}) async-start(f32[8,2,8,192]{3,2,1,0:T(8,128)} %param.23), calls=%async_computation | async-start | bytes 262144 | tf_op jit(solution)/shard_map/all_to_all | solution.py:539
  10.2 0.0 slice-start
  10.2 0.7 slice-done
  10.9 0.2 reshape.46
  11.0 0.1 copy.24
  11.1 0.0 copy-start
  11.1 0.0 copy-start.1
  11.1 0.0 copy-start.2
  11.1 0.1 copy.27.cols_ref
  11.2 0.0 copy-start.5
  11.2 0.6 copy-done
  11.9 0.0 copy-done.1
  11.9 0.0 copy-done.2
  11.9 0.0 copy-done.5
  11.9 0.0 copy-start.4
  11.9 0.0 copy-start.10
  11.9 0.0 copy-start.11
  11.9 0.0 copy-start.16
  11.9 1.9 %shard_map.217 = (f32[128,2048]{1,0:T(8,128)S(1)}, f32[2,2048]{1,0:T(2,128)S(1)}, f32[64,128]{1,0:T(8,128)S(1)}) custom-call(s32[1]{0:T(128)} %bitcast.sheet_ref, s32[512]{0:T(512)S(1)} %copy-done.5, s32[64,64]{1,0:T(8,128)S(1)} %copy.27.cols_ref, s32[1,2048]{1,0:T(1,128)S(1)} %bitcast.15, f32[3,512]{1,0:T(4,128)S(1)} %copy-done, f32[1,2048]{1,0:T(1,128)S(1)} %bitcast.14), custom_call_target="tpu_custom_call" | custom-call | flops 2147483648 | bytes 4194304 | tf_op jit(solution)/shard_map/pallas_call | solution.py:471
  13.9 0.0 copy-start.17
  13.9 0.0 copy-start.3
  13.9 1.5 %all-to-all-done.sticks_ref = f32[8,2,8,192]{3,2,1,0:T(8,128)S(1)} async-done(((f32[8,2,8,192]{3,2,1,0:T(8,128)}), f32[8,2,8,192]{3,2,1,0:T(8,128)S(1)}, u32[]{:S(2)}, u32[]{:S(2)}) %all-to-all-start) | async-done | bytes 98336 | tf_op jit(solution)/shard_map/all_to_all | solution.py:539
  15.4 0.0 copy-done.4
  15.4 0.0 copy-done.10
  15.4 0.0 copy-done.11
  15.5 0.0 copy-done.16
  15.5 0.0 copy-done.3
  15.5 0.0 copy-start.19
  15.5 3.3 %shard_map.218 = f32[256,128]{1,0:T(8,128)} custom-call(f32[8,2,8,192]{3,2,1,0:T(8,128)S(1)} %all-to-all-done.sticks_ref, bf16[384,192]{1,0:T(8,128)(2,1)S(1)} %copy-done.11, bf16[384,192]{1,0:T(8,128)(2,1)S(1)} %copy-done.10, bf16[192,256]{1,0:T(8,128)(2,1)S(1)} %copy-done.16, s32[1,2048]{1,0:T(1,128)S(1)} %bitcast.16, f32[1,2048]{1,0:T(1,128)S(1)} %bitcast.17, ...), custom_call_target="tpu_custom_call" | custom-call | flops 3221225472 | bytes 4194304 | tf_op jit(solution)/shard_map/pallas_call | solution.py:487
  18.7 0.0 copy-done.17
  18.7 11.9 %all-to-all-start.1 = ((f32[64,4,128]{2,1,0:T(4,128)}), f32[64,4,128]{2,1,0:T(4,128)S(1)}, u32[]{:S(2)}, u32[]{:S(2)}) async-start(f32[64,4,128]{2,1,0:T(4,128)} %bitcast.7), calls=%async_computation.1 | async-start | bytes 262144 | tf_op jit(solution)/shard_map/all_to_all | solution.py:522
  30.7 0.0 copy-done.19
  30.7 0.0 copy-start.12
  30.7 0.0 copy-start.13
  30.7 0.0 copy-start.14
  30.7 0.0 copy-start.15
  30.8 1.2 %reshape.54 = f32[3,192,192]{2,1,0:T(8,128)} reshape(f32[3,36864]{1,0:T(4,128)S(1)} %copy-done.19) | data formatting | bytes 884736 | tf_op jit(solution)/shard_map/reshape | solution.py:499
  32.0 0.0 copy-start.6
  32.0 0.0 copy-start.7
  32.0 0.0 copy-start.8
  32.0 0.0 copy-start.9
  32.0 1.2 %pad.4.potential_ref = f32[3,192,256]{2,1,0:T(8,128)S(1)} pad(f32[3,192,192]{2,1,0:T(8,128)} %reshape.54, f32[]{:T(128)} %constant.28.clone.1), padding=0_0x0_0x0_64 | pad | bytes 1032196 | tf_op jit(solution)/shard_map/jit(_pad)/pad | solution.py:499
  33.2 9.1 %all-to-all-done.1 = f32[64,4,128]{2,1,0:T(4,128)S(1)} async-done(((f32[64,4,128]{2,1,0:T(4,128)}), f32[64,4,128]{2,1,0:T(4,128)S(1)}, u32[]{:S(2)}, u32[]{:S(2)}) %all-to-all-start.1) | async-done | bytes 131104 | tf_op jit(solution)/shard_map/all_to_all | solution.py:522
  42.3 0.0 copy-done.12
  42.3 0.0 copy-done.13
  42.3 0.0 copy-done.14
  42.3 0.0 copy-done.15
  42.3 0.0 copy-done.6
  42.3 0.0 copy-done.7
  42.3 0.0 copy-done.8
  42.3 0.0 copy-done.9
  42.3 0.0 copy-start.18
  42.3 7.8 %shard_map.219 = f32[256,128]{1,0:T(8,128)S(1)} custom-call(s32[64,64]{1,0:T(8,128)S(1)} %copy.27.cols_ref, f32[256,128]{1,0:T(8,128)S(1)} %bitcast.11, f32[3,192,256]{2,1,0:T(8,128)S(1)} %pad.4.potential_ref, bf16[256,512]{1,0:T(8,128)(2,1)S(1)} %copy-done.9, bf16[256,512]{1,0:T(8,128)(2,1)S(1)} %copy-done.8, bf16[384,256]{1,0:T(8,128)(2,1)S(1)} %copy-done.15, ...), custom_call_target="tpu_custom_call" | custom-call | flops 8589934592 | bytes 4194304 | tf_op jit(solution)/shard_map/pallas_call | solution.py:500
  50.1 15.5 %all_to_all.20 = f32[64,4,128]{2,1,0:T(4,128)S(1)} all-to-all(f32[64,4,128]{2,1,0:T(4,128)S(1)} %bitcast.12), channel_id=1, replica_groups=mesh['tg'=8,'pw'=64] {'pw'}, dimensions={0} | all-to-all | bytes 262144 | tf_op jit(solution)/shard_map/all_to_all | solution.py:522
  65.6 0.0 copy-done.18
  65.6 2.2 %shard_map.220 = f32[8,2,8,192]{3,2,1,0:T(8,128)S(1)} custom-call(s32[1]{0:T(128)} %bitcast.sheet_ref, s32[64,64]{1,0:T(8,128)S(1)} %copy.27.cols_ref, f32[8,2,8,192]{3,2,1,0:T(8,128)S(1)} %all-to-all-done.sticks_ref, f32[256,128]{1,0:T(8,128)S(1)} %bitcast.13, f32[128,2048]{1,0:T(8,128)S(1)} %copy-done.18, f32[2,2048]{1,0:T(2,128)S(1)} %get-tuple-element.9.place_ref, ...), custom_call_target="tpu_custom_call" | custom-call | flops 3221225472 | bytes 4194304 | tf_op jit(solution)/shard_map/pallas_call | solution.py:515
  67.8 11.7 %all_to_all.21 = f32[8,2,8,192]{3,2,1,0:T(8,128)S(1)} all-to-all(f32[8,2,8,192]{3,2,1,0:T(8,128)S(1)} %shard_map.220), channel_id=1, replica_groups=mesh['tg'=8,'pw'=64] {'tg'}, dimensions={0} | all-to-all | bytes 196608 | tf_op jit(solution)/shard_map/all_to_all | solution.py:546
  79.6 0.7 copy.29
Async XLA Ops:
  0.0 15.4 %all-to-all-start = ((f32[8,2,8,192]{3,2,1,0:T(8,128)}), f32[8,2,8,192]{3,2,1,0:T(8,128)S(1)}, u32[]{:S(2)}, u32[]{:S(2)}) async-start(f32[8,2,8,192]{3,2,1,0:T(8,128)} %param.23), calls=%async_computation | async-start | bytes 262144 | tf_op jit(solution)/shard_map/all_to_all | solution.py:539
  10.2 0.7 slice-start
  11.1 0.7 copy-start
  11.1 0.7 copy-start.1
  11.1 0.7 copy-start.2
  11.2 0.7 copy-start.5
  11.9 3.5 %copy-start.4 = (f32[2048]{0:T(1024)S(1)}, f32[2048]{0:T(1024)}, u32[]{:S(2)}) copy-start(f32[2048]{0:T(1024)} %param.31) | copy-start | bytes 24580
  11.9 3.5 %copy-start.10 = (bf16[384,192]{1,0:T(8,128)(2,1)S(1)}, bf16[384,192]{1,0:T(8,128)(2,1)}, u32[]{:S(2)}) copy-start(bf16[384,192]{1,0:T(8,128)(2,1)} %constant.30.clone.tl_ref) | copy-start | bytes 442372
  11.9 3.5 %copy-start.11 = (bf16[384,192]{1,0:T(8,128)(2,1)S(1)}, bf16[384,192]{1,0:T(8,128)(2,1)}, u32[]{:S(2)}) copy-start(bf16[384,192]{1,0:T(8,128)(2,1)} %constant.29.clone.th_ref) | copy-start | bytes 442372
  11.9 3.5 %copy-start.16 = (bf16[192,256]{1,0:T(8,128)(2,1)S(1)}, bf16[192,256]{1,0:T(8,128)(2,1)}, u32[]{:S(2)}) copy-start(bf16[192,256]{1,0:T(8,128)(2,1)} %constant.31.clone.fold_ref) | copy-start | bytes 294916
  13.9 4.9 %copy-start.17 = (f32[128,2048]{1,0:T(8,128)}, f32[128,2048]{1,0:T(8,128)S(1)}, u32[]{:S(2)}) copy-start(f32[128,2048]{1,0:T(8,128)S(1)} %get-tuple-element.8.a_ref) | copy-start | bytes 3145732
  13.9 1.6 %copy-start.3 = (f32[2048]{0:T(1024)S(1)}, f32[2048]{0:T(1024)}, u32[]{:S(2)}) copy-start(f32[2048]{0:T(1024)} %param.30) | copy-start | bytes 24580
  15.5 15.2 %copy-start.19 = (f32[3,36864]{1,0:T(4,128)S(1)}, f32[3,36864]{1,0:T(4,128)}, u32[]{:S(2)}) copy-start(f32[3,36864]{1,0:T(4,128)} %param.24) | copy-start | bytes 1327108
  18.7 23.5 %all-to-all-start.1 = ((f32[64,4,128]{2,1,0:T(4,128)}), f32[64,4,128]{2,1,0:T(4,128)S(1)}, u32[]{:S(2)}, u32[]{:S(2)}) async-start(f32[64,4,128]{2,1,0:T(4,128)} %bitcast.7), calls=%async_computation.1 | async-start | bytes 262144 | tf_op jit(solution)/shard_map/all_to_all | solution.py:522
  30.7 11.6 %copy-start.12 = (bf16[256,384]{1,0:T(8,128)(2,1)S(1)}, bf16[256,384]{1,0:T(8,128)(2,1)}, u32[]{:S(2)}) copy-start(bf16[256,384]{1,0:T(8,128)(2,1)} %constant.37.clone.xfl_ref) | copy-start | bytes 589828
  30.7 11.6 %copy-start.13 = (bf16[256,384]{1,0:T(8,128)(2,1)S(1)}, bf16[256,384]{1,0:T(8,128)(2,1)}, u32[]{:S(2)}) copy-start(bf16[256,384]{1,0:T(8,128)(2,1)} %constant.36.clone.xfh_ref) | copy-start | bytes 589828
  30.7 11.6 %copy-start.14 = (bf16[384,256]{1,0:T(8,128)(2,1)S(1)}, bf16[384,256]{1,0:T(8,128)(2,1)}, u32[]{:S(2)}) copy-start(bf16[384,256]{1,0:T(8,128)(2,1)} %constant.35.clone.xil_ref) | copy-start | bytes 589828
  30.7 11.5 %copy-start.15 = (bf16[384,256]{1,0:T(8,128)(2,1)S(1)}, bf16[384,256]{1,0:T(8,128)(2,1)}, u32[]{:S(2)}) copy-start(bf16[384,256]{1,0:T(8,128)(2,1)} %constant.34.clone.xih_ref) | copy-start | bytes 589828
  32.0 10.3 %copy-start.6 = (bf16[512,256]{1,0:T(8,128)(2,1)S(1)}, bf16[512,256]{1,0:T(8,128)(2,1)}, u32[]{:S(2)}) copy-start(bf16[512,256]{1,0:T(8,128)(2,1)} %constant.39.clone.yfl_ref) | copy-start | bytes 786436
  32.0 10.3 %copy-start.7 = (bf16[512,256]{1,0:T(8,128)(2,1)S(1)}, bf16[512,256]{1,0:T(8,128)(2,1)}, u32[]{:S(2)}) copy-start(bf16[512,256]{1,0:T(8,128)(2,1)} %constant.38.clone.yfh_ref) | copy-start | bytes 786436
  32.0 10.3 %copy-start.8 = (bf16[256,512]{1,0:T(8,128)(2,1)S(1)}, bf16[256,512]{1,0:T(8,128)(2,1)}, u32[]{:S(2)}) copy-start(bf16[256,512]{1,0:T(8,128)(2,1)} %constant.33.clone.yil_ref) | copy-start | bytes 786436
  32.0 10.3 %copy-start.9 = (bf16[256,512]{1,0:T(8,128)(2,1)S(1)}, bf16[256,512]{1,0:T(8,128)(2,1)}, u32[]{:S(2)}) copy-start(bf16[256,512]{1,0:T(8,128)(2,1)} %constant.32.clone.yih_ref) | copy-start | bytes 786436
  42.3 23.3 %copy-start.18 = (f32[128,2048]{1,0:T(8,128)S(1)}, f32[128,2048]{1,0:T(8,128)}, u32[]{:S(2)}) copy-start(f32[128,2048]{1,0:T(8,128)} %copy-done.17) | copy-start | bytes 3145732

commit v5 on v4

--- a/solution.py
+++ b/solution.py
@@ -82,6 +82,12 @@
 
 def dot3(left, right, form):
     return mul(left[0], right[0], form) + mul(left[0], right[1], form) + mul(left[1], right[0], form)
+
+
+def stacked(left, right, form):
+    rows = left[0].shape[0]
+    both = mul(jnp.concatenate(left, axis=0), right[0], form)
+    return both[:rows] + both[rows:] + mul(left[0], right[1], form)
 
 
 def lateral_split(cols):
@@ -205,6 +211,11 @@
                     bl_ref[base : base + 16, here] = low
 
 
+def factor_kernel(place_ref, token_ref, bh_ref, bl_ref):
+    del token_ref
+    depth_factors(place_ref, bh_ref, bl_ref)
+
+
 def rows_of(re, im):
     re_high = re.astype(BF16).astype(F32)
     im_high = im.astype(BF16).astype(F32)
@@ -245,7 +256,7 @@
     out_ref[every(DEPTH), :] = jnp.zeros((SHEETS, 128), F32)
     for at in range(0, NPROJ, PCHUNK):
         here = slice(at, at + PCHUNK)
-        y = dot3(paired, (bh_ref[:, here], bl_ref[:, here]), NN)
+        y = stacked(paired, (bh_ref[:, here], bl_ref[:, here]), NN)
         y_re, y_im = y[:STICKS], y[STICKS:]
         a_re, a_im = a_ref[:STICKS, here], a_ref[STICKS:, here]
         becp_ref[0:1, here] = jnp.sum(a_re * y_re + a_im * y_im, axis=0, keepdims=True)
@@ -270,7 +281,7 @@
 def plane_kernel(
     cols_ref, sticks_ref, potential_ref,
     yih_ref, yil_ref, xih_ref, xil_ref, xfh_ref, xfl_ref, yfh_ref, yfl_ref,
-    out_ref, x_ref, v_ref, hot_ref, left_ref, pick_ref,
+    out_ref, token_ref, x_ref, v_ref, hot_ref, left_ref, pick_ref,
 ):
     half = SHEETS // 2
     x, y = lateral_split(jnp.concatenate([cols_ref[:half, :], cols_ref[half:, :]], axis=1))
@@ -287,6 +298,7 @@
             at = 2 * (2 * plane + part)
             v_ref[at] = high
             v_ref[at + 1] = value - high
+    token_ref[...] = jnp.zeros((8, 128), F32)
     summed = jnp.sum(sticks_ref[every(DEPTH), :], axis=0, keepdims=True)
     out_ref[every(DEPTH), :] = jnp.broadcast_to(summed, (SHEETS, 128))
     row_of = lax.broadcasted_iota(jnp.int32, (HALF_ROWS, 128), 0)
@@ -364,10 +376,10 @@
                 jnp.concatenate([block[:HALF_ROWS], block[HALF_ROWS : 2 * HALF_ROWS]], axis=1)
             )
             extras.append(whole(jnp.where(lone_spot, block[2 * HALF_ROWS :], 0.0)))
-    high, low = split(jnp.concatenate(pieces, axis=0))
+    stack = jnp.concatenate(split(jnp.concatenate(pieces, axis=0)), axis=0)
     for chunk in range(CHUNKS):
-        hot = hot_ref[chunk]
-        found = mul(high, hot, NN) + mul(low, hot, NN)
+        found = mul(stack, hot_ref[chunk], NN)
+        found = found[: 6 * HALF_ROWS] + found[6 * HALF_ROWS :]
         for inner in range(per):
             r = chunk * per + inner
             lanes = slice(inner * 128, (inner + 1) * 128)
@@ -391,11 +403,9 @@
 
 
 def finish_kernel(
-    sheet_ref, cols_ref, sticks_ref, back_ref, a_ref, place_ref, live_ref, th_ref, tl_ref, fold_ref,
-    out_ref, bh_ref, bl_ref,
+    sheet_ref, cols_ref, sticks_ref, back_ref, a_ref, live_ref, bh_ref, bl_ref, th_ref, tl_ref, fold_ref, out_ref,
 ):
     sheet = sheet_ref[0]
-    depth_factors(place_ref, bh_ref, bl_ref)
     vnl = jnp.zeros((2 * STICKS, 256), F32)
     step = 2 * PCHUNK
     for at in range(0, NPROJ, step):
@@ -418,7 +428,7 @@
         weighted = split(
             jnp.concatenate([a_re * w_re - a_im * w_im, a_re * w_im + a_im * w_re], axis=0)
         )
-        vnl = vnl + dot3(weighted, (bh_ref[:, here], bl_ref[:, here]), NT)
+        vnl = vnl + stacked(weighted, (bh_ref[:, here], bl_ref[:, here]), NT)
     vnl = split(
         jnp.concatenate(
             [
@@ -498,7 +508,7 @@
     tables = [piece for table in lateral_tables() for piece in split_table(table)]
     padded = jnp.pad(potential.reshape(DEPTH, EDGE, EDGE), ((0, 0), (0, 0), (0, 256 - EDGE)))
     return call(
-        plane_kernel, "v" * 11, shape((SHEETS * ROWS, 2 * STICKS)),
+        plane_kernel, "v" * 11, (shape((SHEETS * ROWS, 2 * STICKS)), shape((8, 128))),
         [
             pltpu.VMEM((2, SHEETS // 2, 128), jnp.int32),
             pltpu.VMEM((12, SHEETS // 2, 128), F32),
@@ -511,9 +521,14 @@
     )(cols, sticks, padded, *tables)
 
 
-def finish(sheet, cols, sticks, back, places):
-    return call(finish_kernel, "s" + "v" * 9, shape((TEAMS, 2, LINES, EDGE)), FACTORS, flops=3 << 30)(
-        sheet, cols, sticks, back, *places, *split_table(depth_table()), fold_matrix()
+def make_factors(place, token):
+    factor = shape((256, NPROJ), BF16)
+    return call(factor_kernel, "vv", (factor, factor), flops=1 << 30)(place, token)
+
+
+def finish(sheet, cols, sticks, back, a, live, factors):
+    return call(finish_kernel, "s" + "v" * 10, shape((TEAMS, 2, LINES, EDGE)), flops=3 << 30)(
+        sheet, cols, sticks, back, a, live, *factors, *split_table(depth_table()), fold_matrix()
     )
 
 
@@ -540,9 +555,10 @@
     places = make_places(sheet, stick_count, cols, proj_atom, atom_pos, proj_radius)
     by_depth = project(sticks, places, proj_atom, proj_diag, ionic_pseudo_dij)
     by_plane = over_sheets(by_depth)
-    picked = plane_work(cols, by_plane, potential)
+    picked, token = plane_work(cols, by_plane, potential)
     back = over_sheets(picked)
-    done = finish(sheet, cols, sticks, back, places)
+    a, place, live = places
+    done = finish(sheet, cols, sticks, back, a, live, make_factors(place, token))
     return lax.all_to_all(done, "tg", split_axis=0, concat_axis=0, tiled=True)
 
 

time: 80.7 us -> 84.2 us (1.043)
  blocking collectives: 27.2 us -> 11.7 us
  waiting for transfers between devices: 10.6 us -> 20.4 us
  starting transfers between devices: 22.1 us -> 26.9 us
  local copies, waits for them, and re-layouts: 4.91 us -> 8.28 us
  Pallas kernels: 15.2 us -> 16.1 us
    all_to_all x1 -> x0, blocking collectives: 15.5 us -> none  [over_sheets(): lax.all_to_all(sent, 'pw', split_axis=0, concat_axis=0, tiled=True)]
    all_to_all x1 -> x2, waiting for transfers between devices: 9.08 us -> 18.9 us  [over_sheets(): lax.all_to_all(sent, 'pw', split_axis=0, concat_axis=0, tiled=True)]
    all_to_all x1 -> x2, starting transfers between devices: 11.9 us -> 16.7 us  [over_sheets(): lax.all_to_all(sent, 'pw', split_axis=0, concat_axis=0, tiled=True)]
    unnamed x41 -> x45, local copies, waits for them, and re-layouts: 1.43 us -> 4.84 us
    pallas_call x2 -> x3, Pallas kernels: 9.99 us -> 10.9 us  [the longest x1 8.62 us: plane_work(): call(plane_kernel, 'v' * 11, (shape((SHEETS * ROWS, 2 * STICKS)), shape((...]
  transfers between devices with their start and end apart: 2 -> 3, of which waited for: 2 -> 3; matrix products, arithmetic and copies ran while one was open for 3% -> 3% of each run, Pallas kernels for 2% -> 4%
where the time goes in v5:
time: 84.2 us; the launch traced here: 83.6 us
  starting transfers between devices  26.9 us (32%)
  waiting for transfers between devices  20.4 us (24%)
  Pallas kernels  16.1 us (19%)
  blocking collectives  11.7 us (14%)
  local copies, waits for them, and re-layouts  8.28 us (10%)
    all_to_all x2, waiting for transfers between devices, over_sheets(): lax.all_to_all(sent, 'pw', split_axis=0, concat_axis=0, tiled=True)  18.9 us
    all_to_all x2, starting transfers between devices, over_sheets(): lax.all_to_all(sent, 'pw', split_axis=0, concat_axis=0, tiled=True)  16.7 us
    all_to_all x1, blocking collectives, body(): return lax.all_to_all(done, 'tg', split_axis=0, concat_axis=0, tiled=True)  11.7 us
    all_to_all x1, starting transfers between devices, body(): lax.all_to_all(orbital_coefficients, 'tg', split_axis=0, concat_axis=0, t...  10.1 us
    pallas_call x1, Pallas kernels, plane_work(): call(plane_kernel, 'v' * 11, (shape((SHEETS * ROWS, 2 * STICKS)), shape((...  8.62 us
    unnamed x45, local copies, waits for them, and re-layouts  4.84 us
    pallas_call x1, Pallas kernels, project(): call(project_kernel, 'v' * 10, shape((SHEETS * ROWS, 2 * STICKS)), [*FACT...  3.28 us
    pallas_call x1, Pallas kernels, make_places(): call(place_kernel, 'ssvhhh', (shape((2 * STICKS, NPROJ)), shape((2, NPROJ...  1.94 us
  transfers between devices with their start and end apart: 3, of which 3 were waited for; matrix products, arithmetic and copies ran while one was open for 3% of the time, Pallas kernels for 4%

profile of v5, /device:TPU:1, one launch (start us, length us, event | category | flops | bytes accessed | tf_op | source)
XLA Modules:
  0.0 83.6 jit_solution(5037884149120399819)
XLA Ops:
  0.0 10.1 %all-to-all-start = ((f32[8,2,8,192]{3,2,1,0:T(8,128)}), f32[8,2,8,192]{3,2,1,0:T(8,128)S(1)}, u32[]{:S(2)}, u32[]{:S(2)}) async-start(f32[8,2,8,192]{3,2,1,0:T(8,128)} %param.23), calls=%async_computation | async-start | bytes 262144 | tf_op jit(solution)/shard_map/all_to_all | solution.py:554
  10.2 0.0 slice-start
  10.2 0.7 slice-done
  10.9 0.2 reshape.46
  11.0 0.1 copy.24
  11.1 0.0 copy-start
  11.1 0.0 copy-start.1
  11.1 0.0 copy-start.2
  11.1 0.1 copy.27.cols_ref
  11.2 0.0 copy-start.5
  11.2 0.6 copy-done
  11.9 0.0 copy-done.1
  11.9 0.0 copy-done.2
  11.9 0.0 copy-done.5
  11.9 0.0 copy-start.4
  11.9 0.0 copy-start.10
  11.9 0.0 copy-start.11
  11.9 0.0 copy-start.16
  11.9 1.9 %shard_map.217 = (f32[128,2048]{1,0:T(8,128)S(1)}, f32[2,2048]{1,0:T(2,128)S(1)}, f32[64,128]{1,0:T(8,128)S(1)}) custom-call(s32[1]{0:T(128)} %bitcast.sheet_ref, s32[512]{0:T(512)S(1)} %copy-done.5, s32[64,64]{1,0:T(8,128)S(1)} %copy.27.cols_ref, s32[1,2048]{1,0:T(1,128)S(1)} %bitcast.14, f32[3,512]{1,0:T(4,128)S(1)} %copy-done, f32[1,2048]{1,0:T(1,128)S(1)} %bitcast.13), custom_call_target="tpu_custom_call" | custom-call | flops 2147483648 | bytes 4194304 | tf_op jit(solution)/shard_map/pallas_call | solution.py:481
  13.9 0.0 copy-start.19
  13.9 0.0 copy-start.3
  13.9 1.5 %all-to-all-done.sticks_ref = f32[8,2,8,192]{3,2,1,0:T(8,128)S(1)} async-done(((f32[8,2,8,192]{3,2,1,0:T(8,128)}), f32[8,2,8,192]{3,2,1,0:T(8,128)S(1)}, u32[]{:S(2)}, u32[]{:S(2)}) %all-to-all-start) | async-done | bytes 98336 | tf_op jit(solution)/shard_map/all_to_all | solution.py:554
  15.4 0.0 copy-done.4
  15.4 0.0 copy-done.10
  15.4 0.0 copy-done.11
  15.5 0.0 copy-done.16
  15.5 0.0 copy-done.3
  15.5 0.0 copy-start.21
  15.5 3.3 %shard_map.218 = f32[256,128]{1,0:T(8,128)} custom-call(f32[8,2,8,192]{3,2,1,0:T(8,128)S(1)} %all-to-all-done.sticks_ref, bf16[384,192]{1,0:T(8,128)(2,1)S(1)} %copy-done.11, bf16[384,192]{1,0:T(8,128)(2,1)S(1)} %copy-done.10, bf16[192,256]{1,0:T(8,128)(2,1)S(1)} %copy-done.16, s32[1,2048]{1,0:T(1,128)S(1)} %bitcast.15, f32[1,2048]{1,0:T(1,128)S(1)} %bitcast.16, ...), custom_call_target="tpu_custom_call" | custom-call | flops 3221225472 | bytes 4194304 | tf_op jit(solution)/shard_map/pallas_call | solution.py:497
  18.8 0.0 copy-done.19
  18.8 11.9 %all-to-all-start.1 = ((f32[64,4,128]{2,1,0:T(4,128)}), f32[64,4,128]{2,1,0:T(4,128)S(1)}, u32[]{:S(2)}, u32[]{:S(2)}) async-start(f32[64,4,128]{2,1,0:T(4,128)} %bitcast.7), calls=%async_computation.1 | async-start | bytes 262144 | tf_op jit(solution)/shard_map/all_to_all | solution.py:537
  30.7 0.0 copy-done.21
  30.7 0.0 copy-start.12
  30.7 0.0 copy-start.13
  30.7 0.0 copy-start.14
  30.8 0.0 copy-start.15
  30.8 1.2 %reshape.54 = f32[3,192,192]{2,1,0:T(8,128)} reshape(f32[3,36864]{1,0:T(4,128)S(1)} %copy-done.21) | data formatting | bytes 884736 | tf_op jit(solution)/shard_map/reshape | solution.py:509
  31.9 0.0 copy-start.6
  32.0 0.0 copy-start.7
  32.0 0.0 copy-start.8
  32.0 0.0 copy-start.9
  32.0 1.2 %pad.4.potential_ref = f32[3,192,256]{2,1,0:T(8,128)S(1)} pad(f32[3,192,192]{2,1,0:T(8,128)} %reshape.54, f32[]{:T(128)} %constant.28.clone.1), padding=0_0x0_0x0_64 | pad | bytes 1032196 | tf_op jit(solution)/shard_map/jit(_pad)/pad | solution.py:509
  33.2 9.1 %all-to-all-done.1 = f32[64,4,128]{2,1,0:T(4,128)S(1)} async-done(((f32[64,4,128]{2,1,0:T(4,128)}), f32[64,4,128]{2,1,0:T(4,128)S(1)}, u32[]{:S(2)}, u32[]{:S(2)}) %all-to-all-start.1) | async-done | bytes 131104 | tf_op jit(solution)/shard_map/all_to_all | solution.py:537
  42.3 0.0 copy-done.12
  42.3 0.0 copy-done.13
  42.3 0.0 copy-done.14
  42.3 0.0 copy-done.15
  42.3 0.0 copy-done.6
  42.3 0.0 copy-done.7
  42.3 0.0 copy-done.8
  42.3 0.0 copy-done.9
  42.3 8.6 %shard_map.219 = (f32[256,128]{1,0:T(8,128)}, f32[8,128]{1,0:T(8,128)S(1)}) custom-call(s32[64,64]{1,0:T(8,128)S(1)} %copy.27.cols_ref, f32[256,128]{1,0:T(8,128)S(1)} %bitcast.12, f32[3,192,256]{2,1,0:T(8,128)S(1)} %pad.4.potential_ref, bf16[256,512]{1,0:T(8,128)(2,1)S(1)} %copy-done.9, bf16[256,512]{1,0:T(8,128)(2,1)S(1)} %copy-done.8, ...), custom_call_target="tpu_custom_call" | custom-call | flops 8589934592 | bytes 4194304 | tf_op jit(solution)/shard_map/pallas_call | solution.py:510
  51.0 4.8 %all-to-all-start.2 = ((f32[64,4,128]{2,1,0:T(4,128)}), f32[64,4,128]{2,1,0:T(4,128)S(1)}, u32[]{:S(2)}, u32[]{:S(2)}) async-start(f32[64,4,128]{2,1,0:T(4,128)} %bitcast.9), calls=%async_computation.2 | async-start | bytes 262144 | tf_op jit(solution)/shard_map/all_to_all | solution.py:537
  55.8 1.0 %shard_map.220 = (bf16[256,2048]{1,0:T(8,128)(2,1)S(1)}, bf16[256,2048]{1,0:T(8,128)(2,1)S(1)}) custom-call(f32[2,2048]{1,0:T(2,128)S(1)} %get-tuple-element.13.place_ref, f32[8,128]{1,0:T(8,128)S(1)} %get-tuple-element.16.token_ref), custom_call_target="tpu_custom_call" | custom-call | flops 1073741824 | bytes 4194304 | tf_op jit(solution)/shard_map/pallas_call | solution.py:526
  56.8 0.0 copy-start.17
  56.8 1.0 %copy-done.17 = bf16[256,2048]{1,0:T(8,128)(2,1)} copy-done((bf16[256,2048]{1,0:T(8,128)(2,1)}, bf16[256,2048]{1,0:T(8,128)(2,1)S(1)}, u32[]{:S(2)}) %copy-start.17) | copy-done | bytes 1048600
  57.8 9.7 %all-to-all-done.2 = f32[64,4,128]{2,1,0:T(4,128)S(1)} async-done(((f32[64,4,128]{2,1,0:T(4,128)}), f32[64,4,128]{2,1,0:T(4,128)S(1)}, u32[]{:S(2)}, u32[]{:S(2)}) %all-to-all-start.2) | async-done | bytes 131104 | tf_op jit(solution)/shard_map/all_to_all | solution.py:537
  67.5 0.0 copy-start.18
  67.5 1.2 %copy-done.18 = bf16[256,2048]{1,0:T(8,128)(2,1)S(1)} copy-done((bf16[256,2048]{1,0:T(8,128)(2,1)S(1)}, bf16[256,2048]{1,0:T(8,128)(2,1)}, u32[]{:S(2)}) %copy-start.18) | copy-done | bytes 1048600
  68.7 0.0 copy-start.20
  68.7 1.2 %copy-done.20 = f32[128,2048]{1,0:T(8,128)S(1)} copy-done((f32[128,2048]{1,0:T(8,128)S(1)}, f32[128,2048]{1,0:T(8,128)}, u32[]{:S(2)}) %copy-start.20) | copy-done | bytes 1048600
  69.9 1.3 %shard_map.221 = f32[8,2,8,192]{3,2,1,0:T(8,128)S(1)} custom-call(s32[1]{0:T(128)} %bitcast.sheet_ref, s32[64,64]{1,0:T(8,128)S(1)} %copy.27.cols_ref, f32[8,2,8,192]{3,2,1,0:T(8,128)S(1)} %all-to-all-done.sticks_ref, f32[256,128]{1,0:T(8,128)S(1)} %bitcast.11, f32[128,2048]{1,0:T(8,128)S(1)} %copy-done.20, f32[64,128]{1,0:T(8,128)S(1)} %get-tuple-element.14.live_ref, ...), custom_call_target="tpu_custom_call" | custom-call | flops 3221225472 | bytes 4194304 | tf_op jit(solution)/shard_map/pallas_call | solution.py:530
  71.3 11.7 %all_to_all.20 = f32[8,2,8,192]{3,2,1,0:T(8,128)S(1)} all-to-all(f32[8,2,8,192]{3,2,1,0:T(8,128)S(1)} %shard_map.221), channel_id=1, replica_groups=mesh['tg'=8,'pw'=64] {'tg'}, dimensions={0} | all-to-all | bytes 196608 | tf_op jit(solution)/shard_map/all_to_all | solution.py:562
  82.9 0.7 copy.29
Async XLA Ops:
  0.0 15.4 %all-to-all-start = ((f32[8,2,8,192]{3,2,1,0:T(8,128)}), f32[8,2,8,192]{3,2,1,0:T(8,128)S(1)}, u32[]{:S(2)}, u32[]{:S(2)}) async-start(f32[8,2,8,192]{3,2,1,0:T(8,128)} %param.23), calls=%async_computation | async-start | bytes 262144 | tf_op jit(solution)/shard_map/all_to_all | solution.py:554
  10.2 0.7 slice-start
  11.1 0.7 copy-start
  11.1 0.7 copy-start.1
  11.1 0.7 copy-start.2
  11.2 0.7 copy-start.5
  11.9 3.5 %copy-start.4 = (f32[2048]{0:T(1024)S(1)}, f32[2048]{0:T(1024)}, u32[]{:S(2)}) copy-start(f32[2048]{0:T(1024)} %param.31) | copy-start | bytes 24580
  11.9 3.5 %copy-start.10 = (bf16[384,192]{1,0:T(8,128)(2,1)S(1)}, bf16[384,192]{1,0:T(8,128)(2,1)}, u32[]{:S(2)}) copy-start(bf16[384,192]{1,0:T(8,128)(2,1)} %constant.30.clone.tl_ref) | copy-start | bytes 442372
  11.9 3.5 %copy-start.11 = (bf16[384,192]{1,0:T(8,128)(2,1)S(1)}, bf16[384,192]{1,0:T(8,128)(2,1)}, u32[]{:S(2)}) copy-start(bf16[384,192]{1,0:T(8,128)(2,1)} %constant.29.clone.th_ref) | copy-start | bytes 442372
  11.9 3.5 %copy-start.16 = (bf16[192,256]{1,0:T(8,128)(2,1)S(1)}, bf16[192,256]{1,0:T(8,128)(2,1)}, u32[]{:S(2)}) copy-start(bf16[192,256]{1,0:T(8,128)(2,1)} %constant.31.clone.fold_ref) | copy-start | bytes 294916
  13.9 4.9 %copy-start.19 = (f32[128,2048]{1,0:T(8,128)}, f32[128,2048]{1,0:T(8,128)S(1)}, u32[]{:S(2)}) copy-start(f32[128,2048]{1,0:T(8,128)S(1)} %get-tuple-element.12.a_ref) | copy-start | bytes 3145732
  13.9 1.6 %copy-start.3 = (f32[2048]{0:T(1024)S(1)}, f32[2048]{0:T(1024)}, u32[]{:S(2)}) copy-start(f32[2048]{0:T(1024)} %param.30) | copy-start | bytes 24580
  15.5 15.2 %copy-start.21 = (f32[3,36864]{1,0:T(4,128)S(1)}, f32[3,36864]{1,0:T(4,128)}, u32[]{:S(2)}) copy-start(f32[3,36864]{1,0:T(4,128)} %param.24) | copy-start | bytes 1327108
  18.8 23.5 %all-to-all-start.1 = ((f32[64,4,128]{2,1,0:T(4,128)}), f32[64,4,128]{2,1,0:T(4,128)S(1)}, u32[]{:S(2)}, u32[]{:S(2)}) async-start(f32[64,4,128]{2,1,0:T(4,128)} %bitcast.7), calls=%async_computation.1 | async-start | bytes 262144 | tf_op jit(solution)/shard_map/all_to_all | solution.py:537
  30.7 11.6 %copy-start.12 = (bf16[256,384]{1,0:T(8,128)(2,1)S(1)}, bf16[256,384]{1,0:T(8,128)(2,1)}, u32[]{:S(2)}) copy-start(bf16[256,384]{1,0:T(8,128)(2,1)} %constant.37.clone.xfl_ref) | copy-start | bytes 589828
  30.7 11.6 %copy-start.13 = (bf16[256,384]{1,0:T(8,128)(2,1)S(1)}, bf16[256,384]{1,0:T(8,128)(2,1)}, u32[]{:S(2)}) copy-start(bf16[256,384]{1,0:T(8,128)(2,1)} %constant.36.clone.xfh_ref) | copy-start | bytes 589828
  30.7 11.6 %copy-start.14 = (bf16[384,256]{1,0:T(8,128)(2,1)S(1)}, bf16[384,256]{1,0:T(8,128)(2,1)}, u32[]{:S(2)}) copy-start(bf16[384,256]{1,0:T(8,128)(2,1)} %constant.35.clone.xil_ref) | copy-start | bytes 589828
  30.8 11.5 %copy-start.15 = (bf16[384,256]{1,0:T(8,128)(2,1)S(1)}, bf16[384,256]{1,0:T(8,128)(2,1)}, u32[]{:S(2)}) copy-start(bf16[384,256]{1,0:T(8,128)(2,1)} %constant.34.clone.xih_ref) | copy-start | bytes 589828
  31.9 10.4 %copy-start.6 = (bf16[512,256]{1,0:T(8,128)(2,1)S(1)}, bf16[512,256]{1,0:T(8,128)(2,1)}, u32[]{:S(2)}) copy-start(bf16[512,256]{1,0:T(8,128)(2,1)} %constant.39.clone.yfl_ref) | copy-start | bytes 786436
  32.0 10.4 %copy-start.7 = (bf16[512,256]{1,0:T(8,128)(2,1)S(1)}, bf16[512,256]{1,0:T(8,128)(2,1)}, u32[]{:S(2)}) copy-start(bf16[512,256]{1,0:T(8,128)(2,1)} %constant.38.clone.yfh_ref) | copy-start | bytes 786436
  32.0 10.4 %copy-start.8 = (bf16[256,512]{1,0:T(8,128)(2,1)S(1)}, bf16[256,512]{1,0:T(8,128)(2,1)}, u32[]{:S(2)}) copy-start(bf16[256,512]{1,0:T(8,128)(2,1)} %constant.33.clone.yil_ref) | copy-start | bytes 786436
  32.0 10.4 %copy-start.9 = (bf16[256,512]{1,0:T(8,128)(2,1)S(1)}, bf16[256,512]{1,0:T(8,128)(2,1)}, u32[]{:S(2)}) copy-start(bf16[256,512]{1,0:T(8,128)(2,1)} %constant.32.clone.yih_ref) | copy-start | bytes 786436
  51.0 16.5 %all-to-all-start.2 = ((f32[64,4,128]{2,1,0:T(4,128)}), f32[64,4,128]{2,1,0:T(4,128)S(1)}, u32[]{:S(2)}, u32[]{:S(2)}) async-start(f32[64,4,128]{2,1,0:T(4,128)} %bitcast.9), calls=%async_computation.2 | async-start | bytes 262144 | tf_op jit(solution)/shard_map/all_to_all | solution.py:537
  56.8 1.0 %copy-start.17 = (bf16[256,2048]{1,0:T(8,128)(2,1)}, bf16[256,2048]{1,0:T(8,128)(2,1)S(1)}, u32[]{:S(2)}) copy-start(bf16[256,2048]{1,0:T(8,128)(2,1)S(1)} %get-tuple-element.18.bl_ref) | copy-start | bytes 3145732
  67.5 1.2 %copy-start.18 = (bf16[256,2048]{1,0:T(8,128)(2,1)S(1)}, bf16[256,2048]{1,0:T(8,128)(2,1)}, u32[]{:S(2)}) copy-start(bf16[256,2048]{1,0:T(8,128)(2,1)} %copy-done.17) | copy-start | bytes 3145732
  68.7 1.2 %copy-start.20 = (f32[128,2048]{1,0:T(8,128)S(1)}, f32[128,2048]{1,0:T(8,128)}, u32[]{:S(2)}) copy-start(f32[128,2048]{1,0:T(8,128)} %copy-done.19) | copy-start | bytes 3145732

commit v6 on v4

--- a/solution.py
+++ b/solution.py
@@ -182,6 +182,9 @@
 
 def depth_factors(place_ref, bh_ref, bl_ref):
     low_g = lax.broadcasted_iota(jnp.int32, (8, PCHUNK), 0).astype(F32)
+    for factor_ref in (bh_ref, bl_ref):
+        for z in (112, 240):
+            factor_ref[z : z + 16, :] = jnp.zeros((16, NPROJ), BF16)
     for at in range(0, NPROJ, PCHUNK):
         here = slice(at, at + PCHUNK)
         tz, spread = place_ref[0:1, here], place_ref[1:2, here]
@@ -189,7 +192,7 @@
         for bank in range(2):
             high_g = lax.broadcasted_iota(jnp.int32, (8, PCHUNK), 0) * 8 + bank * 64
             high_c, high_s = sincos_turns(high_g.astype(F32) * tz)
-            for pair in range(4):
+            for pair in range(4 - bank):
                 re_rows, im_rows = [], []
                 for inner in range(2):
                     row = pair * 2 + inner
@@ -333,28 +336,19 @@
         grids.append(jnp.concatenate(parts, axis=1))
     work = jnp.concatenate(grids, axis=0)
     work = dot3(split(work), (yih_ref[...], yil_ref[...]), NN)
-    work = jnp.concatenate(
-        [
-            jnp.concatenate(
-                [work[p * 128 : (p + 1) * 128, :256], work[p * 128 : (p + 1) * 128, 256:]], axis=0
-            )
-            for p in range(DEPTH)
-        ],
-        axis=1,
-    )
-    work = dot3((xih_ref[...], xil_ref[...]), split(work), NN)
-    local = jnp.concatenate([potential_ref[p] for p in range(DEPTH)], axis=1)
-    work = jnp.concatenate([work[:EDGE] * local, work[EDGE:] * local], axis=0)
-    work = dot3((xfh_ref[...], xfl_ref[...]), split(work), NN)
-    work = jnp.concatenate(
-        [
-            jnp.concatenate(
-                [work[:128, p * 256 : (p + 1) * 256], work[128:, p * 256 : (p + 1) * 256]], axis=1
-            )
-            for p in range(DEPTH)
-        ],
-        axis=0,
-    )
+    x_inverse, x_forward = (xih_ref[...], xil_ref[...]), (xfh_ref[...], xfl_ref[...])
+    fields = []
+    for p in range(DEPTH):
+        rows = slice(p * 128, (p + 1) * 128)
+        field = jnp.concatenate([work[rows, :256], work[rows, 256:]], axis=0)
+        fields.append(dot3(x_inverse, split(field), NN))
+    grids = []
+    for p in range(DEPTH):
+        local = potential_ref[p]
+        field = jnp.concatenate([fields[p][:EDGE] * local, fields[p][EDGE:] * local], axis=0)
+        grid = dot3(x_forward, split(field), NN)
+        grids.append(jnp.concatenate([grid[:128], grid[128:]], axis=1))
+    work = jnp.concatenate(grids, axis=0)
     work = dot3(split(work), (yfh_ref[...], yfl_ref[...]), NN)
     pieces, extras = [], []
     for p in range(DEPTH):

time: 80.7 us -> 80.5 us (level)
  no operation moved by 1% of the time
where the time goes in v6:
time: 80.5 us; the launch traced here: 80 us
  blocking collectives  27.2 us (34%)
  starting transfers between devices  22.1 us (27%)
  Pallas kernels  15 us (19%)
  waiting for transfers between devices  10.6 us (13%)
  local copies, waits for them, and re-layouts  4.91 us (6%)
    all_to_all x1, blocking collectives, over_sheets(): lax.all_to_all(sent, 'pw', split_axis=0, concat_axis=0, tiled=True)  15.5 us
    all_to_all x1, starting transfers between devices, over_sheets(): lax.all_to_all(sent, 'pw', split_axis=0, concat_axis=0, tiled=True)  11.9 us
    all_to_all x1, blocking collectives, body(): return lax.all_to_all(done, 'tg', split_axis=0, concat_axis=0, tiled=True)  11.7 us
    all_to_all x1, starting transfers between devices, body(): lax.all_to_all(orbital_coefficients, 'tg', split_axis=0, concat_axis=0, t...  10.1 us
    all_to_all x1, waiting for transfers between devices, over_sheets(): lax.all_to_all(sent, 'pw', split_axis=0, concat_axis=0, tiled=True)  9.08 us
    pallas_call x1, Pallas kernels, plane_work(): call(plane_kernel, 'v' * 11, shape((SHEETS * ROWS, 2 * STICKS)), [pltpu.V...  7.81 us
    pallas_call x1, Pallas kernels, project(): call(project_kernel, 'v' * 10, shape((SHEETS * ROWS, 2 * STICKS)), [*FACT...  3.15 us
    pallas_call x1, Pallas kernels, finish(): call(finish_kernel, 's' + 'v' * 9, shape((TEAMS, 2, LINES, EDGE)), FACTOR...  2.08 us
  transfers between devices with their start and end apart: 2, of which 2 were waited for; matrix products, arithmetic and copies ran while one was open for 3% of the time, Pallas kernels for 2%

profile of v6, /device:TPU:1, one launch (start us, length us, event | category | flops | bytes accessed | tf_op | source)
XLA Modules:
  0.0 80.0 jit_solution(16836503900583450057)
XLA Ops:
  0.0 10.1 %all-to-all-start = ((f32[8,2,8,192]{3,2,1,0:T(8,128)}), f32[8,2,8,192]{3,2,1,0:T(8,128)S(1)}, u32[]{:S(2)}, u32[]{:S(2)}) async-start(f32[8,2,8,192]{3,2,1,0:T(8,128)} %param.23), calls=%async_computation | async-start | bytes 262144 | tf_op jit(solution)/shard_map/all_to_all | solution.py:533
  10.2 0.0 slice-start
  10.2 0.7 slice-done
  10.9 0.2 reshape.46
  11.0 0.1 copy.24
  11.1 0.0 copy-start
  11.1 0.0 copy-start.1
  11.1 0.0 copy-start.2
  11.1 0.1 copy.27.cols_ref
  11.2 0.0 copy-start.5
  11.2 0.6 copy-done
  11.9 0.0 copy-done.1
  11.9 0.0 copy-done.2
  11.9 0.0 copy-done.5
  11.9 0.0 copy-start.4
  11.9 0.0 copy-start.10
  11.9 0.0 copy-start.11
  11.9 0.0 copy-start.16
  11.9 1.9 %shard_map.217 = (f32[128,2048]{1,0:T(8,128)S(1)}, f32[2,2048]{1,0:T(2,128)S(1)}, f32[64,128]{1,0:T(8,128)S(1)}) custom-call(s32[1]{0:T(128)} %bitcast.sheet_ref, s32[512]{0:T(512)S(1)} %copy-done.5, s32[64,64]{1,0:T(8,128)S(1)} %copy.27.cols_ref, s32[1,2048]{1,0:T(1,128)S(1)} %bitcast.15, f32[3,512]{1,0:T(4,128)S(1)} %copy-done, f32[1,2048]{1,0:T(1,128)S(1)} %bitcast.14), custom_call_target="tpu_custom_call" | custom-call | flops 2147483648 | bytes 4194304 | tf_op jit(solution)/shard_map/pallas_call | solution.py:465
  13.9 0.0 copy-start.17
  13.9 0.0 copy-start.3
  13.9 1.5 %all-to-all-done.sticks_ref = f32[8,2,8,192]{3,2,1,0:T(8,128)S(1)} async-done(((f32[8,2,8,192]{3,2,1,0:T(8,128)}), f32[8,2,8,192]{3,2,1,0:T(8,128)S(1)}, u32[]{:S(2)}, u32[]{:S(2)}) %all-to-all-start) | async-done | bytes 98336 | tf_op jit(solution)/shard_map/all_to_all | solution.py:533
  15.4 0.0 copy-done.4
  15.4 0.0 copy-done.10
  15.4 0.0 copy-done.11
  15.5 0.0 copy-done.16
  15.5 0.0 copy-done.3
  15.5 0.0 copy-start.19
  15.5 3.2 %shard_map.218 = f32[256,128]{1,0:T(8,128)} custom-call(f32[8,2,8,192]{3,2,1,0:T(8,128)S(1)} %all-to-all-done.sticks_ref, bf16[384,192]{1,0:T(8,128)(2,1)S(1)} %copy-done.11, bf16[384,192]{1,0:T(8,128)(2,1)S(1)} %copy-done.10, bf16[192,256]{1,0:T(8,128)(2,1)S(1)} %copy-done.16, s32[1,2048]{1,0:T(1,128)S(1)} %bitcast.16, f32[1,2048]{1,0:T(1,128)S(1)} %bitcast.17, ...), custom_call_target="tpu_custom_call" | custom-call | flops 3221225472 | bytes 4194304 | tf_op jit(solution)/shard_map/pallas_call | solution.py:481
  18.6 0.0 copy-done.17
  18.6 11.9 %all-to-all-start.1 = ((f32[64,4,128]{2,1,0:T(4,128)}), f32[64,4,128]{2,1,0:T(4,128)S(1)}, u32[]{:S(2)}, u32[]{:S(2)}) async-start(f32[64,4,128]{2,1,0:T(4,128)} %bitcast.7), calls=%async_computation.1 | async-start | bytes 262144 | tf_op jit(solution)/shard_map/all_to_all | solution.py:516
  30.6 0.0 copy-done.19
  30.6 0.0 copy-start.12
  30.6 0.0 copy-start.13
  30.6 0.0 copy-start.14
  30.6 0.0 copy-start.15
  30.7 1.2 %reshape.54 = f32[3,192,192]{2,1,0:T(8,128)} reshape(f32[3,36864]{1,0:T(4,128)S(1)} %copy-done.19) | data formatting | bytes 884736 | tf_op jit(solution)/shard_map/reshape | solution.py:493
  31.9 0.0 copy-start.6
  31.9 0.0 copy-start.7
  31.9 0.0 copy-start.8
  31.9 0.0 copy-start.9
  31.9 1.2 %pad.4.potential_ref = f32[3,192,256]{2,1,0:T(8,128)S(1)} pad(f32[3,192,192]{2,1,0:T(8,128)} %reshape.54, f32[]{:T(128)} %constant.28.clone.1), padding=0_0x0_0x0_64 | pad | bytes 1032196 | tf_op jit(solution)/shard_map/jit(_pad)/pad | solution.py:493
  33.1 9.1 %all-to-all-done.1 = f32[64,4,128]{2,1,0:T(4,128)S(1)} async-done(((f32[64,4,128]{2,1,0:T(4,128)}), f32[64,4,128]{2,1,0:T(4,128)S(1)}, u32[]{:S(2)}, u32[]{:S(2)}) %all-to-all-start.1) | async-done | bytes 131104 | tf_op jit(solution)/shard_map/all_to_all | solution.py:516
  42.2 0.0 copy-done.12
  42.2 0.0 copy-done.13
  42.2 0.0 copy-done.14
  42.2 0.0 copy-done.15
  42.2 0.0 copy-done.6
  42.2 0.0 copy-done.7
  42.2 0.0 copy-done.8
  42.2 0.0 copy-done.9
  42.2 0.0 copy-start.18
  42.2 7.8 %shard_map.219 = f32[256,128]{1,0:T(8,128)S(1)} custom-call(s32[64,64]{1,0:T(8,128)S(1)} %copy.27.cols_ref, f32[256,128]{1,0:T(8,128)S(1)} %bitcast.11, f32[3,192,256]{2,1,0:T(8,128)S(1)} %pad.4.potential_ref, bf16[256,512]{1,0:T(8,128)(2,1)S(1)} %copy-done.9, bf16[256,512]{1,0:T(8,128)(2,1)S(1)} %copy-done.8, bf16[384,256]{1,0:T(8,128)(2,1)S(1)} %copy-done.15, ...), custom_call_target="tpu_custom_call" | custom-call | flops 8589934592 | bytes 4194304 | tf_op jit(solution)/shard_map/pallas_call | solution.py:494
  50.1 15.5 %all_to_all.20 = f32[64,4,128]{2,1,0:T(4,128)S(1)} all-to-all(f32[64,4,128]{2,1,0:T(4,128)S(1)} %bitcast.12), channel_id=1, replica_groups=mesh['tg'=8,'pw'=64] {'pw'}, dimensions={0} | all-to-all | bytes 262144 | tf_op jit(solution)/shard_map/all_to_all | solution.py:516
  65.6 0.0 copy-done.18
  65.6 2.1 %shard_map.220 = f32[8,2,8,192]{3,2,1,0:T(8,128)S(1)} custom-call(s32[1]{0:T(128)} %bitcast.sheet_ref, s32[64,64]{1,0:T(8,128)S(1)} %copy.27.cols_ref, f32[8,2,8,192]{3,2,1,0:T(8,128)S(1)} %all-to-all-done.sticks_ref, f32[256,128]{1,0:T(8,128)S(1)} %bitcast.13, f32[128,2048]{1,0:T(8,128)S(1)} %copy-done.18, f32[2,2048]{1,0:T(2,128)S(1)} %get-tuple-element.9.place_ref, ...), custom_call_target="tpu_custom_call" | custom-call | flops 3221225472 | bytes 4194304 | tf_op jit(solution)/shard_map/pallas_call | solution.py:509
  67.6 11.7 %all_to_all.21 = f32[8,2,8,192]{3,2,1,0:T(8,128)S(1)} all-to-all(f32[8,2,8,192]{3,2,1,0:T(8,128)S(1)} %shard_map.220), channel_id=1, replica_groups=mesh['tg'=8,'pw'=64] {'tg'}, dimensions={0} | all-to-all | bytes 196608 | tf_op jit(solution)/shard_map/all_to_all | solution.py:540
  79.3 0.7 copy.29
Async XLA Ops:
  0.0 15.4 %all-to-all-start = ((f32[8,2,8,192]{3,2,1,0:T(8,128)}), f32[8,2,8,192]{3,2,1,0:T(8,128)S(1)}, u32[]{:S(2)}, u32[]{:S(2)}) async-start(f32[8,2,8,192]{3,2,1,0:T(8,128)} %param.23), calls=%async_computation | async-start | bytes 262144 | tf_op jit(solution)/shard_map/all_to_all | solution.py:533
  10.2 0.7 slice-start
  11.1 0.7 copy-start
  11.1 0.7 copy-start.1
  11.1 0.7 copy-start.2
  11.2 0.7 copy-start.5
  11.9 3.5 %copy-start.4 = (f32[2048]{0:T(1024)S(1)}, f32[2048]{0:T(1024)}, u32[]{:S(2)}) copy-start(f32[2048]{0:T(1024)} %param.31) | copy-start | bytes 24580
  11.9 3.5 %copy-start.10 = (bf16[384,192]{1,0:T(8,128)(2,1)S(1)}, bf16[384,192]{1,0:T(8,128)(2,1)}, u32[]{:S(2)}) copy-start(bf16[384,192]{1,0:T(8,128)(2,1)} %constant.30.clone.tl_ref) | copy-start | bytes 442372
  11.9 3.5 %copy-start.11 = (bf16[384,192]{1,0:T(8,128)(2,1)S(1)}, bf16[384,192]{1,0:T(8,128)(2,1)}, u32[]{:S(2)}) copy-start(bf16[384,192]{1,0:T(8,128)(2,1)} %constant.29.clone.th_ref) | copy-start | bytes 442372
  11.9 3.5 %copy-start.16 = (bf16[192,256]{1,0:T(8,128)(2,1)S(1)}, bf16[192,256]{1,0:T(8,128)(2,1)}, u32[]{:S(2)}) copy-start(bf16[192,256]{1,0:T(8,128)(2,1)} %constant.31.clone.fold_ref) | copy-start | bytes 294916
  13.9 4.8 %copy-start.17 = (f32[128,2048]{1,0:T(8,128)}, f32[128,2048]{1,0:T(8,128)S(1)}, u32[]{:S(2)}) copy-start(f32[128,2048]{1,0:T(8,128)S(1)} %get-tuple-element.8.a_ref) | copy-start | bytes 3145732
  13.9 1.6 %copy-start.3 = (f32[2048]{0:T(1024)S(1)}, f32[2048]{0:T(1024)}, u32[]{:S(2)}) copy-start(f32[2048]{0:T(1024)} %param.30) | copy-start | bytes 24580
  15.5 15.1 %copy-start.19 = (f32[3,36864]{1,0:T(4,128)S(1)}, f32[3,36864]{1,0:T(4,128)}, u32[]{:S(2)}) copy-start(f32[3,36864]{1,0:T(4,128)} %param.24) | copy-start | bytes 1327108
  18.6 23.5 %all-to-all-start.1 = ((f32[64,4,128]{2,1,0:T(4,128)}), f32[64,4,128]{2,1,0:T(4,128)S(1)}, u32[]{:S(2)}, u32[]{:S(2)}) async-start(f32[64,4,128]{2,1,0:T(4,128)} %bitcast.7), calls=%async_computation.1 | async-start | bytes 262144 | tf_op jit(solution)/shard_map/all_to_all | solution.py:516
  30.6 11.6 %copy-start.12 = (bf16[256,384]{1,0:T(8,128)(2,1)S(1)}, bf16[256,384]{1,0:T(8,128)(2,1)}, u32[]{:S(2)}) copy-start(bf16[256,384]{1,0:T(8,128)(2,1)} %constant.37.clone.xfl_ref) | copy-start | bytes 589828
  30.6 11.6 %copy-start.13 = (bf16[256,384]{1,0:T(8,128)(2,1)S(1)}, bf16[256,384]{1,0:T(8,128)(2,1)}, u32[]{:S(2)}) copy-start(bf16[256,384]{1,0:T(8,128)(2,1)} %constant.36.clone.xfh_ref) | copy-start | bytes 589828
  30.6 11.6 %copy-start.14 = (bf16[384,256]{1,0:T(8,128)(2,1)S(1)}, bf16[384,256]{1,0:T(8,128)(2,1)}, u32[]{:S(2)}) copy-start(bf16[384,256]{1,0:T(8,128)(2,1)} %constant.35.clone.xil_ref) | copy-start | bytes 589828
  30.6 11.5 %copy-start.15 = (bf16[384,256]{1,0:T(8,128)(2,1)S(1)}, bf16[384,256]{1,0:T(8,128)(2,1)}, u32[]{:S(2)}) copy-start(bf16[384,256]{1,0:T(8,128)(2,1)} %constant.34.clone.xih_ref) | copy-start | bytes 589828
  31.9 10.3 %copy-start.6 = (bf16[512,256]{1,0:T(8,128)(2,1)S(1)}, bf16[512,256]{1,0:T(8,128)(2,1)}, u32[]{:S(2)}) copy-start(bf16[512,256]{1,0:T(8,128)(2,1)} %constant.39.clone.yfl_ref) | copy-start | bytes 786436
  31.9 10.3 %copy-start.7 = (bf16[512,256]{1,0:T(8,128)(2,1)S(1)}, bf16[512,256]{1,0:T(8,128)(2,1)}, u32[]{:S(2)}) copy-start(bf16[512,256]{1,0:T(8,128)(2,1)} %constant.38.clone.yfh_ref) | copy-start | bytes 786436
  31.9 10.3 %copy-start.8 = (bf16[256,512]{1,0:T(8,128)(2,1)S(1)}, bf16[256,512]{1,0:T(8,128)(2,1)}, u32[]{:S(2)}) copy-start(bf16[256,512]{1,0:T(8,128)(2,1)} %constant.33.clone.yil_ref) | copy-start | bytes 786436
  31.9 10.3 %copy-start.9 = (bf16[256,512]{1,0:T(8,128)(2,1)S(1)}, bf16[256,512]{1,0:T(8,128)(2,1)}, u32[]{:S(2)}) copy-start(bf16[256,512]{1,0:T(8,128)(2,1)} %constant.32.clone.yih_ref) | copy-start | bytes 786436
  42.2 23.3 %copy-start.18 = (f32[128,2048]{1,0:T(8,128)S(1)}, f32[128,2048]{1,0:T(8,128)}, u32[]{:S(2)}) copy-start(f32[128,2048]{1,0:T(8,128)} %copy-done.17) | copy-start | bytes 3145732

commit v7 on v6

--- a/solution.py
+++ b/solution.py
@@ -18,7 +18,8 @@
 NPROJ = 2048
 NATOM = 512
 CUT = 48
-HALF_ROWS = 48
+PACK = 32
+CENTERS = (48, 142, 223)
 CHUNK = 1024
 CHUNKS = SHEETS * STICKS // CHUNK
 PCHUNK = 256
@@ -59,14 +60,20 @@
     return np.cos(turns) * keep, np.sin(turns) * keep
 
 
+def packed_x(band, row):
+    inner = row % 16
+    size = 16 * band + (15 - inner if band == 2 else inner)
+    return -size - 1 if row >= 16 else size
+
+
 def lateral_tables():
     spot = np.arange(128)
     y_cos, y_sin = column_phase(spot - CUT, spot <= 2 * CUT)
     pad = ((0, 0), (0, 256 - EDGE))
     y_cos, y_sin = np.pad(y_cos, pad), np.pad(y_sin, pad)
     y_inverse = np.block([[y_cos, y_sin], [-y_sin, y_cos]])
-    x_spot = np.where(spot < 2 * HALF_ROWS, 2 * (spot % HALF_ROWS) + spot // HALF_ROWS, spot)
-    x_cos, x_sin = column_phase(x_spot - CUT, x_spot <= 2 * CUT)
+    x_freq = np.array([packed_x(band, row) for band in range(3) for row in range(PACK)] + [CUT] * 32)
+    x_cos, x_sin = column_phase(x_freq, spot <= 3 * PACK)
     x_forward = np.block([[x_cos, x_sin], [-x_sin, x_cos]])
     return y_inverse, x_forward.T, x_forward, y_inverse.T
 
@@ -277,9 +284,12 @@
 ):
     half = SHEETS // 2
     x, y = lateral_split(jnp.concatenate([cols_ref[:half, :], cols_ref[half:, :]], axis=1))
-    x, y = x + CUT, y + CUT
-    x_ref[0] = x >> 1
-    x_ref[1] = (x & 1) * 128 + y
+    size = jnp.where(x >= 0, x, -x - 1)
+    band = size >> 4
+    row = jnp.where(band == 2, 15 - (size & 15), size & 15) + jnp.where(x < 0, 16, 0)
+    lane = y + jnp.where(band == 0, CENTERS[0], jnp.where(band == 1, CENTERS[1], CENTERS[2]))
+    x_ref[0] = jnp.where(band > 2, PACK, row)
+    x_ref[1] = jnp.where(lane >= 256, lane - 256, lane)
     for plane in range(DEPTH):
         rows = sticks_ref[every(plane), :]
         top, bottom = rows[:half], rows[half:]
@@ -292,7 +302,7 @@
             v_ref[at + 1] = value - high
     summed = jnp.sum(sticks_ref[every(DEPTH), :], axis=0, keepdims=True)
     out_ref[every(DEPTH), :] = jnp.broadcast_to(summed, (SHEETS, 128))
-    row_of = lax.broadcasted_iota(jnp.int32, (HALF_ROWS, 128), 0)
+    row_of = lax.broadcasted_iota(jnp.int32, (PACK, 128), 0)
     half_rows = row_of.astype(F32).astype(BF16)
     full_rows = lax.broadcasted_iota(jnp.int32, (256, 128), 0).astype(F32).astype(BF16)
     one, zero = jnp.ones((), BF16), jnp.zeros((), BF16)
@@ -302,37 +312,52 @@
         return jnp.concatenate([packed] * (height // 16), axis=0)
 
     per = CHUNK // 128
-    total = jnp.zeros((12 * HALF_ROWS, 256), F32)
+    total = jnp.zeros((12 * PACK, 256), F32)
     for chunk in range(CHUNKS):
         slot = chunk % 2
         for inner in range(per):
             r = chunk * per + inner
             lanes = slice(inner * 128, (inner + 1) * 128)
             spot = x_ref[:, r : r + 1, :].astype(F32)
-            member = jnp.where(half_rows == tall(spot[0], HALF_ROWS), one, zero)
+            member = jnp.where(half_rows == tall(spot[0], PACK), one, zero)
             hot_ref[chunk, :, lanes] = jnp.where(full_rows == tall(spot[1], 256), one, zero)
             for k in range(12):
-                value = tall(v_ref[k, r : r + 1, :], HALF_ROWS)
-                left_ref[slot, k * HALF_ROWS : (k + 1) * HALF_ROWS, lanes] = member * value
+                value = tall(v_ref[k, r : r + 1, :], PACK)
+                left_ref[slot, k * PACK : (k + 1) * PACK, lanes] = member * value
         total = total + mul(left_ref[slot], hot_ref[chunk], NT)
-    lone = x_ref[0] == HALF_ROWS
+    lone = x_ref[0] == PACK
     lone_spot = (lax.broadcasted_iota(jnp.int32, (32, 128), 0) == 0) & (
         lax.broadcasted_iota(jnp.int32, (32, 128), 1) == CUT
     )
 
     def whole(value):
         return jnp.sum(jnp.sum(value, axis=0, keepdims=True), axis=1, keepdims=True)
+
+    held = []
+    row = lax.broadcasted_iota(jnp.int32, (PACK, 128), 0)
+    y = lax.broadcasted_iota(jnp.int32, (PACK, 128), 1) - CUT
+    for band in range(3):
+        size = 16 * band + jnp.where(band == 2, 15 - (row & 15), row & 15)
+        x = jnp.where(row >= 16, -size - 1, size)
+        held.append(x * x + y * y <= CUT * CUT)
+
+    def turned(grid, shift):
+        return grid if shift == 0 else pltpu.roll(grid, shift, 1)
 
     grids = []
     for plane in range(DEPTH):
         parts = []
         for part in range(2):
-            at = 2 * (2 * plane + part) * HALF_ROWS
-            grid = total[at : at + HALF_ROWS] + total[at + HALF_ROWS : at + 2 * HALF_ROWS]
+            at = 2 * (2 * plane + part) * PACK
+            grid = total[at : at + PACK] + total[at + PACK : at + 2 * PACK]
             at = 2 * (2 * plane + part)
             extra = whole(jnp.where(lone, v_ref[at] + v_ref[at + 1], 0.0))
             extra = jnp.where(lone_spot, extra, 0.0)
-            parts.append(jnp.concatenate([grid[:, :128], grid[:, 128:], extra], axis=0))
+            bands = [
+                jnp.where(held[band], turned(grid, (256 + CUT - CENTERS[band]) % 256)[:, :128], 0.0)
+                for band in range(3)
+            ]
+            parts.append(jnp.concatenate([*bands, extra], axis=0))
         grids.append(jnp.concatenate(parts, axis=1))
     work = jnp.concatenate(grids, axis=0)
     work = dot3(split(work), (yih_ref[...], yil_ref[...]), NN)
@@ -354,21 +379,24 @@
     for p in range(DEPTH):
         for c in range(2):
             block = work[p * 128 : (p + 1) * 128, c * 128 : (c + 1) * 128]
-            pieces.append(
-                jnp.concatenate([block[:HALF_ROWS], block[HALF_ROWS : 2 * HALF_ROWS]], axis=1)
-            )
-            extras.append(whole(jnp.where(lone_spot, block[2 * HALF_ROWS :], 0.0)))
-    high, low = split(jnp.concatenate(pieces, axis=0))
+            packed = jnp.zeros((PACK, 256), F32)
+            for band in range(3):
+                rows = jnp.where(held[band], block[band * PACK : (band + 1) * PACK], 0.0)
+                wide = jnp.concatenate([rows, jnp.zeros((PACK, 128), F32)], axis=1)
+                packed = packed + turned(wide, CENTERS[band] - CUT)
+            pieces.append(packed)
+            extras.append(whole(jnp.where(lone_spot, block[3 * PACK :], 0.0)))
+    stack = jnp.concatenate(split(jnp.concatenate(pieces, axis=0)), axis=0)
     for chunk in range(CHUNKS):
-        hot = hot_ref[chunk]
-        found = mul(high, hot, NN) + mul(low, hot, NN)
+        found = mul(stack, hot_ref[chunk], NN)
+        found = found[: 6 * PACK] + found[6 * PACK :]
         for inner in range(per):
             r = chunk * per + inner
             lanes = slice(inner * 128, (inner + 1) * 128)
             member = row_of == x_ref[0, r : r + 1, :]
             for k in range(6):
                 pick_ref[k, r : r + 1, :] = jnp.sum(
-                    jnp.where(member, found[k * HALF_ROWS : (k + 1) * HALF_ROWS, lanes], 0.0),
+                    jnp.where(member, found[k * PACK : (k + 1) * PACK, lanes], 0.0),
                     axis=0,
                     keepdims=True,
                 )
@@ -497,7 +525,7 @@
             pltpu.VMEM((2, SHEETS // 2, 128), jnp.int32),
             pltpu.VMEM((12, SHEETS // 2, 128), F32),
             pltpu.VMEM((CHUNKS, 256, CHUNK), BF16),
-            pltpu.VMEM((2, 12 * HALF_ROWS, CHUNK), BF16),
+            pltpu.VMEM((2, 12 * PACK, CHUNK), BF16),
             pltpu.VMEM((6, SHEETS // 2, 128), F32),
         ],
         flops=8 << 30,

time: 80.5 us -> 79.3 us (0.985)
  Pallas kernels: 15 us -> 13.7 us
    pallas_call x1, Pallas kernels: 7.81 us -> 6.55 us  [plane_work(): call(plane_kernel, 'v' * 11, shape((SHEETS * ROWS, 2 * STICKS)), [pltpu.V...]
  transfers between devices with their start and end apart: 2 -> 2, of which waited for: 2 -> 2; matrix products, arithmetic and copies ran while one was open for 3% -> 4% of each run, Pallas kernels for 2% -> 2%
where the time goes in v7:
time: 79.3 us; the launch traced here: 78.7 us
  blocking collectives  27.2 us (34%)
  starting transfers between devices  22.1 us (28%)
  Pallas kernels  13.7 us (17%)
  waiting for transfers between devices  10.6 us (13%)
  local copies, waits for them, and re-layouts  4.91 us (6%)
    all_to_all x1, blocking collectives, over_sheets(): lax.all_to_all(sent, 'pw', split_axis=0, concat_axis=0, tiled=True)  15.5 us
    all_to_all x1, starting transfers between devices, over_sheets(): lax.all_to_all(sent, 'pw', split_axis=0, concat_axis=0, tiled=True)  11.9 us
    all_to_all x1, blocking collectives, body(): return lax.all_to_all(done, 'tg', split_axis=0, concat_axis=0, tiled=True)  11.7 us
    all_to_all x1, starting transfers between devices, body(): lax.all_to_all(orbital_coefficients, 'tg', split_axis=0, concat_axis=0, t...  10.1 us
    all_to_all x1, waiting for transfers between devices, over_sheets(): lax.all_to_all(sent, 'pw', split_axis=0, concat_axis=0, tiled=True)  9.08 us
    pallas_call x1, Pallas kernels, plane_work(): call(plane_kernel, 'v' * 11, shape((SHEETS * ROWS, 2 * STICKS)), [pltpu.V...  6.55 us
    pallas_call x1, Pallas kernels, project(): call(project_kernel, 'v' * 10, shape((SHEETS * ROWS, 2 * STICKS)), [*FACT...  3.15 us
    pallas_call x1, Pallas kernels, finish(): call(finish_kernel, 's' + 'v' * 9, shape((TEAMS, 2, LINES, EDGE)), FACTOR...  2.08 us
  transfers between devices with their start and end apart: 2, of which 2 were waited for; matrix products, arithmetic and copies ran while one was open for 4% of the time, Pallas kernels for 2%

profile of v7, /device:TPU:1, one launch (start us, length us, event | category | flops | bytes accessed | tf_op | source)
XLA Modules:
  0.0 78.7 jit_solution(11334588426380523819)
XLA Ops:
  0.0 10.1 %all-to-all-start = ((f32[8,2,8,192]{3,2,1,0:T(8,128)}), f32[8,2,8,192]{3,2,1,0:T(8,128)S(1)}, u32[]{:S(2)}, u32[]{:S(2)}) async-start(f32[8,2,8,192]{3,2,1,0:T(8,128)} %param.23), calls=%async_computation | async-start | bytes 262144 | tf_op jit(solution)/shard_map/all_to_all | solution.py:561
  10.2 0.0 slice-start
  10.2 0.7 slice-done
  10.9 0.2 reshape.46
  11.0 0.1 copy.24
  11.1 0.0 copy-start
  11.1 0.0 copy-start.1
  11.1 0.0 copy-start.2
  11.1 0.1 copy.27.cols_ref
  11.2 0.0 copy-start.5
  11.2 0.6 copy-done
  11.9 0.0 copy-done.1
  11.9 0.0 copy-done.2
  11.9 0.0 copy-done.5
  11.9 0.0 copy-start.4
  11.9 0.0 copy-start.10
  11.9 0.0 copy-start.11
  11.9 0.0 copy-start.16
  11.9 1.9 %shard_map.217 = (f32[128,2048]{1,0:T(8,128)S(1)}, f32[2,2048]{1,0:T(2,128)S(1)}, f32[64,128]{1,0:T(8,128)S(1)}) custom-call(s32[1]{0:T(128)} %bitcast.sheet_ref, s32[512]{0:T(512)S(1)} %copy-done.5, s32[64,64]{1,0:T(8,128)S(1)} %copy.27.cols_ref, s32[1,2048]{1,0:T(1,128)S(1)} %bitcast.15, f32[3,512]{1,0:T(4,128)S(1)} %copy-done, f32[1,2048]{1,0:T(1,128)S(1)} %bitcast.14), custom_call_target="tpu_custom_call" | custom-call | flops 2147483648 | bytes 4194304 | tf_op jit(solution)/shard_map/pallas_call | solution.py:493
  13.9 0.0 copy-start.17
  13.9 0.0 copy-start.3
  13.9 1.5 %all-to-all-done.sticks_ref = f32[8,2,8,192]{3,2,1,0:T(8,128)S(1)} async-done(((f32[8,2,8,192]{3,2,1,0:T(8,128)}), f32[8,2,8,192]{3,2,1,0:T(8,128)S(1)}, u32[]{:S(2)}, u32[]{:S(2)}) %all-to-all-start) | async-done | bytes 98336 | tf_op jit(solution)/shard_map/all_to_all | solution.py:561
  15.4 0.0 copy-done.4
  15.4 0.0 copy-done.10
  15.4 0.0 copy-done.11
  15.5 0.0 copy-done.16
  15.5 0.0 copy-done.3
  15.5 0.0 copy-start.19
  15.5 3.2 %shard_map.218 = f32[256,128]{1,0:T(8,128)} custom-call(f32[8,2,8,192]{3,2,1,0:T(8,128)S(1)} %all-to-all-done.sticks_ref, bf16[384,192]{1,0:T(8,128)(2,1)S(1)} %copy-done.11, bf16[384,192]{1,0:T(8,128)(2,1)S(1)} %copy-done.10, bf16[192,256]{1,0:T(8,128)(2,1)S(1)} %copy-done.16, s32[1,2048]{1,0:T(1,128)S(1)} %bitcast.16, f32[1,2048]{1,0:T(1,128)S(1)} %bitcast.17, ...), custom_call_target="tpu_custom_call" | custom-call | flops 3221225472 | bytes 4194304 | tf_op jit(solution)/shard_map/pallas_call | solution.py:509
  18.6 0.0 copy-done.17
  18.6 11.9 %all-to-all-start.1 = ((f32[64,4,128]{2,1,0:T(4,128)}), f32[64,4,128]{2,1,0:T(4,128)S(1)}, u32[]{:S(2)}, u32[]{:S(2)}) async-start(f32[64,4,128]{2,1,0:T(4,128)} %bitcast.7), calls=%async_computation.1 | async-start | bytes 262144 | tf_op jit(solution)/shard_map/all_to_all | solution.py:544
  30.6 0.0 copy-done.19
  30.6 0.0 copy-start.12
  30.6 0.0 copy-start.13
  30.6 0.0 copy-start.14
  30.6 0.0 copy-start.15
  30.7 1.2 %reshape.54 = f32[3,192,192]{2,1,0:T(8,128)} reshape(f32[3,36864]{1,0:T(4,128)S(1)} %copy-done.19) | data formatting | bytes 884736 | tf_op jit(solution)/shard_map/reshape | solution.py:521
  31.9 0.0 copy-start.6
  31.9 0.0 copy-start.7
  31.9 0.0 copy-start.8
  31.9 0.0 copy-start.9
  31.9 1.2 %pad.4.potential_ref = f32[3,192,256]{2,1,0:T(8,128)S(1)} pad(f32[3,192,192]{2,1,0:T(8,128)} %reshape.54, f32[]{:T(128)} %constant.28.clone.1), padding=0_0x0_0x0_64 | pad | bytes 1032196 | tf_op jit(solution)/shard_map/jit(_pad)/pad | solution.py:521
  33.1 9.1 %all-to-all-done.1 = f32[64,4,128]{2,1,0:T(4,128)S(1)} async-done(((f32[64,4,128]{2,1,0:T(4,128)}), f32[64,4,128]{2,1,0:T(4,128)S(1)}, u32[]{:S(2)}, u32[]{:S(2)}) %all-to-all-start.1) | async-done | bytes 131104 | tf_op jit(solution)/shard_map/all_to_all | solution.py:544
  42.2 0.0 copy-done.12
  42.2 0.0 copy-done.13
  42.2 0.0 copy-done.14
  42.2 0.0 copy-done.15
  42.2 0.0 copy-done.6
  42.2 0.0 copy-done.7
  42.2 0.0 copy-done.8
  42.2 0.0 copy-done.9
  42.2 0.0 copy-start.18
  42.2 6.5 %shard_map.219 = f32[256,128]{1,0:T(8,128)S(1)} custom-call(s32[64,64]{1,0:T(8,128)S(1)} %copy.27.cols_ref, f32[256,128]{1,0:T(8,128)S(1)} %bitcast.11, f32[3,192,256]{2,1,0:T(8,128)S(1)} %pad.4.potential_ref, bf16[256,512]{1,0:T(8,128)(2,1)S(1)} %copy-done.9, bf16[256,512]{1,0:T(8,128)(2,1)S(1)} %copy-done.8, bf16[384,256]{1,0:T(8,128)(2,1)S(1)} %copy-done.15, ...), custom_call_target="tpu_custom_call" | custom-call | flops 8589934592 | bytes 4194304 | tf_op jit(solution)/shard_map/pallas_call | solution.py:522
  48.8 15.5 %all_to_all.20 = f32[64,4,128]{2,1,0:T(4,128)S(1)} all-to-all(f32[64,4,128]{2,1,0:T(4,128)S(1)} %bitcast.12), channel_id=1, replica_groups=mesh['tg'=8,'pw'=64] {'pw'}, dimensions={0} | all-to-all | bytes 262144 | tf_op jit(solution)/shard_map/all_to_all | solution.py:544
  64.3 0.0 copy-done.18
  64.3 2.1 %shard_map.220 = f32[8,2,8,192]{3,2,1,0:T(8,128)S(1)} custom-call(s32[1]{0:T(128)} %bitcast.sheet_ref, s32[64,64]{1,0:T(8,128)S(1)} %copy.27.cols_ref, f32[8,2,8,192]{3,2,1,0:T(8,128)S(1)} %all-to-all-done.sticks_ref, f32[256,128]{1,0:T(8,128)S(1)} %bitcast.13, f32[128,2048]{1,0:T(8,128)S(1)} %copy-done.18, f32[2,2048]{1,0:T(2,128)S(1)} %get-tuple-element.9.place_ref, ...), custom_call_target="tpu_custom_call" | custom-call | flops 3221225472 | bytes 4194304 | tf_op jit(solution)/shard_map/pallas_call | solution.py:537
  66.4 11.7 %all_to_all.21 = f32[8,2,8,192]{3,2,1,0:T(8,128)S(1)} all-to-all(f32[8,2,8,192]{3,2,1,0:T(8,128)S(1)} %shard_map.220), channel_id=1, replica_groups=mesh['tg'=8,'pw'=64] {'tg'}, dimensions={0} | all-to-all | bytes 196608 | tf_op jit(solution)/shard_map/all_to_all | solution.py:568
  78.1 0.7 copy.29
Async XLA Ops:
  0.0 15.4 %all-to-all-start = ((f32[8,2,8,192]{3,2,1,0:T(8,128)}), f32[8,2,8,192]{3,2,1,0:T(8,128)S(1)}, u32[]{:S(2)}, u32[]{:S(2)}) async-start(f32[8,2,8,192]{3,2,1,0:T(8,128)} %param.23), calls=%async_computation | async-start | bytes 262144 | tf_op jit(solution)/shard_map/all_to_all | solution.py:561
  10.2 0.7 slice-start
  11.1 0.7 copy-start
  11.1 0.7 copy-start.1
  11.1 0.7 copy-start.2
  11.2 0.7 copy-start.5
  11.9 3.5 %copy-start.4 = (f32[2048]{0:T(1024)S(1)}, f32[2048]{0:T(1024)}, u32[]{:S(2)}) copy-start(f32[2048]{0:T(1024)} %param.31) | copy-start | bytes 24580
  11.9 3.5 %copy-start.10 = (bf16[384,192]{1,0:T(8,128)(2,1)S(1)}, bf16[384,192]{1,0:T(8,128)(2,1)}, u32[]{:S(2)}) copy-start(bf16[384,192]{1,0:T(8,128)(2,1)} %constant.30.clone.tl_ref) | copy-start | bytes 442372
  11.9 3.5 %copy-start.11 = (bf16[384,192]{1,0:T(8,128)(2,1)S(1)}, bf16[384,192]{1,0:T(8,128)(2,1)}, u32[]{:S(2)}) copy-start(bf16[384,192]{1,0:T(8,128)(2,1)} %constant.29.clone.th_ref) | copy-start | bytes 442372
  11.9 3.5 %copy-start.16 = (bf16[192,256]{1,0:T(8,128)(2,1)S(1)}, bf16[192,256]{1,0:T(8,128)(2,1)}, u32[]{:S(2)}) copy-start(bf16[192,256]{1,0:T(8,128)(2,1)} %constant.31.clone.fold_ref) | copy-start | bytes 294916
  13.9 4.8 %copy-start.17 = (f32[128,2048]{1,0:T(8,128)}, f32[128,2048]{1,0:T(8,128)S(1)}, u32[]{:S(2)}) copy-start(f32[128,2048]{1,0:T(8,128)S(1)} %get-tuple-element.8.a_ref) | copy-start | bytes 3145732
  13.9 1.6 %copy-start.3 = (f32[2048]{0:T(1024)S(1)}, f32[2048]{0:T(1024)}, u32[]{:S(2)}) copy-start(f32[2048]{0:T(1024)} %param.30) | copy-start | bytes 24580
  15.5 15.1 %copy-start.19 = (f32[3,36864]{1,0:T(4,128)S(1)}, f32[3,36864]{1,0:T(4,128)}, u32[]{:S(2)}) copy-start(f32[3,36864]{1,0:T(4,128)} %param.24) | copy-start | bytes 1327108
  18.6 23.5 %all-to-all-start.1 = ((f32[64,4,128]{2,1,0:T(4,128)}), f32[64,4,128]{2,1,0:T(4,128)S(1)}, u32[]{:S(2)}, u32[]{:S(2)}) async-start(f32[64,4,128]{2,1,0:T(4,128)} %bitcast.7), calls=%async_computation.1 | async-start | bytes 262144 | tf_op jit(solution)/shard_map/all_to_all | solution.py:544
  30.6 11.6 %copy-start.12 = (bf16[256,384]{1,0:T(8,128)(2,1)S(1)}, bf16[256,384]{1,0:T(8,128)(2,1)}, u32[]{:S(2)}) copy-start(bf16[256,384]{1,0:T(8,128)(2,1)} %constant.37.clone.xfl_ref) | copy-start | bytes 589828
  30.6 11.6 %copy-start.13 = (bf16[256,384]{1,0:T(8,128)(2,1)S(1)}, bf16[256,384]{1,0:T(8,128)(2,1)}, u32[]{:S(2)}) copy-start(bf16[256,384]{1,0:T(8,128)(2,1)} %constant.36.clone.xfh_ref) | copy-start | bytes 589828
  30.6 11.6 %copy-start.14 = (bf16[384,256]{1,0:T(8,128)(2,1)S(1)}, bf16[384,256]{1,0:T(8,128)(2,1)}, u32[]{:S(2)}) copy-start(bf16[384,256]{1,0:T(8,128)(2,1)} %constant.35.clone.xil_ref) | copy-start | bytes 589828
  30.6 11.5 %copy-start.15 = (bf16[384,256]{1,0:T(8,128)(2,1)S(1)}, bf16[384,256]{1,0:T(8,128)(2,1)}, u32[]{:S(2)}) copy-start(bf16[384,256]{1,0:T(8,128)(2,1)} %constant.34.clone.xih_ref) | copy-start | bytes 589828
  31.9 10.3 %copy-start.6 = (bf16[512,256]{1,0:T(8,128)(2,1)S(1)}, bf16[512,256]{1,0:T(8,128)(2,1)}, u32[]{:S(2)}) copy-start(bf16[512,256]{1,0:T(8,128)(2,1)} %constant.39.clone.yfl_ref) | copy-start | bytes 786436
  31.9 10.3 %copy-start.7 = (bf16[512,256]{1,0:T(8,128)(2,1)S(1)}, bf16[512,256]{1,0:T(8,128)(2,1)}, u32[]{:S(2)}) copy-start(bf16[512,256]{1,0:T(8,128)(2,1)} %constant.38.clone.yfh_ref) | copy-start | bytes 786436
  31.9 10.3 %copy-start.8 = (bf16[256,512]{1,0:T(8,128)(2,1)S(1)}, bf16[256,512]{1,0:T(8,128)(2,1)}, u32[]{:S(2)}) copy-start(bf16[256,512]{1,0:T(8,128)(2,1)} %constant.33.clone.yil_ref) | copy-start | bytes 786436
  31.9 10.3 %copy-start.9 = (bf16[256,512]{1,0:T(8,128)(2,1)S(1)}, bf16[256,512]{1,0:T(8,128)(2,1)}, u32[]{:S(2)}) copy-start(bf16[256,512]{1,0:T(8,128)(2,1)} %constant.32.clone.yih_ref) | copy-start | bytes 786436
  42.2 22.1 %copy-start.18 = (f32[128,2048]{1,0:T(8,128)S(1)}, f32[128,2048]{1,0:T(8,128)}, u32[]{:S(2)}) copy-start(f32[128,2048]{1,0:T(8,128)} %copy-done.17) | copy-start | bytes 3145732
